TPU v7x, 32 devices: a whole 2x2x4 slice. The times are simulated.
32 devices in a mesh: grp: 1, blk: 32 (over z, y, x, core), shot: 1.
Axes of the slice: x: 2, y: 2, z: 4, core: 2. Of those that a mesh axis runs over, the one named last changes fastest.
Arguments:
- adjoint_in: float32 [1, 2, 32, 8, 32, 256], P(('grp', 'shot'), None, 'blk'), may hold values from -6 to 6
- forward: float32 [1, 4, 32, 8, 32, 256], P(('grp', 'shot'), None, 'blk'), may hold values from -6 to 6
- modulus: float32 [32, 8, 32, 256], P(('grp', 'blk')), may hold values from 0.5 to 2
- buoyancy: float32 [32, 8, 32, 256], P(('grp', 'blk')), may hold values from 0.5 to 2
- topography: int32 [32, 8, 32], P(('grp', 'blk')), may hold values from 1 to 63
- receivers: int32 [4096, 2], P('grp'), may hold values from 0 to 127, as said below
- residuals: float32 [1, 2, 4096], P(('grp', 'shot')), may hold values from -6 to 6
Outputs:
- image_modulus: float32 [32, 8, 32, 256], P(('grp', 'blk'))
- image_buoyancy: float32 [32, 8, 32, 256], P(('grp', 'blk'))
- adjoint_out: float32 [1, 2, 32, 8, 32, 256], P(('grp', 'shot'), None, 'blk')
Inputs may be any that keep to these rules, and one draw needn't show every extreme that they name: Column 0 holds indices below 64, column 1 indices below 128; several receivers may share a cell.
All inputs are finite; a program needn't handle non-finite values.
Results may differ from a plain program's by a relative error of at most 0.0003.
Values sent between devices are 32-bit elements; how exact they have to be, the bound alone decides.
No kernel may reach another device: no remote copies, remote signals or barrier semaphores. Data moves between devices by JAX's collectives and lax.ppermute only.
A program may use at most 64 MiB of HBM per device.

v0:
```python
import jax
import jax.numpy as jnp
from jax import lax
from jax.sharding import PartitionSpec as P

STEPS = 2
YBLOCKS = 4


laplace_coeffs = (-205.0 / 72.0, 8.0 / 5.0, -1.0 / 5.0, 8.0 / 315.0, -1.0 / 560.0)
slope_coeffs = (4.0 / 5.0, -1.0 / 5.0, 4.0 / 105.0, -1.0 / 280.0)
time_factor = 0.03


def shifted(value, axis, by):
    size = lax.axis_size(axis)
    pairs = [(i, i + by) for i in range(size) if 0 <= i + by < size]
    return lax.ppermute(value, axis, pairs)


def window(padded, axis, offset, width_x, width_y, width_z):
    start = [4, 4, 4]
    start[axis] = start[axis] + offset
    return padded[
        start[0] : start[0] + width_x, start[1] : start[1] + width_y, start[2] : start[2] + width_z
    ]


def stencil(extended, want_laplace):
    width_x = extended.shape[0] - 8
    width_y = extended.shape[1] - 8
    width_z = extended.shape[2]
    padded = jnp.pad(extended, ((0, 0), (0, 0), (4, 4)))
    centre = window(padded, 0, 0, width_x, width_y, width_z)
    laplace = 3.0 * laplace_coeffs[0] * centre
    slopes = []
    for axis in range(3):
        slope = jnp.zeros_like(centre)
        for offset in range(1, 5):
            upper = window(padded, axis, offset, width_x, width_y, width_z)
            lower = window(padded, axis, -offset, width_x, width_y, width_z)
            if want_laplace:
                laplace = laplace + laplace_coeffs[offset] * (upper + lower)
            slope = slope + slope_coeffs[offset - 1] * (upper - lower)
        slopes.append(slope)
    return (laplace, slopes)


def inject(receivers, topography, values, anchor_x, anchor_y, width_x, width_y, width_z):
    local_x = receivers[:, 0] - anchor_x
    local_y = receivers[:, 1] - anchor_y
    inside = (local_x >= 0) & (local_x < width_x) & (local_y >= 0) & (local_y < width_y)
    safe_x = jnp.clip(local_x, 0, width_x - 1)
    safe_y = jnp.clip(local_y, 0, width_y - 1)
    column = topography[safe_x, safe_y] + 1
    flat = jnp.where(
        inside, (safe_x * width_y + safe_y) * width_z + column, width_x * width_y * width_z
    )
    placed = (
        jnp.zeros((width_x * width_y * width_z,), jnp.float32).at[flat].add(values, mode="drop")
    )
    return placed.reshape(width_x, width_y, width_z)


def extend(stack):
    column_index = lax.axis_index("blk") % YBLOCKS
    below_x = shifted(stack[:, -4:], "blk", YBLOCKS)
    above_x = shifted(stack[:, :4], "blk", -YBLOCKS)
    below_y = shifted(stack[:, :, -4:], "blk", 1)
    above_y = shifted(stack[:, :, :4], "blk", -1)
    below_y = jnp.where(column_index > 0, below_y, 0.0)
    above_y = jnp.where(column_index < YBLOCKS - 1, above_y, 0.0)
    middle = jnp.concatenate([below_y, stack, above_y], axis=2)
    edge = ((0, 0), (0, 0), (4, 4), (0, 0))
    return jnp.concatenate([jnp.pad(below_x, edge), middle, jnp.pad(above_x, edge)], axis=1)


def shards(adjoint_in, forward, modulus, buoyancy, topography, receivers, residuals):
    modulus = modulus[0]
    buoyancy = buoyancy[0]
    topography = topography[0]
    width_x, width_y, width_z = modulus.shape
    index = lax.axis_index("blk")
    anchor_x = index // YBLOCKS * width_x
    anchor_y = index % YBLOCKS * width_y
    depth = lax.broadcasted_iota(jnp.int32, (width_x, width_y, width_z), 2)
    mask = (depth >= topography[:, :, None]).astype(jnp.float32)
    fields = forward[0, :, 0]
    later = adjoint_in[0, 0, 0]
    current = adjoint_in[0, 1, 0]
    image_mod = jnp.zeros((width_x, width_y, width_z), jnp.float32)
    image_buo = jnp.zeros((width_x, width_y, width_z), jnp.float32)
    statics = jnp.concatenate([buoyancy[None], fields[1 : STEPS + 1]], axis=0)
    fixed = extend(statics)
    grad_buoy = stencil(fixed[0], False)[1]
    states = []
    for level in range(STEPS):
        scaled = mask * modulus * current
        adjoint_ext = extend(scaled[None])[0]
        forward_ext = fixed[level + 1]
        laplace, slopes = stencil(adjoint_ext, True)
        operated = buoyancy * laplace
        for axis in range(3):
            operated = operated + grad_buoy[axis] * slopes[axis]
        source = inject(
            receivers,
            topography,
            residuals[0, level],
            anchor_x,
            anchor_y,
            width_x,
            width_y,
            width_z,
        )
        earlier = mask * (2.0 * current - later + time_factor * operated + source)
        term_mod = current * (fields[level] - 2.0 * fields[level + 1] + fields[level + 2])
        forward_slopes = stencil(forward_ext, False)[1]
        term_buo = (
            forward_slopes[0] * slopes[0]
            + forward_slopes[1] * slopes[1]
            + forward_slopes[2] * slopes[2]
        )
        image_mod = image_mod + term_mod
        image_buo = image_buo + term_buo
        states.append(earlier)
        later = current
        current = earlier
    totals = lax.psum(jnp.stack([image_mod, image_buo]), "shot")
    image_mod = totals[0]
    image_buo = totals[1]
    return (image_mod[None], image_buo[None], jnp.stack(states)[None, :, None])


def solution(mesh):
    placed = (
        P(("grp", "shot"), None, "blk", None, None, None),
        P(("grp", "shot"), None, "blk", None, None, None),
        P(("grp", "blk"), None, None, None),
        P(("grp", "blk"), None, None, None),
        P(("grp", "blk"), None, None),
        P("grp", None),
        P(("grp", "shot"), None, None),
    )
    return jax.shard_map(
        shards,
        mesh=mesh,
        in_specs=placed,
        out_specs=(
            P(("grp", "blk"), None, None, None),
            P(("grp", "blk"), None, None, None),
            P(("grp", "shot"), None, "blk", None, None, None),
        ),
        check_vma=False,
    )
```

profile of v0, /device:TPU:4, one launch (start us, length us, event | category | flops | bytes accessed | tf_op | source)
XLA Modules:
  0.0 125.5 jit_solution(2702137016507478552)
XLA Ops:
  0.6 0.0 copy-start.1
  0.6 0.0 copy-start
  0.7 0.0 copy-start.2
  0.7 0.0 copy-start.4
  0.7 1.2 slice_bitcast_fusion.3
  1.8 0.0 copy-start.5
  1.8 1.6 %fusion.142 = (f32[3,8,4,256]{3,2,1,0:T(4,128)}, f32[3,8,4,256]{3,2,1,0:T(4,128)}) fusion(f32[2,8,32,256]{3,2,1,0:T(8,128)S(1)} %slice_bitcast_fusion.3, f32[1,8,32,256]{3,2,1,0:T(8,128)} %param.10), kind=kLoop, calls=%fused_computation.250 | loop fusion | flops 49152 | bytes 983040 | tf_op jit(solution)/shard_map/concatenate | solution.py:93
  3.4 2.8 %collective-permute-start.6 = (f32[3,8,4,256]{3,2,1,0:T(4,128)}, f32[3,8,4,256]{3,2,1,0:T(4,128)}, u32[]{:S(2)}, u32[]{:S(2)}) collective-permute-start(f32[3,8,4,256]{3,2,1,0:T(4,128)} %get-tuple-element.18), channel_id=1, source_target_pairs={{1,0},{2,1},{3,2},{4,3},{5,4},{6,5},{7,6},{8,7},{9,8},{10,9},{11,1... | collective-permute-start | bytes 294920 | tf_op jit(solution)/shard_map/ppermute | solution.py:18
  6.2 1.9 %collective-permute-start.5 = (f32[3,8,4,256]{3,2,1,0:T(4,128)}, f32[3,8,4,256]{3,2,1,0:T(4,128)S(1)}, u32[]{:S(2)}, u32[]{:S(2)}) collective-permute-start(f32[3,8,4,256]{3,2,1,0:T(4,128)} %get-tuple-element.17), channel_id=1, source_target_pairs={{0,1},{1,2},{2,3},{3,4},{4,5},{5,6},{6,7},{7,8},{8,9},{9,10},{10,1... | collective-permute-start | bytes 294920 | tf_op jit(solution)/shard_map/ppermute | solution.py:18
  8.1 0.0 copy-done.1
  8.2 0.9 fusion.2
  9.1 4.3 %collective-permute-start.4 = (f32[3,4,32,256]{3,2,1,0:T(8,128)}, f32[3,4,32,256]{3,2,1,0:T(8,128)S(1)}, u32[]{:S(2)}, u32[]{:S(2)}) collective-permute-start(f32[3,4,32,256]{3,2,1,0:T(8,128)} %get-tuple-element.19), channel_id=1, source_target_pairs={{0,4},{1,5},{2,6},{3,7},{4,8},{5,9},{6,10},{7,11},{8,12},{9,13},{1... | collective-permute-start | bytes 1179656 | tf_op jit(solution)/shard_map/ppermute | solution.py:18
  13.4 1.9 %collective-permute-start.7 = (f32[3,4,32,256]{3,2,1,0:T(8,128)}, f32[3,4,32,256]{3,2,1,0:T(8,128)S(1)}, u32[]{:S(2)}, u32[]{:S(2)}) collective-permute-start(f32[3,4,32,256]{3,2,1,0:T(8,128)} %get-tuple-element.20), channel_id=1, source_target_pairs={{4,0},{5,1},{6,2},{7,3},{8,4},{9,5},{10,6},{11,7},{12,8},{13,9},{1... | collective-permute-start | bytes 1179656 | tf_op jit(solution)/shard_map/ppermute | solution.py:18
  15.3 0.0 copy-done
  15.3 0.0 copy-done.2
  15.3 0.0 copy-done.4
  15.4 0.1 bitcast_multiply_fusion
  15.5 0.6 fusion.154
  16.1 3.6 %collective-permute-start.2 = (f32[1,8,4,256]{3,2,1,0:T(4,128)}, f32[1,8,4,256]{3,2,1,0:T(4,128)}, u32[]{:S(2)}, u32[]{:S(2)}) collective-permute-start(f32[1,8,4,256]{3,2,1,0:T(4,128)} %get-tuple-element.26), channel_id=1, source_target_pairs={{1,0},{2,1},{3,2},{4,3},{5,4},{6,5},{7,6},{8,7},{9,8},{10,9},{11,1... | collective-permute-start | bytes 98312 | tf_op jit(solution)/shard_map/ppermute | solution.py:18
  19.8 0.0 copy-done.5
  19.8 0.1 fusion.145
  19.9 0.0 copy-start.6
  19.9 17.7 %gather_fusion = s32[4096]{0:T(1024)S(1)} fusion(s32[8,32]{1,0:T(8,128)S(1)} %bitcast.99, s32[4096]{0:T(1024)S(1)} %bitcast.102), kind=kCustom, calls=%fused_computation | custom fusion | bytes 65536 | tf_op jit(solution)/shard_map/gather | solution.py:55
  37.7 0.1 compare_select_fusion
  37.8 0.0 copy-done.6
  37.9 0.7 fusion.155
  38.6 22.0 %scatter_custom_fusion = f32[65536]{0:T(1024)S(1)} fusion(s32[4096]{0:T(1024)S(1)} %bitcast.106, f32[4096]{0:T(1024)S(1)} %bitcast.109, f32[]{:T(128)} %constant.27.clone.1), kind=kCustom, calls=%fused_computation.247 | custom fusion | flops 4096 | bytes 262148 | tf_op jit(solution)/shard_map/scatter-add | solution.py:60
  60.6 0.1 reshape.39
  60.7 22.0 %scatter_custom_fusion.1 = f32[65536]{0:T(1024)S(1)} fusion(s32[4096]{0:T(1024)S(1)} %bitcast.107, f32[4096]{0:T(1024)S(1)} %bitcast.108, f32[]{:T(128)} %constant.27.clone.1), kind=kCustom, calls=%fused_computation.245 | custom fusion | flops 4096 | bytes 262148 | tf_op jit(solution)/shard_map/scatter-add | solution.py:60
  82.6 0.1 reshape.40
  82.7 0.0 collective-permute-done.2
  82.7 1.9 %collective-permute-start.1 = (f32[1,8,4,256]{3,2,1,0:T(4,128)}, f32[1,8,4,256]{3,2,1,0:T(4,128)S(1)}, u32[]{:S(2)}, u32[]{:S(2)}) collective-permute-start(f32[1,8,4,256]{3,2,1,0:T(4,128)} %get-tuple-element.25), channel_id=1, source_target_pairs={{0,1},{1,2},{2,3},{3,4},{4,5},{5,6},{6,7},{7,8},{8,9},{9,10},{10,1... | collective-permute-start | bytes 98312 | tf_op jit(solution)/shard_map/ppermute | solution.py:18
  84.7 0.8 broadcast_select_fusion.4
  85.4 3.6 %collective-permute-done.1 = f32[1,8,4,256]{3,2,1,0:T(4,128)S(1)} collective-permute-done((f32[1,8,4,256]{3,2,1,0:T(4,128)}, f32[1,8,4,256]{3,2,1,0:T(4,128)S(1)}, u32[]{:S(2)}, u32[]{:S(2)}) %collective-permute-start.1) | collective-permute-done | bytes 32800 | tf_op jit(solution)/shard_map/ppermute | solution.py:18
  89.1 6.1 %collective-permute-start = (f32[1,4,32,256]{3,2,1,0:T(8,128)}, f32[1,4,32,256]{3,2,1,0:T(8,128)S(1)}, u32[]{:S(2)}, u32[]{:S(2)}) collective-permute-start(f32[1,4,32,256]{3,2,1,0:T(8,128)} %get-tuple-element.27), channel_id=1, source_target_pairs={{0,4},{1,5},{2,6},{3,7},{4,8},{5,9},{6,10},{7,11},{8,12},{9,13},{1... | collective-permute-start | bytes 393224 | tf_op jit(solution)/shard_map/ppermute | solution.py:18
  95.2 0.0 collective-permute-done.6
  95.2 1.9 %collective-permute-start.3 = (f32[1,4,32,256]{3,2,1,0:T(8,128)}, f32[1,4,32,256]{3,2,1,0:T(8,128)S(1)}, u32[]{:S(2)}, u32[]{:S(2)}) collective-permute-start(f32[1,4,32,256]{3,2,1,0:T(8,128)} %get-tuple-element.28), channel_id=1, source_target_pairs={{4,0},{5,1},{6,2},{7,3},{8,4},{9,5},{10,6},{11,7},{12,8},{13,9},{1... | collective-permute-start | bytes 393224 | tf_op jit(solution)/shard_map/ppermute | solution.py:18
  97.1 0.9 broadcast_select_fusion
  98.0 0.0 collective-permute-done.5
  98.1 0.0 collective-permute-done
  98.1 5.1 %collective-permute-done.3 = f32[1,4,32,256]{3,2,1,0:T(8,128)S(1)} collective-permute-done((f32[1,4,32,256]{3,2,1,0:T(8,128)}, f32[1,4,32,256]{3,2,1,0:T(8,128)S(1)}, u32[]{:S(2)}, u32[]{:S(2)}) %collective-permute-start.3) | collective-permute-done | bytes 131104 | tf_op jit(solution)/shard_map/ppermute | solution.py:18
  103.1 0.1 fusion.1
  103.2 0.0 collective-permute-done.4
  103.2 0.0 collective-permute-done.7
  103.2 0.3 select_maximum_fusion
  103.5 0.1 slice_bitcast_fusion
  103.7 0.0 copy-start.3
  103.7 2.4 %fusion.123 = (f32[1,8,32,256]{3,2,1,0:T(8,128)S(1)}, f32[8,32,256]{2,1,0:T(8,128)S(1)}, f32[8,32,256]{2,1,0:T(8,128)S(1)}, f32[8,32,256]{2,1,0:T(8,128)S(1)}, f...) fusion(f32[1,8,32,256]{3,2,1,0:T(8,128)S(1)} %copy-done.4, ...), kind=kLoop, calls=%fused_computation.215 | loop fusion | flops 7798784 | bytes 13373440 | tf_op jit(solution)/shard_map/broadcast_in_dim | solution.py:99
  106.1 1.9 %collective-permute-start.11 = (f32[1,4,32,256]{3,2,1,0:T(8,128)S(1)}, f32[1,4,32,256]{3,2,1,0:T(8,128)S(1)}, u32[]{:S(2)}, u32[]{:S(2)}) collective-permute-start(f32[1,4,32,256]{3,2,1,0:T(8,128)S(1)} %get-tuple-element.24), channel_id=1, source_target_pairs={{4,0},{5,1},{6,2},{7,3},{8,4},{9,5},{10,6},{11,7},{12,8},{13,9},{1... | collective-permute-start | bytes 393224 | tf_op jit(solution)/shard_map/ppermute | solution.py:18
  108.0 4.8 %collective-permute-start.8 = (f32[1,4,32,256]{3,2,1,0:T(8,128)S(1)}, f32[1,4,32,256]{3,2,1,0:T(8,128)S(1)}, u32[]{:S(2)}, u32[]{:S(2)}) collective-permute-start(f32[1,4,32,256]{3,2,1,0:T(8,128)S(1)} %get-tuple-element.23), channel_id=1, source_target_pairs={{0,4},{1,5},{2,6},{3,7},{4,8},{5,9},{6,10},{7,11},{8,12},{9,13},{1... | collective-permute-start | bytes 393224 | tf_op jit(solution)/shard_map/ppermute | solution.py:18
  112.8 1.9 %collective-permute-start.10 = (f32[1,8,4,256]{3,2,1,0:T(4,128)S(1)}, f32[1,8,4,256]{3,2,1,0:T(4,128)S(1)}, u32[]{:S(2)}, u32[]{:S(2)}) collective-permute-start(f32[1,8,4,256]{3,2,1,0:T(4,128)S(1)} %get-tuple-element.22), channel_id=1, source_target_pairs={{1,0},{2,1},{3,2},{4,3},{5,4},{6,5},{7,6},{8,7},{9,8},{10,9},{11,1... | collective-permute-start | bytes 98312 | tf_op jit(solution)/shard_map/ppermute | solution.py:18
  114.8 2.4 %collective-permute-start.9 = (f32[1,8,4,256]{3,2,1,0:T(4,128)S(1)}, f32[1,8,4,256]{3,2,1,0:T(4,128)S(1)}, u32[]{:S(2)}, u32[]{:S(2)}) collective-permute-start(f32[1,8,4,256]{3,2,1,0:T(4,128)S(1)} %get-tuple-element.21), channel_id=1, source_target_pairs={{0,1},{1,2},{2,3},{3,4},{4,5},{5,6},{6,7},{7,8},{8,9},{9,10},{10,1... | collective-permute-start | bytes 98312 | tf_op jit(solution)/shard_map/ppermute | solution.py:18
  117.2 0.0 copy-done.3
  117.2 0.8 fusion.126
  118.0 0.0 collective-permute-done.10
  118.0 2.9 %collective-permute-done.9 = f32[1,8,4,256]{3,2,1,0:T(4,128)S(1)} collective-permute-done((f32[1,8,4,256]{3,2,1,0:T(4,128)S(1)}, f32[1,8,4,256]{3,2,1,0:T(4,128)S(1)}, u32[]{:S(2)}, u32[]{:S(2)}) %collective-permute-start.9) | collective-permute-done | bytes 32800 | tf_op jit(solution)/shard_map/ppermute | solution.py:18
  120.9 0.0 collective-permute-done.11
  120.9 0.0 collective-permute-done.8
  120.9 0.1 fusion
  121.0 1.0 fusion.136
  122.0 0.8 maximum_bitcast_fusion
  122.9 2.7 %fusion.22 = f32[1,8,32,256]{3,2,1,0:T(8,128)} fusion(f32[8,32,256]{2,1,0:T(8,128)S(1)} %get-tuple-element.12, f32[16,40,256]{2,1,0:T(8,128)S(1)} %get-tuple-element.15, f32[16,40,256]{2,1,0:T(8,128)S(1)} %get-tuple-element.14, f32[8,32,256]{2,1,0:T(8,128)S(1)} %get-tuple-element.5, f32[8,32,256]{2,1,0:T(8,128)S(1)} %get-tuple-element.4, ...), kind=kLoop, calls=%fused_computation.87 | loop fusion | flops 5767168 | bytes 11927552 | tf_op jit(solution)/shard_map/stack | solution.py:128
  (8 shorter events, 0.1 us)
Async XLA Ops:
  0.6 7.5 %copy-start.1 = (f32[1,8,32,256]{3,2,1,0:T(8,128)S(1)}, f32[1,8,32,256]{3,2,1,0:T(8,128)}, u32[]{:S(2)}) copy-start(f32[1,8,32,256]{3,2,1,0:T(8,128)} %param.10) | copy-start | bytes 786436
  0.6 14.7 %copy-start = (s32[1,8,32]{2,1,0:T(8,128)S(1)}, s32[1,8,32]{2,1,0:T(8,128)}, u32[]{:S(2)}) copy-start(s32[1,8,32]{2,1,0:T(8,128)} %param.11) | copy-start | bytes 3076
  0.7 14.7 %copy-start.2 = (f32[1,2,1,8,32,256]{5,4,3,2,1,0:T(8,128)S(1)}, f32[1,2,1,8,32,256]{5,4,3,2,1,0:T(8,128)}, u32[]{:S(2)}) copy-start(f32[1,2,1,8,32,256]{5,4,3,2,1,0:T(8,128)} %param.7) | copy-start | bytes 1572868
  0.7 14.7 %copy-start.4 = (f32[1,8,32,256]{3,2,1,0:T(8,128)S(1)}, f32[1,8,32,256]{3,2,1,0:T(8,128)}, u32[]{:S(2)}) copy-start(f32[1,8,32,256]{3,2,1,0:T(8,128)} %param.9) | copy-start | bytes 786436
  1.8 17.9 %copy-start.5 = (s32[4096,2]{0,1:T(2,128)S(1)}, s32[4096,2]{0,1:T(2,128)}, u32[]{:S(2)}) copy-start(s32[4096,2]{0,1:T(2,128)} %param.12) | copy-start | bytes 98308
  3.4 91.7 %collective-permute-start.6 = (f32[3,8,4,256]{3,2,1,0:T(4,128)}, f32[3,8,4,256]{3,2,1,0:T(4,128)}, u32[]{:S(2)}, u32[]{:S(2)}) collective-permute-start(f32[3,8,4,256]{3,2,1,0:T(4,128)} %get-tuple-element.18), channel_id=1, source_target_pairs={{1,0},{2,1},{3,2},{4,3},{5,4},{6,5},{7,6},{8,7},{9,8},{10,9},{11,1... | collective-permute-start | bytes 294920 | tf_op jit(solution)/shard_map/ppermute | solution.py:18
  6.2 91.8 %collective-permute-start.5 = (f32[3,8,4,256]{3,2,1,0:T(4,128)}, f32[3,8,4,256]{3,2,1,0:T(4,128)S(1)}, u32[]{:S(2)}, u32[]{:S(2)}) collective-permute-start(f32[3,8,4,256]{3,2,1,0:T(4,128)} %get-tuple-element.17), channel_id=1, source_target_pairs={{0,1},{1,2},{2,3},{3,4},{4,5},{5,6},{6,7},{7,8},{8,9},{9,10},{10,1... | collective-permute-start | bytes 294920 | tf_op jit(solution)/shard_map/ppermute | solution.py:18
  9.1 94.1 %collective-permute-start.4 = (f32[3,4,32,256]{3,2,1,0:T(8,128)}, f32[3,4,32,256]{3,2,1,0:T(8,128)S(1)}, u32[]{:S(2)}, u32[]{:S(2)}) collective-permute-start(f32[3,4,32,256]{3,2,1,0:T(8,128)} %get-tuple-element.19), channel_id=1, source_target_pairs={{0,4},{1,5},{2,6},{3,7},{4,8},{5,9},{6,10},{7,11},{8,12},{9,13},{1... | collective-permute-start | bytes 1179656 | tf_op jit(solution)/shard_map/ppermute | solution.py:18
  13.4 89.8 %collective-permute-start.7 = (f32[3,4,32,256]{3,2,1,0:T(8,128)}, f32[3,4,32,256]{3,2,1,0:T(8,128)S(1)}, u32[]{:S(2)}, u32[]{:S(2)}) collective-permute-start(f32[3,4,32,256]{3,2,1,0:T(8,128)} %get-tuple-element.20), channel_id=1, source_target_pairs={{4,0},{5,1},{6,2},{7,3},{8,4},{9,5},{10,6},{11,7},{12,8},{13,9},{1... | collective-permute-start | bytes 1179656 | tf_op jit(solution)/shard_map/ppermute | solution.py:18
  16.1 66.6 %collective-permute-start.2 = (f32[1,8,4,256]{3,2,1,0:T(4,128)}, f32[1,8,4,256]{3,2,1,0:T(4,128)}, u32[]{:S(2)}, u32[]{:S(2)}) collective-permute-start(f32[1,8,4,256]{3,2,1,0:T(4,128)} %get-tuple-element.26), channel_id=1, source_target_pairs={{1,0},{2,1},{3,2},{4,3},{5,4},{6,5},{7,6},{8,7},{9,8},{10,9},{11,1... | collective-permute-start | bytes 98312 | tf_op jit(solution)/shard_map/ppermute | solution.py:18
  19.9 17.9 %copy-start.6 = (f32[1,2,4096]{2,1,0:T(2,128)S(1)}, f32[1,2,4096]{2,1,0:T(2,128)}, u32[]{:S(2)}) copy-start(f32[1,2,4096]{2,1,0:T(2,128)} %param.13) | copy-start | bytes 98308
  82.7 6.3 %collective-permute-start.1 = (f32[1,8,4,256]{3,2,1,0:T(4,128)}, f32[1,8,4,256]{3,2,1,0:T(4,128)S(1)}, u32[]{:S(2)}, u32[]{:S(2)}) collective-permute-start(f32[1,8,4,256]{3,2,1,0:T(4,128)} %get-tuple-element.25), channel_id=1, source_target_pairs={{0,1},{1,2},{2,3},{3,4},{4,5},{5,6},{6,7},{7,8},{8,9},{9,10},{10,1... | collective-permute-start | bytes 98312 | tf_op jit(solution)/shard_map/ppermute | solution.py:18
  89.1 9.0 %collective-permute-start = (f32[1,4,32,256]{3,2,1,0:T(8,128)}, f32[1,4,32,256]{3,2,1,0:T(8,128)S(1)}, u32[]{:S(2)}, u32[]{:S(2)}) collective-permute-start(f32[1,4,32,256]{3,2,1,0:T(8,128)} %get-tuple-element.27), channel_id=1, source_target_pairs={{0,4},{1,5},{2,6},{3,7},{4,8},{5,9},{6,10},{7,11},{8,12},{9,13},{1... | collective-permute-start | bytes 393224 | tf_op jit(solution)/shard_map/ppermute | solution.py:18
  95.2 8.0 %collective-permute-start.3 = (f32[1,4,32,256]{3,2,1,0:T(8,128)}, f32[1,4,32,256]{3,2,1,0:T(8,128)S(1)}, u32[]{:S(2)}, u32[]{:S(2)}) collective-permute-start(f32[1,4,32,256]{3,2,1,0:T(8,128)} %get-tuple-element.28), channel_id=1, source_target_pairs={{4,0},{5,1},{6,2},{7,3},{8,4},{9,5},{10,6},{11,7},{12,8},{13,9},{1... | collective-permute-start | bytes 393224 | tf_op jit(solution)/shard_map/ppermute | solution.py:18
  103.7 13.5 %copy-start.3 = (f32[1,4,1,8,32,256]{5,4,3,2,1,0:T(8,128)S(1)}, f32[1,4,1,8,32,256]{5,4,3,2,1,0:T(8,128)}, u32[]{:S(2)}) copy-start(f32[1,4,1,8,32,256]{5,4,3,2,1,0:T(8,128)} %param.8) | copy-start | bytes 3145732
  106.1 14.8 %collective-permute-start.11 = (f32[1,4,32,256]{3,2,1,0:T(8,128)S(1)}, f32[1,4,32,256]{3,2,1,0:T(8,128)S(1)}, u32[]{:S(2)}, u32[]{:S(2)}) collective-permute-start(f32[1,4,32,256]{3,2,1,0:T(8,128)S(1)} %get-tuple-element.24), channel_id=1, source_target_pairs={{4,0},{5,1},{6,2},{7,3},{8,4},{9,5},{10,6},{11,7},{12,8},{13,9},{1... | collective-permute-start | bytes 393224 | tf_op jit(solution)/shard_map/ppermute | solution.py:18
  108.0 12.9 %collective-permute-start.8 = (f32[1,4,32,256]{3,2,1,0:T(8,128)S(1)}, f32[1,4,32,256]{3,2,1,0:T(8,128)S(1)}, u32[]{:S(2)}, u32[]{:S(2)}) collective-permute-start(f32[1,4,32,256]{3,2,1,0:T(8,128)S(1)} %get-tuple-element.23), channel_id=1, source_target_pairs={{0,4},{1,5},{2,6},{3,7},{4,8},{5,9},{6,10},{7,11},{8,12},{9,13},{1... | collective-permute-start | bytes 393224 | tf_op jit(solution)/shard_map/ppermute | solution.py:18
  112.8 5.2 %collective-permute-start.10 = (f32[1,8,4,256]{3,2,1,0:T(4,128)S(1)}, f32[1,8,4,256]{3,2,1,0:T(4,128)S(1)}, u32[]{:S(2)}, u32[]{:S(2)}) collective-permute-start(f32[1,8,4,256]{3,2,1,0:T(4,128)S(1)} %get-tuple-element.22), channel_id=1, source_target_pairs={{1,0},{2,1},{3,2},{4,3},{5,4},{6,5},{7,6},{8,7},{9,8},{10,9},{11,1... | collective-permute-start | bytes 98312 | tf_op jit(solution)/shard_map/ppermute | solution.py:18
  114.8 6.1 %collective-permute-start.9 = (f32[1,8,4,256]{3,2,1,0:T(4,128)S(1)}, f32[1,8,4,256]{3,2,1,0:T(4,128)S(1)}, u32[]{:S(2)}, u32[]{:S(2)}) collective-permute-start(f32[1,8,4,256]{3,2,1,0:T(4,128)S(1)} %get-tuple-element.21), channel_id=1, source_target_pairs={{0,1},{1,2},{2,3},{3,4},{4,5},{5,6},{6,7},{7,8},{8,9},{9,10},{10,1... | collective-permute-start | bytes 98312 | tf_op jit(solution)/shard_map/ppermute | solution.py:18
where the time goes:
time: 126 us
  other arithmetic  56.7 us (45%)
  starting transfers between devices  35.5 us (28%)
  local copies, waits for them, and re-layouts  20.7 us (16%)
  waiting for transfers between devices  11.6 us (9%)
    scatter-add x2, other arithmetic, inject(): jnp.zeros((width_x * width_y * width_z,), jnp.float32).at[flat]  43.9 us
    ppermute x12, starting transfers between devices, shifted(): return lax.ppermute(value, axis, pairs)  35.5 us
    gather x1, local copies, waits for them, and re-layouts, inject(): column = topography[safe_x, safe_y] + 1  17.7 us
    ppermute x12, waiting for transfers between devices, shifted(): return lax.ppermute(value, axis, pairs)  11.6 us
    another operation x2, other arithmetic, shards(): totals = lax.psum(jnp.stack([image_mod, image_buo]), 'shot')  3.48 us
  transfers between devices with their start and end apart: 12, of which 3 were waited for; matrix products, arithmetic and copies ran while one was open for 54% of the time, Pallas kernels for 0%

commit v1 on v0

--- a/solution.py
+++ b/solution.py
@@ -47,19 +47,16 @@
 
 
 def inject(receivers, topography, values, anchor_x, anchor_y, width_x, width_y, width_z):
-    local_x = receivers[:, 0] - anchor_x
-    local_y = receivers[:, 1] - anchor_y
-    inside = (local_x >= 0) & (local_x < width_x) & (local_y >= 0) & (local_y < width_y)
-    safe_x = jnp.clip(local_x, 0, width_x - 1)
-    safe_y = jnp.clip(local_y, 0, width_y - 1)
-    column = topography[safe_x, safe_y] + 1
-    flat = jnp.where(
-        inside, (safe_x * width_y + safe_y) * width_z + column, width_x * width_y * width_z
+    in_x = receivers[:, 0][None, :] - anchor_x == lax.broadcasted_iota(jnp.int32, (width_x, 1), 0)
+    in_y = receivers[:, 1][None, :] - anchor_y == lax.broadcasted_iota(jnp.int32, (width_y, 1), 0)
+    plane = lax.dot_general(
+        jnp.where(in_x, values[None, :], 0.0),
+        in_y.astype(jnp.float32),
+        (((1,), (1,)), ((), ())),
+        precision=lax.Precision.HIGHEST,
     )
-    placed = (
-        jnp.zeros((width_x * width_y * width_z,), jnp.float32).at[flat].add(values, mode="drop")
-    )
-    return placed.reshape(width_x, width_y, width_z)
+    depth = lax.broadcasted_iota(jnp.int32, (width_x, width_y, width_z), 2)
+    return jnp.where(depth == topography[:, :, None] + 1, plane[:, :, None], 0.0)
 
 
 def extend(stack):

time: 126 us -> 67.9 us (0.54)
  other arithmetic: 56.7 us -> 12.8 us
  local copies, waits for them, and re-layouts: 20.7 us -> 4.12 us
  matrix products: 0 us -> 2.15 us
    scatter-add x2 -> x0, other arithmetic: 43.9 us -> none  [inject(): jnp.zeros((width_x * width_y * width_z,), jnp.float32).at[flat]]
    gather x1 -> x0, local copies, waits for them, and re-layouts: 17.7 us -> none  [inject(): column = topography[safe_x, safe_y] + 1]
    dot_general x0 -> x2, matrix products: none -> 2.15 us  [inject(): lax.dot_general(jnp.where(in_x, values[None, :], 0.0), in_y.astype(jnp.fl...]
    slice x1, local copies, waits for them, and re-layouts: 0.03 us -> 1.46 us  [shards(): residuals[0, level]]
  transfers between devices with their start and end apart: 12 -> 12, of which waited for: 3 -> 3; matrix products, arithmetic and copies ran while one was open for 54% -> 13% of each run, Pallas kernels for 0% -> 0%
where the time goes in v1:
time: 67.9 us; the launch traced here: 67.1 us
  starting transfers between devices  35.4 us (52%)
  other arithmetic  12.8 us (19%)
  waiting for transfers between devices  11.5 us (17%)
  local copies, waits for them, and re-layouts  4.12 us (6%)
  matrix products  2.15 us (3%)
  between operations  1 us (1%)
    ppermute x12, starting transfers between devices, shifted(): return lax.ppermute(value, axis, pairs)  35.4 us
    ppermute x12, waiting for transfers between devices, shifted(): return lax.ppermute(value, axis, pairs)  11.5 us
    another operation x2, other arithmetic, shards(): totals = lax.psum(jnp.stack([image_mod, image_buo]), 'shot')  3.5 us
    broadcast_in_dim x1, other arithmetic, shards(): adjoint_ext = extend(scaled[None])[0]  2.58 us
    dot_general x2, matrix products, inject(): lax.dot_general(jnp.where(in_x, values[None, :], 0.0), in_y.astype(jnp.fl...  2.15 us
    select_n x3, other arithmetic, extend(): above_y = jnp.where(column_index < YBLOCKS - 1, above_y, 0.0)  1.71 us
    concatenate x2, other arithmetic, shards(): statics = jnp.concatenate([buoyancy[None], fields[1:STEPS + 1]], axis=0)  1.65 us
    slice x1, local copies, waits for them, and re-layouts, shards(): residuals[0, level]  1.46 us
  transfers between devices with their start and end apart: 12, of which 3 were waited for; matrix products, arithmetic and copies ran while one was open for 13% of the time, Pallas kernels for 0%

profile of v1, /device:TPU:4, one launch (start us, length us, event | category | flops | bytes accessed | tf_op | source)
XLA Modules:
  0.0 67.1 jit_solution(2789720949993204794)
XLA Ops:
  0.6 0.0 copy-start
  0.6 0.0 copy-start.4
  0.7 0.0 copy-start.1
  0.7 0.0 copy-start.3
  0.7 1.2 %slice_bitcast_fusion.3 = f32[2,8,32,256]{3,2,1,0:T(8,128)S(1)} fusion(f32[1,4,1,8,32,256]{5,4,3,1,2,0:T(8,128)} %bitcast.99), kind=kLoop, calls=%fused_computation.61 | loop fusion | bytes 1048576 | tf_op jit(solution)/shard_map/slice | solution.py:90
  1.8 1.6 %fusion.144 = (f32[3,8,4,256]{3,2,1,0:T(4,128)}, f32[3,8,4,256]{3,2,1,0:T(4,128)}) fusion(f32[2,8,32,256]{3,2,1,0:T(8,128)S(1)} %slice_bitcast_fusion.3, f32[1,8,32,256]{3,2,1,0:T(8,128)} %param.10), kind=kLoop, calls=%fused_computation.252 | loop fusion | flops 49152 | bytes 983040 | tf_op jit(solution)/shard_map/concatenate | solution.py:90
  3.4 2.8 %collective-permute-start.6 = (f32[3,8,4,256]{3,2,1,0:T(4,128)}, f32[3,8,4,256]{3,2,1,0:T(4,128)}, u32[]{:S(2)}, u32[]{:S(2)}) collective-permute-start(f32[3,8,4,256]{3,2,1,0:T(4,128)} %get-tuple-element.18), channel_id=1, source_target_pairs={{1,0},{2,1},{3,2},{4,3},{5,4},{6,5},{7,6},{8,7},{9,8},{10,9},{11,1... | collective-permute-start | bytes 294920 | tf_op jit(solution)/shard_map/ppermute | solution.py:18
  6.2 1.9 %collective-permute-start.5 = (f32[3,8,4,256]{3,2,1,0:T(4,128)}, f32[3,8,4,256]{3,2,1,0:T(4,128)}, u32[]{:S(2)}, u32[]{:S(2)}) collective-permute-start(f32[3,8,4,256]{3,2,1,0:T(4,128)} %get-tuple-element.17), channel_id=1, source_target_pairs={{0,1},{1,2},{2,3},{3,4},{4,5},{5,6},{6,7},{7,8},{8,9},{9,10},{10,1... | collective-permute-start | bytes 294920 | tf_op jit(solution)/shard_map/ppermute | solution.py:18
  8.1 0.0 copy-done
  8.2 0.1 fusion.4
  8.2 4.3 %collective-permute-start.4 = (f32[3,4,32,256]{3,2,1,0:T(8,128)S(1)}, f32[3,4,32,256]{3,2,1,0:T(8,128)S(1)}, u32[]{:S(2)}, u32[]{:S(2)}) collective-permute-start(f32[3,4,32,256]{3,2,1,0:T(8,128)S(1)} %get-tuple-element.19), channel_id=1, source_target_pairs={{0,4},{1,5},{2,6},{3,7},{4,8},{5,9},{6,10},{7,11},{8,12},{9,13},{1... | collective-permute-start | bytes 1179656 | tf_op jit(solution)/shard_map/ppermute | solution.py:18
  12.6 1.9 %collective-permute-start.7 = (f32[3,4,32,256]{3,2,1,0:T(8,128)S(1)}, f32[3,4,32,256]{3,2,1,0:T(8,128)S(1)}, u32[]{:S(2)}, u32[]{:S(2)}) collective-permute-start(f32[3,4,32,256]{3,2,1,0:T(8,128)S(1)} %get-tuple-element.20), channel_id=1, source_target_pairs={{4,0},{5,1},{6,2},{7,3},{8,4},{9,5},{10,6},{11,7},{12,8},{13,9},{1... | collective-permute-start | bytes 1179656 | tf_op jit(solution)/shard_map/ppermute | solution.py:18
  14.5 0.0 copy-done.4
  14.5 0.0 copy-done.1
  14.5 0.0 copy-done.3
  14.5 0.1 bitcast_multiply_fusion
  14.6 0.6 fusion.159
  15.3 3.6 %collective-permute-start.2 = (f32[1,8,4,256]{3,2,1,0:T(4,128)}, f32[1,8,4,256]{3,2,1,0:T(4,128)}, u32[]{:S(2)}, u32[]{:S(2)}) collective-permute-start(f32[1,8,4,256]{3,2,1,0:T(4,128)} %get-tuple-element.26), channel_id=1, source_target_pairs={{1,0},{2,1},{3,2},{4,3},{5,4},{6,5},{7,6},{8,7},{9,8},{10,9},{11,1... | collective-permute-start | bytes 98312 | tf_op jit(solution)/shard_map/ppermute | solution.py:18
  18.9 0.7 %fusion.160 = (f32[1,4,32,256]{3,2,1,0:T(8,128)}, f32[1,4,32,256]{3,2,1,0:T(8,128)S(1)}) fusion(f32[1,8,32,256]{3,2,1,0:T(8,128)S(1)} %bitcast_multiply_fusion), kind=kLoop, calls=%fused_computation.273 | loop fusion | bytes 524288 | tf_op jit(solution)/shard_map/slice | solution.py:64
  19.6 1.5 %fusion.161 = (f32[1,1,4096]{2,1,0:T(1,128)}, f32[1,1,4096]{2,1,0:T(1,128)}) fusion(f32[1,2,4096]{2,1,0:T(2,128)} %param.13), kind=kLoop, calls=%fused_computation.274 | loop fusion | bytes 65536 | tf_op jit(solution)/shard_map/slice | solution.py:105
  21.1 0.9 %slice_subtract_fusion.25 = (s32[4096,1]{0,1:T(1,128)S(1)}, s32[4096,1]{0,1:T(1,128)S(1)}) fusion(s32[4096,2]{0,1:T(2,128)} %param.12, s32[]{:T(128)S(6)} %mul.396, s32[]{:T(128)S(6)} %mul.397), kind=kLoop, calls=%fused_computation.262 | loop fusion | flops 8192 | bytes 65544 | tf_op jit(solution)/shard_map/sub | solution.py:50
  21.9 1.1 %fusion.3 = f32[8,32]{1,0:T(8,128)S(1)} fusion(s32[4096]{0:T(1024)S(1)} %bitcast.107, f32[4096]{0:T(1024)} %bitcast.104, s32[4096]{0:T(1024)S(1)} %bitcast.105), kind=kOutput, calls=%fused_computation.65 | convolution fusion | flops 12779520 | bytes 50176 | tf_op jit(solution)/shard_map/dot_general | solution.py:52
  23.0 1.1 %fusion.2 = f32[8,32]{1,0:T(8,128)S(1)} fusion(s32[4096]{0:T(1024)S(1)} %bitcast.108, f32[4096]{0:T(1024)} %bitcast.103, s32[4096]{0:T(1024)S(1)} %bitcast.106), kind=kOutput, calls=%fused_computation.64 | convolution fusion | flops 12779520 | bytes 50176 | tf_op jit(solution)/shard_map/dot_general | solution.py:52
  24.1 0.0 collective-permute-done.2
  24.1 1.9 %collective-permute-start.1 = (f32[1,8,4,256]{3,2,1,0:T(4,128)}, f32[1,8,4,256]{3,2,1,0:T(4,128)S(1)}, u32[]{:S(2)}, u32[]{:S(2)}) collective-permute-start(f32[1,8,4,256]{3,2,1,0:T(4,128)} %get-tuple-element.25), channel_id=1, source_target_pairs={{0,1},{1,2},{2,3},{3,4},{4,5},{5,6},{6,7},{7,8},{8,9},{9,10},{10,1... | collective-permute-start | bytes 98312 | tf_op jit(solution)/shard_map/ppermute | solution.py:18
  26.0 0.8 %broadcast_select_fusion.4 = f32[1,8,4,256]{3,2,1,0:T(4,128)S(1)} fusion(f32[1,8,4,256]{3,2,1,0:T(4,128)} %collective-permute-done.2, pred[]{:T(512)S(6)} %lt.18), kind=kLoop, calls=%fused_computation.265 | loop fusion | flops 8192 | bytes 65537 | tf_op jit(solution)/shard_map/jit(_where)/select_n | solution.py:69
  26.8 3.7 %collective-permute-done.1 = f32[1,8,4,256]{3,2,1,0:T(4,128)S(1)} collective-permute-done((f32[1,8,4,256]{3,2,1,0:T(4,128)}, f32[1,8,4,256]{3,2,1,0:T(4,128)S(1)}, u32[]{:S(2)}, u32[]{:S(2)}) %collective-permute-start.1) | collective-permute-done | bytes 32800 | tf_op jit(solution)/shard_map/ppermute | solution.py:18
  30.6 5.9 %collective-permute-start = (f32[1,4,32,256]{3,2,1,0:T(8,128)}, f32[1,4,32,256]{3,2,1,0:T(8,128)S(1)}, u32[]{:S(2)}, u32[]{:S(2)}) collective-permute-start(f32[1,4,32,256]{3,2,1,0:T(8,128)} %get-tuple-element.27), channel_id=1, source_target_pairs={{0,4},{1,5},{2,6},{3,7},{4,8},{5,9},{6,10},{7,11},{8,12},{9,13},{1... | collective-permute-start | bytes 393224 | tf_op jit(solution)/shard_map/ppermute | solution.py:18
  36.5 0.0 collective-permute-done.6
  36.5 1.9 %collective-permute-start.3 = (f32[1,4,32,256]{3,2,1,0:T(8,128)S(1)}, f32[1,4,32,256]{3,2,1,0:T(8,128)S(1)}, u32[]{:S(2)}, u32[]{:S(2)}) collective-permute-start(f32[1,4,32,256]{3,2,1,0:T(8,128)S(1)} %get-tuple-element.28), channel_id=1, source_target_pairs={{4,0},{5,1},{6,2},{7,3},{8,4},{9,5},{10,6},{11,7},{12,8},{13,9},{1... | collective-permute-start | bytes 393224 | tf_op jit(solution)/shard_map/ppermute | solution.py:18
  38.5 0.9 %broadcast_select_fusion = f32[3,8,4,256]{3,2,1,0:T(4,128)S(1)} fusion(f32[3,8,4,256]{3,2,1,0:T(4,128)} %collective-permute-done.6, pred[]{:T(512)S(6)} %lt.18), kind=kLoop, calls=%fused_computation.259 | loop fusion | flops 24576 | bytes 196609 | tf_op jit(solution)/shard_map/jit(_where)/select_n | solution.py:69
  39.4 0.0 collective-permute-done.5
  39.5 0.0 collective-permute-done
  39.5 4.8 %collective-permute-done.3 = f32[1,4,32,256]{3,2,1,0:T(8,128)S(1)} collective-permute-done((f32[1,4,32,256]{3,2,1,0:T(8,128)S(1)}, f32[1,4,32,256]{3,2,1,0:T(8,128)S(1)}, u32[]{:S(2)}, u32[]{:S(2)}) %collective-permute-start.3) | collective-permute-done | bytes 131104 | tf_op jit(solution)/shard_map/ppermute | solution.py:18
  44.3 0.1 fusion.1
  44.4 0.0 collective-permute-done.4
  44.4 0.0 collective-permute-done.7
  44.4 0.2 select_maximum_fusion
  44.6 0.1 slice_bitcast_fusion
  44.8 0.0 copy-start.2
  44.8 2.6 %fusion.125 = (f32[1,8,32,256]{3,2,1,0:T(8,128)S(1)}, f32[8,32,256]{2,1,0:T(8,128)S(1)}, f32[8,32,256]{2,1,0:T(8,128)S(1)}, f32[8,32,256]{2,1,0:T(8,128)S(1)}, f...) fusion(f32[1,8,32,256]{3,2,1,0:T(8,128)S(1)} %copy-done.3, ...), kind=kLoop, calls=%fused_computation.215 | loop fusion | flops 7929856 | bytes 13119488 | tf_op jit(solution)/shard_map/broadcast_in_dim | solution.py:96
  47.4 1.9 %collective-permute-start.11 = (f32[1,4,32,256]{3,2,1,0:T(8,128)S(1)}, f32[1,4,32,256]{3,2,1,0:T(8,128)S(1)}, u32[]{:S(2)}, u32[]{:S(2)}) collective-permute-start(f32[1,4,32,256]{3,2,1,0:T(8,128)S(1)} %get-tuple-element.24), channel_id=1, source_target_pairs={{4,0},{5,1},{6,2},{7,3},{8,4},{9,5},{10,6},{11,7},{12,8},{13,9},{1... | collective-permute-start | bytes 393224 | tf_op jit(solution)/shard_map/ppermute | solution.py:18
  49.3 4.8 %collective-permute-start.8 = (f32[1,4,32,256]{3,2,1,0:T(8,128)S(1)}, f32[1,4,32,256]{3,2,1,0:T(8,128)S(1)}, u32[]{:S(2)}, u32[]{:S(2)}) collective-permute-start(f32[1,4,32,256]{3,2,1,0:T(8,128)S(1)} %get-tuple-element.23), channel_id=1, source_target_pairs={{0,4},{1,5},{2,6},{3,7},{4,8},{5,9},{6,10},{7,11},{8,12},{9,13},{1... | collective-permute-start | bytes 393224 | tf_op jit(solution)/shard_map/ppermute | solution.py:18
  54.2 1.9 %collective-permute-start.10 = (f32[1,8,4,256]{3,2,1,0:T(4,128)S(1)}, f32[1,8,4,256]{3,2,1,0:T(4,128)S(1)}, u32[]{:S(2)}, u32[]{:S(2)}) collective-permute-start(f32[1,8,4,256]{3,2,1,0:T(4,128)S(1)} %get-tuple-element.22), channel_id=1, source_target_pairs={{1,0},{2,1},{3,2},{4,3},{5,4},{6,5},{7,6},{8,7},{9,8},{10,9},{11,1... | collective-permute-start | bytes 98312 | tf_op jit(solution)/shard_map/ppermute | solution.py:18
  56.1 2.4 %collective-permute-start.9 = (f32[1,8,4,256]{3,2,1,0:T(4,128)S(1)}, f32[1,8,4,256]{3,2,1,0:T(4,128)S(1)}, u32[]{:S(2)}, u32[]{:S(2)}) collective-permute-start(f32[1,8,4,256]{3,2,1,0:T(4,128)S(1)} %get-tuple-element.21), channel_id=1, source_target_pairs={{0,1},{1,2},{2,3},{3,4},{4,5},{5,6},{6,7},{7,8},{8,9},{9,10},{10,1... | collective-permute-start | bytes 98312 | tf_op jit(solution)/shard_map/ppermute | solution.py:18
  58.5 0.0 copy-done.2
  58.5 0.8 %fusion.128 = f32[1,8,32,256]{3,2,1,0:T(8,128)} fusion(f32[8,32,256]{2,1,0:T(8,128)S(1)} %get-tuple-element.7, f32[1,4,1,8,32,256]{5,4,3,2,1,0:T(8,128)S(1)} %copy-done.2, f32[1,2,1,8,32,256]{5,4,3,2,1,0:T(8,128)S(1)} %copy-done.1), kind=kLoop, calls=%fused_computation.219 | loop fusion | flops 589824 | bytes 1835008 | tf_op jit(solution)/shard_map/stack | solution.py:125
  59.3 0.0 collective-permute-done.10
  59.4 2.9 %collective-permute-done.9 = f32[1,8,4,256]{3,2,1,0:T(4,128)S(1)} collective-permute-done((f32[1,8,4,256]{3,2,1,0:T(4,128)S(1)}, f32[1,8,4,256]{3,2,1,0:T(4,128)S(1)}, u32[]{:S(2)}, u32[]{:S(2)}) %collective-permute-start.9) | collective-permute-done | bytes 32800 | tf_op jit(solution)/shard_map/ppermute | solution.py:18
  62.2 0.0 collective-permute-done.11
  62.3 0.0 collective-permute-done.8
  62.3 0.1 fusion
  62.3 1.2 %fusion.138 = (f32[1,8,32,256]{3,2,1,0:T(8,128)S(1)}, f32[8,32,256]{2,1,0:T(8,128)S(1)}, f32[8,32,256]{2,1,0:T(8,128)S(1)}) fusion(f32[8,32,256]{2,1,0:T(8,128)S(1)} %get-tuple-element.13, f32[16,40,256]{2,1,0:T(8,128)S(1)} %fusion, f32[1,8,32,256]{3,2,1,0:T(8,128)S(1)} %copy-done, f32[8,32,256]{2,1,0:T(8,128)S(1)} %get-tuple-element.11, ...), kind=kLoop, calls=%fused_computation.236 | loop fusion | flops 5636096 | bytes 7483392 | tf_op jit(solution)/shard_map/stack | solution.py:128
  63.5 0.8 %maximum_bitcast_fusion = f32[1,2,1,8,32,256]{5,4,3,2,1,0:T(8,128)} fusion(f32[1,8,32,256]{3,2,1,0:T(8,128)S(1)} %get-tuple-element.3, f32[1,8,32,256]{3,2,1,0:T(8,128)S(1)} %bitcast.98), kind=kLoop, calls=%fused_computation.62 | loop fusion | flops 131072 | bytes 1048576 | tf_op jit(solution)/shard_map/broadcast_in_dim | solution.py:128
  64.4 2.7 %fusion.24 = f32[1,8,32,256]{3,2,1,0:T(8,128)} fusion(f32[8,32,256]{2,1,0:T(8,128)S(1)} %get-tuple-element.12, f32[16,40,256]{2,1,0:T(8,128)S(1)} %get-tuple-element.15, f32[16,40,256]{2,1,0:T(8,128)S(1)} %get-tuple-element.14, f32[8,32,256]{2,1,0:T(8,128)S(1)} %get-tuple-element.5, f32[8,32,256]{2,1,0:T(8,128)S(1)} %get-tuple-element.4, ...), kind=kLoop, calls=%fused_computation.87 | loop fusion | flops 5767168 | bytes 11927552 | tf_op jit(solution)/shard_map/stack | solution.py:125
  (7 shorter events, 0.1 us)
Async XLA Ops:
  0.6 7.5 %copy-start = (f32[1,8,32,256]{3,2,1,0:T(8,128)S(1)}, f32[1,8,32,256]{3,2,1,0:T(8,128)}, u32[]{:S(2)}) copy-start(f32[1,8,32,256]{3,2,1,0:T(8,128)} %param.10) | copy-start | bytes 786436
  0.6 13.8 %copy-start.4 = (s32[1,8,32]{2,1,0:T(8,128)S(1)}, s32[1,8,32]{2,1,0:T(8,128)}, u32[]{:S(2)}) copy-start(s32[1,8,32]{2,1,0:T(8,128)} %param.11) | copy-start | bytes 3076
  0.7 13.8 %copy-start.1 = (f32[1,2,1,8,32,256]{5,4,3,2,1,0:T(8,128)S(1)}, f32[1,2,1,8,32,256]{5,4,3,2,1,0:T(8,128)}, u32[]{:S(2)}) copy-start(f32[1,2,1,8,32,256]{5,4,3,2,1,0:T(8,128)} %param.7) | copy-start | bytes 1572868
  0.7 13.8 %copy-start.3 = (f32[1,8,32,256]{3,2,1,0:T(8,128)S(1)}, f32[1,8,32,256]{3,2,1,0:T(8,128)}, u32[]{:S(2)}) copy-start(f32[1,8,32,256]{3,2,1,0:T(8,128)} %param.9) | copy-start | bytes 786436
  3.4 33.1 %collective-permute-start.6 = (f32[3,8,4,256]{3,2,1,0:T(4,128)}, f32[3,8,4,256]{3,2,1,0:T(4,128)}, u32[]{:S(2)}, u32[]{:S(2)}) collective-permute-start(f32[3,8,4,256]{3,2,1,0:T(4,128)} %get-tuple-element.18), channel_id=1, source_target_pairs={{1,0},{2,1},{3,2},{4,3},{5,4},{6,5},{7,6},{8,7},{9,8},{10,9},{11,1... | collective-permute-start | bytes 294920 | tf_op jit(solution)/shard_map/ppermute | solution.py:18
  6.2 33.2 %collective-permute-start.5 = (f32[3,8,4,256]{3,2,1,0:T(4,128)}, f32[3,8,4,256]{3,2,1,0:T(4,128)}, u32[]{:S(2)}, u32[]{:S(2)}) collective-permute-start(f32[3,8,4,256]{3,2,1,0:T(4,128)} %get-tuple-element.17), channel_id=1, source_target_pairs={{0,1},{1,2},{2,3},{3,4},{4,5},{5,6},{6,7},{7,8},{8,9},{9,10},{10,1... | collective-permute-start | bytes 294920 | tf_op jit(solution)/shard_map/ppermute | solution.py:18
  8.2 36.1 %collective-permute-start.4 = (f32[3,4,32,256]{3,2,1,0:T(8,128)S(1)}, f32[3,4,32,256]{3,2,1,0:T(8,128)S(1)}, u32[]{:S(2)}, u32[]{:S(2)}) collective-permute-start(f32[3,4,32,256]{3,2,1,0:T(8,128)S(1)} %get-tuple-element.19), channel_id=1, source_target_pairs={{0,4},{1,5},{2,6},{3,7},{4,8},{5,9},{6,10},{7,11},{8,12},{9,13},{1... | collective-permute-start | bytes 1179656 | tf_op jit(solution)/shard_map/ppermute | solution.py:18
  12.6 31.8 %collective-permute-start.7 = (f32[3,4,32,256]{3,2,1,0:T(8,128)S(1)}, f32[3,4,32,256]{3,2,1,0:T(8,128)S(1)}, u32[]{:S(2)}, u32[]{:S(2)}) collective-permute-start(f32[3,4,32,256]{3,2,1,0:T(8,128)S(1)} %get-tuple-element.20), channel_id=1, source_target_pairs={{4,0},{5,1},{6,2},{7,3},{8,4},{9,5},{10,6},{11,7},{12,8},{13,9},{1... | collective-permute-start | bytes 1179656 | tf_op jit(solution)/shard_map/ppermute | solution.py:18
  15.3 8.8 %collective-permute-start.2 = (f32[1,8,4,256]{3,2,1,0:T(4,128)}, f32[1,8,4,256]{3,2,1,0:T(4,128)}, u32[]{:S(2)}, u32[]{:S(2)}) collective-permute-start(f32[1,8,4,256]{3,2,1,0:T(4,128)} %get-tuple-element.26), channel_id=1, source_target_pairs={{1,0},{2,1},{3,2},{4,3},{5,4},{6,5},{7,6},{8,7},{9,8},{10,9},{11,1... | collective-permute-start | bytes 98312 | tf_op jit(solution)/shard_map/ppermute | solution.py:18
  24.1 6.5 %collective-permute-start.1 = (f32[1,8,4,256]{3,2,1,0:T(4,128)}, f32[1,8,4,256]{3,2,1,0:T(4,128)S(1)}, u32[]{:S(2)}, u32[]{:S(2)}) collective-permute-start(f32[1,8,4,256]{3,2,1,0:T(4,128)} %get-tuple-element.25), channel_id=1, source_target_pairs={{0,1},{1,2},{2,3},{3,4},{4,5},{5,6},{6,7},{7,8},{8,9},{9,10},{10,1... | collective-permute-start | bytes 98312 | tf_op jit(solution)/shard_map/ppermute | solution.py:18
  30.6 8.9 %collective-permute-start = (f32[1,4,32,256]{3,2,1,0:T(8,128)}, f32[1,4,32,256]{3,2,1,0:T(8,128)S(1)}, u32[]{:S(2)}, u32[]{:S(2)}) collective-permute-start(f32[1,4,32,256]{3,2,1,0:T(8,128)} %get-tuple-element.27), channel_id=1, source_target_pairs={{0,4},{1,5},{2,6},{3,7},{4,8},{5,9},{6,10},{7,11},{8,12},{9,13},{1... | collective-permute-start | bytes 393224 | tf_op jit(solution)/shard_map/ppermute | solution.py:18
  36.5 7.8 %collective-permute-start.3 = (f32[1,4,32,256]{3,2,1,0:T(8,128)S(1)}, f32[1,4,32,256]{3,2,1,0:T(8,128)S(1)}, u32[]{:S(2)}, u32[]{:S(2)}) collective-permute-start(f32[1,4,32,256]{3,2,1,0:T(8,128)S(1)} %get-tuple-element.28), channel_id=1, source_target_pairs={{4,0},{5,1},{6,2},{7,3},{8,4},{9,5},{10,6},{11,7},{12,8},{13,9},{1... | collective-permute-start | bytes 393224 | tf_op jit(solution)/shard_map/ppermute | solution.py:18
  44.8 13.7 %copy-start.2 = (f32[1,4,1,8,32,256]{5,4,3,2,1,0:T(8,128)S(1)}, f32[1,4,1,8,32,256]{5,4,3,2,1,0:T(8,128)}, u32[]{:S(2)}) copy-start(f32[1,4,1,8,32,256]{5,4,3,2,1,0:T(8,128)} %param.8) | copy-start | bytes 3145732
  47.4 14.8 %collective-permute-start.11 = (f32[1,4,32,256]{3,2,1,0:T(8,128)S(1)}, f32[1,4,32,256]{3,2,1,0:T(8,128)S(1)}, u32[]{:S(2)}, u32[]{:S(2)}) collective-permute-start(f32[1,4,32,256]{3,2,1,0:T(8,128)S(1)} %get-tuple-element.24), channel_id=1, source_target_pairs={{4,0},{5,1},{6,2},{7,3},{8,4},{9,5},{10,6},{11,7},{12,8},{13,9},{1... | collective-permute-start | bytes 393224 | tf_op jit(solution)/shard_map/ppermute | solution.py:18
  49.3 12.9 %collective-permute-start.8 = (f32[1,4,32,256]{3,2,1,0:T(8,128)S(1)}, f32[1,4,32,256]{3,2,1,0:T(8,128)S(1)}, u32[]{:S(2)}, u32[]{:S(2)}) collective-permute-start(f32[1,4,32,256]{3,2,1,0:T(8,128)S(1)} %get-tuple-element.23), channel_id=1, source_target_pairs={{0,4},{1,5},{2,6},{3,7},{4,8},{5,9},{6,10},{7,11},{8,12},{9,13},{1... | collective-permute-start | bytes 393224 | tf_op jit(solution)/shard_map/ppermute | solution.py:18
  54.2 5.2 %collective-permute-start.10 = (f32[1,8,4,256]{3,2,1,0:T(4,128)S(1)}, f32[1,8,4,256]{3,2,1,0:T(4,128)S(1)}, u32[]{:S(2)}, u32[]{:S(2)}) collective-permute-start(f32[1,8,4,256]{3,2,1,0:T(4,128)S(1)} %get-tuple-element.22), channel_id=1, source_target_pairs={{1,0},{2,1},{3,2},{4,3},{5,4},{6,5},{7,6},{8,7},{9,8},{10,9},{11,1... | collective-permute-start | bytes 98312 | tf_op jit(solution)/shard_map/ppermute | solution.py:18
  56.1 6.1 %collective-permute-start.9 = (f32[1,8,4,256]{3,2,1,0:T(4,128)S(1)}, f32[1,8,4,256]{3,2,1,0:T(4,128)S(1)}, u32[]{:S(2)}, u32[]{:S(2)}) collective-permute-start(f32[1,8,4,256]{3,2,1,0:T(4,128)S(1)} %get-tuple-element.21), channel_id=1, source_target_pairs={{0,1},{1,2},{2,3},{3,4},{4,5},{5,6},{6,7},{7,8},{8,9},{9,10},{10,1... | collective-permute-start | bytes 98312 | tf_op jit(solution)/shard_map/ppermute | solution.py:18

commit v2 on v1

v2 whole, which is shorter than its diff:
```python
import numpy as np
import jax
import jax.numpy as jnp
from jax import lax
from jax.experimental import pallas as pl
from jax.experimental.pallas import tpu as pltpu
from jax.sharding import PartitionSpec as P

STEPS = 2
YBLOCKS = 4
HALO = 4

A0 = -205.0 / 72.0
A = (8.0 / 5.0, -1.0 / 5.0, 8.0 / 315.0, -1.0 / 560.0)
C = (4.0 / 5.0, -1.0 / 5.0, 4.0 / 105.0, -1.0 / 280.0)
A_INT = (8064.0, -1008.0, 128.0, -9.0)
C_INT = (672.0, -168.0, 32.0, -3.0)
A_UNIT = 1.0 / 5040.0
C_UNIT = 1.0 / 840.0
TIME = 0.03
F32 = jnp.float32
BF16 = jnp.bfloat16
VMEM = pltpu.VMEM


def row_pairs(size):
    first, second = [], []
    for i in range(size):
        r = i // YBLOCKS
        partner = i + YBLOCKS if r % 2 == 0 else i - YBLOCKS
        if 0 <= partner < size:
            first.append((i, partner))
        partner = i + YBLOCKS if r % 2 == 1 else i - YBLOCKS
        if 0 <= partner < size:
            second.append((i, partner))
    return first, second


def column_pairs(size):
    first, second = [], []
    for i in range(size):
        c = i % YBLOCKS
        partner = c + 1 if c % 2 == 0 else c - 1
        if 0 <= partner < YBLOCKS:
            first.append((i, i - c + partner))
        partner = c + 1 if c % 2 == 1 else c - 1
        if 0 <= partner < YBLOCKS:
            second.append((i, i - c + partner))
    return first, second


def along_z(depth):
    lap = np.zeros((depth, depth), np.float32)
    slope = np.zeros((depth, depth), np.float32)
    for k in range(1, HALO + 1):
        i = np.arange(depth - k)
        lap[i + k, i] += A_INT[k - 1]
        lap[i, i + k] += A_INT[k - 1]
        slope[i + k, i] += C_INT[k - 1]
        slope[i, i + k] -= C_INT[k - 1]
    return np.concatenate([slope, lap], axis=1)


def along_y(height):
    out = []
    for parity in range(2):
        full = np.zeros((2, height, height + 2 * HALO), np.float32)
        for i in range(height):
            for k in range(1, HALO + 1):
                full[0, i, HALO + i + k] += C_INT[k - 1]
                full[0, i, HALO + i - k] -= C_INT[k - 1]
                full[1, i, HALO + i + k] += A_INT[k - 1]
                full[1, i, HALO + i - k] += A_INT[k - 1]
        full = full.reshape(2 * height, height + 2 * HALO)
        low, own, high = full[:, :HALO], full[:, HALO:-HALO], full[:, -HALO:]
        edge = np.concatenate([high, low] if parity == 0 else [low, high], axis=1)
        out.append(np.concatenate([own, own, edge, edge], axis=1))
    return np.stack(out)


def parts(value):
    lead = value.astype(BF16)
    return lead, (value - lead.astype(F32)).astype(BF16)


def dot(a, b):
    return jnp.dot(a, b, preferred_element_type=F32)


def z_product(block, factor):
    planes, height, depth = block.shape
    lead, trail = parts(block.reshape(planes * height, depth))
    out = dot(lead, factor) + dot(trail, factor)
    return out.reshape(planes, height, out.shape[1])


def y_product(plane, first, second, factor):
    lead, trail = parts(plane)
    edge = jnp.concatenate([first, second], axis=0)
    edge_lead = edge.astype(BF16).astype(F32)
    edges = jnp.concatenate([edge_lead, edge - edge_lead], axis=0).astype(BF16)
    return dot(factor, jnp.concatenate([lead, trail, edges], axis=0))


def x_slope(own):
    out = []
    for i in range(len(own)):
        total = None
        for k in range(1, HALO + 1):
            if i + k < len(own) and i - k >= 0:
                term = C[k - 1] * (own[i + k] - own[i - k])
            elif i + k < len(own):
                term = C[k - 1] * own[i + k]
            elif i - k >= 0:
                term = -C[k - 1] * own[i - k]
            else:
                continue
            total = term if total is None else total + term
        out.append(total)
    return out


def x_laplace(own):
    out = []
    for i in range(len(own)):
        total = 3.0 * A0 * own[i]
        for k in range(1, HALO + 1):
            if i + k < len(own) and i - k >= 0:
                total = total + A[k - 1] * (own[i + k] + own[i - k])
            elif i + k < len(own):
                total = total + A[k - 1] * own[i + k]
            elif i - k >= 0:
                total = total + A[k - 1] * own[i - k]
        out.append(total)
    return out


def edge_terms(i, count, low, high):
    terms = []
    for k in range(1, HALO + 1):
        if i - k < 0:
            terms.append((k, -1.0, low[HALO + i - k]))
        if i + k >= count:
            terms.append((k, 1.0, high[i + k - count]))
    return terms


def edge_slope(i, count, low, high):
    total = None
    for k, sign, value in edge_terms(i, count, low, high):
        term = (sign * C[k - 1]) * value
        total = term if total is None else total + term
    return total


def edge_laplace(i, count, low, high):
    total = None
    for k, _, value in edge_terms(i, count, low, high):
        term = A[k - 1] * value
        total = term if total is None else total + term
    return total


def depth_of_surface(topo_row, height):
    rows = lax.broadcasted_iota(jnp.int32, (height, height), 0)
    lanes = lax.broadcasted_iota(jnp.int32, (height, height), 1)
    picked = jnp.where(rows == lanes, topo_row.astype(F32), 0.0)
    return jnp.sum(picked, axis=1, keepdims=True).astype(jnp.int32)


def row_parity():
    return lax.rem(lax.axis_index("blk") // YBLOCKS, 2)


def column_parity():
    return lax.rem(lax.rem(lax.axis_index("blk"), YBLOCKS), 2)


def copy_all(pairs, sem):
    copies = [pltpu.make_async_copy(a, b, sem.at[n]) for n, (a, b) in enumerate(pairs)]
    for c in copies:
        c.start()
    return copies


def first_kernel(adj, mod, buoy, topo, x1, x2, s0, cur_v, mod_v, sem):
    width, height, depth = s0.shape
    parity = row_parity()
    high_first = (1 - parity) * HALO
    low_first = parity * HALO
    copies = copy_all(
        [
            (adj.at[0, 1, 0], cur_v),
            (mod.at[0], mod_v),
            (buoy.at[0, pl.ds(high_first, HALO)], x1.at[0]),
            (buoy.at[0, pl.ds(low_first, HALO)], x2.at[0]),
        ],
        sem,
    )
    lanes = lax.broadcasted_iota(jnp.int32, (height, depth), 1)
    masks = [lanes >= depth_of_surface(topo[0, i : i + 1, :], height) for i in range(width)]
    copies[0].wait()
    copies[1].wait()
    for i in range(width):
        s0[i] = jnp.where(masks[i], mod_v[i] * cur_v[i], 0.0)
    x1[1] = s0[pl.ds(high_first, HALO)]
    x2[1] = s0[pl.ds(low_first, HALO)]
    copies[2].wait()
    copies[3].wait()


def second_kernel(buoy, fwd, s0, x1, x2, y1, y2, buoy_v, fields_v, sem):
    width, height, depth = s0.shape
    parity = row_parity()
    high_first = (1 - parity) * HALO
    low_first = parity * HALO
    copies = copy_all(
        [
            (buoy.at[0], buoy_v),
            (fwd.at[0, pl.ds(1, 2), 0], fields_v),
            (fwd.at[0, pl.ds(1, 2), 0, pl.ds(high_first, HALO)], x1),
            (fwd.at[0, pl.ds(1, 2), 0, pl.ds(low_first, HALO)], x2),
        ],
        sem,
    )
    even = column_parity() == 0

    def pack(n, value):
        low = value[:, :HALO]
        high = value[:, height - HALO :]
        y1[n] = jnp.where(even, high, low)
        y2[n] = jnp.where(even, low, high)

    pack(1, s0[...])
    copies[0].wait()
    pack(0, buoy_v[...])
    copies[1].wait()
    pack(2, fields_v[0])
    pack(3, fields_v[1])
    copies[2].wait()
    copies[3].wait()


def early_kernel(
    cur, later, mod, buoy, topo, s0, rec, res, y1, y2, zf, yf,
    rest, sx_own, sy, sz, gx_own, gy, gz, weight, scale, source,
    zs, zb, ys, yb,
):
    width, height, depth = s0.shape
    size = lax.axis_index("blk")
    anchor_x = size // YBLOCKS * width
    anchor_y = lax.rem(size, YBLOCKS) * height
    factor_y = yf[column_parity()]
    count = rec.shape[1]
    rx = rec[0:1, :] - anchor_x
    ry = rec[1:2, :] - anchor_y
    ids = lax.broadcasted_iota(jnp.int32, (STEPS * width, count), 0)
    values = jnp.concatenate(
        [jnp.broadcast_to(res[0, s : s + 1, :], (width, count)) for s in range(STEPS)], axis=0
    )
    hit_x = jnp.where(lax.rem(ids, width) == rx, values, 0.0)
    hit_y = (lax.broadcasted_iota(jnp.int32, (height, count), 0) == ry).astype(F32)
    plane = lax.dot_general(
        hit_y,
        hit_x,
        (((1,), (1,)), ((), ())),
        precision=lax.Precision.HIGHEST,
        preferred_element_type=F32,
    )
    zs[...] = z_product(s0[...], zf[...])
    zb[...] = z_product(buoy[0], zf[:, :depth])
    for i in range(width):
        ys[i] = y_product(s0[i], y1[1, i], y2[1, i], factor_y)
        yb[i] = y_product(buoy[0, i], y1[0, i], y2[0, i], factor_y[:height])
    lanes = lax.broadcasted_iota(jnp.int32, (height, depth), 1)
    for i in range(width):
        surface = depth_of_surface(topo[0, i : i + 1, :], height)
        live = lanes >= surface
        at = lanes == surface + 1
        scale[i] = jnp.where(live, TIME, 0.0)
        for s in range(STEPS):
            n = s * width + i
            source[s, i] = jnp.where(at, plane[:, n : n + 1], 0.0)
    for t in range(height // 8):
        rows = pl.ds(8 * t, 8)
        own = [s0[i, rows] for i in range(width)]
        slope = x_slope(own)
        laplace = x_laplace(own)
        for i in range(width):
            sx_own[i, rows] = slope[i]
            edge = ys[i, pl.ds(height + 8 * t, 8)] + zs[i, rows, depth:]
            laplace[i] = laplace[i] + A_UNIT * edge
        own = [buoy[0, i, rows] for i in range(width)]
        slope = x_slope(own)
        for i in range(width):
            w = scale[i, rows]
            gx_own[i, rows] = slope[i] * w
            g_y = (C_UNIT * w) * yb[i, rows]
            g_z = (C_UNIT * w) * zb[i, rows]
            s_y = C_UNIT * ys[i, rows]
            s_z = C_UNIT * zs[i, rows, :depth]
            b = own[i] * w
            weight[i, rows] = b
            gy[i, rows] = g_y
            gz[i, rows] = g_z
            sy[i, rows] = s_y
            sz[i, rows] = s_z
            moved = 2.0 * cur[0, 0, 0, i, rows] - later[0, 0, 0, i, rows] + source[0, i, rows]
            moved = jnp.where(w > 0.0, moved, 0.0)
            rest[i, rows] = moved + b * laplace[i] + g_y * s_y + g_z * s_z


def finish_kernel(
    xa1, xa2, rest, sx_own, gx_own, weight, scale, mod,
    e0, s1, sx, gx, x1, x2, y1, y2,
):
    width, height, depth = e0.shape

    def body(low_ref, high_ref, low_out, high_out):
        for t in range(height // 8):
            rows = pl.ds(8 * t, 8)
            low = [low_ref[1, i, rows] for i in range(HALO)]
            high = [high_ref[1, i, rows] for i in range(HALO)]
            low_b = [low_ref[0, i, rows] for i in range(HALO)]
            high_b = [high_ref[0, i, rows] for i in range(HALO)]
            for i in range(width):
                s_x = sx_own[i, rows] + edge_slope(i, width, low, high)
                g_x = gx_own[i, rows] + scale[i, rows] * edge_slope(i, width, low_b, high_b)
                earlier = (
                    rest[i, rows]
                    + weight[i, rows] * edge_laplace(i, width, low, high)
                    + g_x * s_x
                )
                scaled = mod[0, i, rows] * earlier
                sx[i, rows] = s_x
                gx[i, rows] = g_x
                e0[i, rows] = earlier
                s1[i, rows] = scaled
                if i < HALO:
                    low_out[i, rows] = scaled
                if i >= width - HALO:
                    high_out[i - (width - HALO), rows] = scaled

    @pl.when(row_parity() == 0)
    def _():
        body(xa2, xa1, x2, x1)

    @pl.when(row_parity() == 1)
    def _():
        body(xa1, xa2, x1, x2)

    even = column_parity() == 0
    low = s1[:, :HALO]
    high = s1[:, height - HALO :]
    y1[...] = jnp.where(even, high, low)
    y2[...] = jnp.where(even, low, high)


def middle_kernel(
    cur, e0, s1, sx0, sy0, sz0, gy, gz, weight, scale, source, fwd, xf1, xf2, yf1, yf2, y1, y2, zf, yf,
    rest, sx_own, image, fx, image_mod,
    zs, ys, z1, z2, ya, yb,
):
    width, height, depth = e0.shape
    factor_y = yf[column_parity()]
    zs[...] = z_product(s1[...], zf[...])
    z1[...] = z_product(fwd[0, 1, 0], zf[:, :depth])
    z2[...] = z_product(fwd[0, 2, 0], zf[:, :depth])
    for i in range(width):
        ys[i] = y_product(s1[i], y1[i], y2[i], factor_y)
        ya[i] = y_product(fwd[0, 1, 0, i], yf1[2, i], yf2[2, i], factor_y[:height])
        yb[i] = y_product(fwd[0, 2, 0, i], yf1[3, i], yf2[3, i], factor_y[:height])

    def body(low_ref, high_ref):
        for t in range(height // 8):
            rows = pl.ds(8 * t, 8)
            own = [s1[i, rows] for i in range(width)]
            slope = x_slope(own)
            laplace = x_laplace(own)
            own1 = [fwd[0, 1, 0, i, rows] for i in range(width)]
            own2 = [fwd[0, 2, 0, i, rows] for i in range(width)]
            slope1 = x_slope(own1)
            slope2 = x_slope(own2)
            low1 = [low_ref[0, i, rows] for i in range(HALO)]
            high1 = [high_ref[0, i, rows] for i in range(HALO)]
            low2 = [low_ref[1, i, rows] for i in range(HALO)]
            high2 = [high_ref[1, i, rows] for i in range(HALO)]
            for i in range(width):
                now, before = cur[0, 0, 0, i, rows], e0[i, rows]
                s_y = C_UNIT * ys[i, rows]
                s_z = C_UNIT * zs[i, rows, :depth]
                edge = ys[i, pl.ds(height + 8 * t, 8)] + zs[i, rows, depth:]
                lap = laplace[i] + A_UNIT * edge
                moved = 2.0 * before - now + source[1, i, rows]
                moved = jnp.where(scale[i, rows] > 0.0, moved, 0.0)
                rest[i, rows] = (
                    moved + weight[i, rows] * lap + gy[i, rows] * s_y + gz[i, rows] * s_z
                )
                sx_own[i, rows] = slope[i]
                f1x = slope1[i] + edge_slope(i, width, low1, high1)
                fx[i, rows] = slope2[i] + edge_slope(i, width, low2, high2)
                image[i, rows] = (
                    f1x * sx0[i, rows]
                    + C_UNIT
                    * (
                        ya[i, rows] * sy0[i, rows]
                        + z1[i, rows] * sz0[i, rows]
                        + yb[i, rows] * s_y
                        + z2[i, rows] * s_z
                    )
                )
                f0, f3 = fwd[0, 0, 0, i, rows], fwd[0, 3, 0, i, rows]
                image_mod[0, i, rows] = now * (f0 - 2.0 * own1[i] + own2[i]) + before * (
                    own1[i] - 2.0 * own2[i] + f3
                )

    @pl.when(row_parity() == 0)
    def _():
        body(xf2, xf1)

    @pl.when(row_parity() == 1)
    def _():
        body(xf1, xf2)


def last_kernel(
    xs1, xs2, rest, sx_own, image, fx, gx, weight, e0,
    image_out, states_out,
    image_v, e1_v, sem,
):
    width, height, depth = e0.shape
    first = pltpu.make_async_copy(e0, states_out.at[0, 0, 0], sem.at[0])
    first.start()

    def body(low_ref, high_ref):
        for t in range(height // 8):
            rows = pl.ds(8 * t, 8)
            low = [low_ref[i, rows] for i in range(HALO)]
            high = [high_ref[i, rows] for i in range(HALO)]
            for i in range(width):
                s_x = sx_own[i, rows] + edge_slope(i, width, low, high)
                e1_v[i, rows] = (
                    rest[i, rows]
                    + weight[i, rows] * edge_laplace(i, width, low, high)
                    + gx[i, rows] * s_x
                )
                image_v[i, rows] = image[i, rows] + fx[i, rows] * s_x

    @pl.when(row_parity() == 0)
    def _():
        body(xs2, xs1)

    @pl.when(row_parity() == 1)
    def _():
        body(xs1, xs2)

    second = pltpu.make_async_copy(e1_v, states_out.at[0, 1, 0], sem.at[1])
    third = pltpu.make_async_copy(image_v, image_out.at[0], sem.at[2])
    second.start()
    third.start()
    first.wait()
    second.wait()
    third.wait()


def call(kernel, name, inputs, outputs, scratch=(), us=1.0):
    arrays, in_specs = [], []
    for array, near in inputs:
        if near:
            array = pltpu.with_memory_space_constraint(array, VMEM)
        arrays.append(array)
        in_specs.append(pl.BlockSpec(memory_space=VMEM if near else pl.ANY))
    shapes, out_specs = [], []
    for shape, near in outputs:
        shapes.append(VMEM(shape, F32) if near else jax.ShapeDtypeStruct(shape, F32))
        out_specs.append(pl.BlockSpec(memory_space=VMEM if near else pl.ANY))
    return pl.pallas_call(
        kernel,
        name=name,
        in_specs=in_specs,
        out_specs=out_specs,
        out_shape=shapes,
        scratch_shapes=list(scratch),
        compiler_params=pltpu.CompilerParams(vmem_limit_bytes=16 * 1024 * 1024),
        cost_estimate=pl.CostEstimate(
            flops=0, bytes_accessed=int(us * 3.0e6), transcendentals=0
        ),
    )(*arrays)


def shards(adjoint_in, forward, modulus, buoyancy, topography, receivers, residuals):
    width, height, depth = modulus.shape[1:]
    block = (width, height, depth)
    size = lax.axis_size("blk")
    rows1, rows2 = row_pairs(size)
    cols1, cols2 = column_pairs(size)
    zf = jnp.asarray(along_z(depth), BF16)
    yf = jnp.asarray(along_y(height), BF16)
    dma = pltpu.SemaphoreType.DMA

    def swap(value, pairs):
        return lax.ppermute(value, "blk", pairs)

    ahead = (2, HALO, height, depth)
    xa1, xa2, s0 = call(
        first_kernel,
        "scaled_and_planes",
        [(adjoint_in, False), (modulus, False), (buoyancy, False), (topography, True)],
        [(ahead, True), (ahead, True), (block, True)],
        [VMEM(block, F32), VMEM(block, F32), dma((4,))],
    )
    xa1, xa2 = swap(xa1, rows1), swap(xa2, rows2)
    edge = (4, width, HALO, depth)
    xf1, xf2, ya1, ya2 = call(
        second_kernel,
        "edges",
        [(buoyancy, False), (forward, False), (s0, True)],
        [(ahead, True), (ahead, True), (edge, True), (edge, True)],
        [VMEM(block, F32), VMEM((2,) + block, F32), dma((4,))],
    )
    ya1, ya2 = swap(ya1, cols1), swap(ya2, cols2)
    xf1, xf2 = swap(xf1, rows1), swap(xf2, rows2)
    later = adjoint_in[:, :1]
    current = adjoint_in[:, 1:]
    z_out = (width, height, 2 * depth)
    y_out = (width, 2 * height, depth)
    rest, sx_own, sy, sz, gx_own, gy, gz, weight, scale, source = call(
        early_kernel,
        "step0_own",
        [(current, True), (later, True), (modulus, True), (buoyancy, True), (topography, True), (s0, True),
         (receivers.T, True), (residuals, True), (ya1, True), (ya2, True), (zf, True), (yf, True)],
        [(block, True)] * 9 + [((STEPS,) + block, True)],
        [VMEM(z_out, F32), VMEM(block, F32), VMEM(y_out, F32), VMEM(block, F32)],
        us=4.0,
    )
    half = (HALO, height, depth)
    side = (width, HALO, depth)
    e0, s1, sx, gx, xs1, xs2, ys1, ys2 = call(
        finish_kernel,
        "step0_planes",
        [(xa1, True), (xa2, True), (rest, True), (sx_own, True), (gx_own, True), (weight, True), (scale, True),
         (modulus, True)],
        [(block, True)] * 4 + [(half, True)] * 2 + [(side, True)] * 2,
    )
    xs1, xs2 = swap(xs1, rows1), swap(xs2, rows2)
    ys1, ys2 = swap(ys1, cols1), swap(ys2, cols2)
    rest, sx_own, image, fx, image_mod = call(
        middle_kernel,
        "images_and_step1_own",
        [(current, True), (e0, True), (s1, True), (sx, True), (sy, True), (sz, True), (gy, True), (gz, True),
         (weight, True), (scale, True), (source, True), (forward, True), (xf1, True), (xf2, True), (ya1, True),
         (ya2, True), (ys1, True), (ys2, True), (zf, True), (yf, True)],
        [(block, True)] * 4 + [((1,) + block, True)],
        [VMEM(z_out, F32), VMEM(y_out, F32)] + [VMEM(block, F32)] * 4,
        us=5.0,
    )
    image_buo, states = call(
        last_kernel,
        "step1_planes",
        [(xs1, True), (xs2, True), (rest, True), (sx_own, True), (image, True), (fx, True), (gx, True),
         (weight, True), (e0, True)],
        [((1,) + block, False), ((1, STEPS, 1) + block, False)],
        [VMEM(block, F32), VMEM(block, F32), dma((3,))],
    )
    if lax.axis_size("shot") > 1:
        image_mod, image_buo = lax.psum((image_mod, image_buo), "shot")
    return image_mod, image_buo, states


def solution(mesh):
    placed = (
        P(("grp", "shot"), None, "blk", None, None, None),
        P(("grp", "shot"), None, "blk", None, None, None),
        P(("grp", "blk"), None, None, None),
        P(("grp", "blk"), None, None, None),
        P(("grp", "blk"), None, None),
        P("grp", None),
        P(("grp", "shot"), None, None),
    )
    return jax.shard_map(
        shards,
        mesh=mesh,
        in_specs=placed,
        out_specs=(
            P(("grp", "blk"), None, None, None),
            P(("grp", "blk"), None, None, None),
            P(("grp", "shot"), None, "blk", None, None, None),
        ),
        check_vma=False,
    )
```

time: 67.9 us -> 42.8 us (0.63)
  the two profiles are of different devices: /device:TPU:4 before, /device:TPU:25 now
where the time goes in v2:
time: 42.8 us; the launch traced here: 42.4 us
  starting transfers between devices  24.3 us (57%)
  waiting for transfers between devices  7.3 us (17%)
  local copies, waits for them, and re-layouts  5.11 us (12%)
  Pallas kernels  4.75 us (11%)
  between operations  0.91 us (2%)
    ppermute x10, starting transfers between devices, swap(): return lax.ppermute(value, 'blk', pairs)  24.3 us
    ppermute x10, waiting for transfers between devices, swap(): return lax.ppermute(value, 'blk', pairs)  7.3 us
    unnamed x27, local copies, waits for them, and re-layouts  5.08 us
    pallas_call x6, Pallas kernels, call(): pl.pallas_call(kernel, name=name, in_specs=in_specs, out_specs=out_specs,...  4.75 us
  transfers between devices with their start and end apart: 10, of which 3 were waited for; matrix products, arithmetic and copies ran while one was open for 2% of the time, Pallas kernels for 7%

profile of v2, /device:TPU:25, one launch (start us, length us, event | category | flops | bytes accessed | tf_op | source)
XLA Modules:
  0.0 42.4 jit_solution(9998889693980672092)
XLA Ops:
  0.6 0.0 copy-start
  0.6 0.0 copy-start.1
  0.7 1.0 %copy-done.1 = f32[1,8,32,256]{3,2,1,0:T(8,128)S(1)} copy-done((f32[1,8,32,256]{3,2,1,0:T(8,128)S(1)}, f32[1,8,32,256]{3,2,1,0:T(8,128)}, u32[]{:S(2)}) %copy-start.1) | copy-done | bytes 262168
  1.7 0.0 copy-start.3
  1.7 0.9 %copy-done.3 = f32[1,8,32,256]{3,2,1,0:T(8,128)S(1)} copy-done((f32[1,8,32,256]{3,2,1,0:T(8,128)S(1)}, f32[1,8,32,256]{3,2,1,0:T(8,128)}, u32[]{:S(2)}) %copy-start.3) | copy-done | bytes 262168
  2.6 0.0 copy-start.5
  2.6 1.0 %copy-done.5 = f32[1,2,1,8,32,256]{5,4,3,2,1,0:T(8,128)S(1)} copy-done((f32[1,2,1,8,32,256]{5,4,3,2,1,0:T(8,128)S(1)}, f32[1,2,1,8,32,256]{5,4,3,2,1,0:T(8,128)}, u32[]{:S(2)}) %copy-start.5) | copy-done | bytes 524312
  3.7 0.0 copy-start.11
  3.7 0.7 %copy-done.11 = s32[1,8,32]{2,1,0:T(8,128)S(1)} copy-done((s32[1,8,32]{2,1,0:T(8,128)S(1)}, s32[1,8,32]{2,1,0:T(8,128)}, u32[]{:S(2)}) %copy-start.11) | copy-done | bytes 1048
  4.4 0.6 %scaled_and_planes.1 = (f32[2,4,32,256]{3,2,1,0:T(8,128)S(1)}, f32[2,4,32,256]{3,2,1,0:T(8,128)S(1)}, f32[8,32,256]{2,1,0:T(8,128)S(1)}) custom-call(f32[1,2,1,8,32,256]{5,4,3,2,1,0:T(8,128)S(1)} %copy-done.5, f32[1,8,32,256]{3,2,1,0:T(8,128)S(1)} %copy-done.3, f32[1,8,32,256]{3,2,1,0:T(8,128)S(1)} %copy-done.1, s32[1,8,32]{2,1,0:T(8,128)S(1)} %copy-done.11), custom_call_target="tpu_custom_call" | custom-call | bytes 3000000 | tf_op jit(solution)/shard_map/scaled_and_planes/pallas_call | solution.py:477
  4.9 0.0 copy-done
  5.0 0.0 copy-start.6
  5.0 0.2 edges.1
  5.2 0.7 %collective-permute-start.2 = (f32[4,8,4,256]{3,2,1,0:T(4,128)S(1)}, f32[4,8,4,256]{3,2,1,0:T(4,128)S(1)}, u32[]{:S(2)}, u32[]{:S(2)}) collective-permute-start(f32[4,8,4,256]{3,2,1,0:T(4,128)S(1)} %get-tuple-element.38), channel_id=1, source_target_pairs={{0,1},{1,0},{2,3},{3,2},{4,5},{5,4},{6,7},{7,6},{8,9},{9,8},{10,11... | collective-permute-start | bytes 393224 | tf_op jit(solution)/shard_map/ppermute | solution.py:502
  5.9 1.3 %collective-permute-start = (f32[2,4,32,256]{3,2,1,0:T(8,128)S(1)}, f32[2,4,32,256]{3,2,1,0:T(8,128)S(1)}, u32[]{:S(2)}, u32[]{:S(2)}) collective-permute-start(f32[2,4,32,256]{3,2,1,0:T(8,128)S(1)} %get-tuple-element.35), channel_id=1, source_target_pairs={{0,4},{1,5},{2,6},{3,7},{4,0},{5,1},{6,2},{7,3},{8,12},{9,13},{10,... | collective-permute-start | bytes 786440 | tf_op jit(solution)/shard_map/ppermute | solution.py:502
  7.2 2.0 %collective-permute-start.1 = (f32[2,4,32,256]{3,2,1,0:T(8,128)S(1)}, f32[2,4,32,256]{3,2,1,0:T(8,128)S(1)}, u32[]{:S(2)}, u32[]{:S(2)}) collective-permute-start(f32[2,4,32,256]{3,2,1,0:T(8,128)S(1)} %get-tuple-element.36), channel_id=1, source_target_pairs={{4,8},{5,9},{6,10},{7,11},{8,4},{9,5},{10,6},{11,7},{12,16},{13,17... | collective-permute-start | bytes 786440 | tf_op jit(solution)/shard_map/ppermute | solution.py:502
  9.2 3.6 %collective-permute-start.3 = (f32[4,8,4,256]{3,2,1,0:T(4,128)S(1)}, f32[4,8,4,256]{3,2,1,0:T(4,128)S(1)}, u32[]{:S(2)}, u32[]{:S(2)}) collective-permute-start(f32[4,8,4,256]{3,2,1,0:T(4,128)S(1)} %get-tuple-element.39), channel_id=1, source_target_pairs={{1,2},{2,1},{5,6},{6,5},{9,10},{10,9},{13,14},{14,13},{17,18},{18,... | collective-permute-start | bytes 393224 | tf_op jit(solution)/shard_map/ppermute | solution.py:502
  12.8 0.1 collective-permute-start.4
  12.9 0.0 collective-permute-done.2.y1.yf1
  12.9 0.0 copy-start.2
  12.9 0.0 copy-start.4
  12.9 0.0 copy-start.7
  13.0 0.0 copy-start.8
  13.0 0.0 copy-start.9
  13.0 0.0 copy-start.10
  13.0 4.3 %collective-permute-start.5 = (f32[2,4,32,256]{3,2,1,0:T(8,128)S(1)}, f32[2,4,32,256]{3,2,1,0:T(8,128)S(1)}, u32[]{:S(2)}, u32[]{:S(2)}) collective-permute-start(f32[2,4,32,256]{3,2,1,0:T(8,128)S(1)} %get-tuple-element.54), channel_id=1, source_target_pairs={{4,8},{5,9},{6,10},{7,11},{8,4},{9,5},{10,6},{11,7},{12,16},{13,17... | collective-permute-start | bytes 786440 | tf_op jit(solution)/shard_map/ppermute | solution.py:502
  17.3 0.0 copy-done.6
  17.3 0.0 copy-start.12
  17.4 0.0 collective-permute-done.3.y2.yf2
  17.4 0.0 copy-done.2
  17.4 0.0 copy-done.4
  17.4 0.0 copy-done.7
  17.4 0.0 copy-done.8
  17.4 0.0 copy-done.9
  17.4 0.0 copy-done.10
  17.4 0.6 %copy-done.12 = s32[1,8,32]{2,1,0:T(8,128)S(1)} copy-done((s32[1,8,32]{2,1,0:T(8,128)S(1)}, s32[1,8,32]{2,1,0:T(8,128)}, u32[]{:S(2)}) %copy-start.12) | copy-done | bytes 1048
  18.0 1.4 %step0_own.1 = (f32[8,32,256]{2,1,0:T(8,128)S(1)}, f32[8,32,256]{2,1,0:T(8,128)S(1)}, f32[8,32,256]{2,1,0:T(8,128)S(1)}, f32[8,32,256]{2,1,0:T(8,128)S(1)}, f32[...) custom-call(f32[1,1,1,8,32,256]{5,4,3,2,1,0:T(8,128)S(1)} %get-tuple, ...), custom_call_target="tpu_custom_call" | custom-call | bytes 12000000 | tf_op jit(solution)/shard_map/step0_own/pallas_call | solution.py:477
  19.4 5.6 %collective-permute-done.xa1 = f32[2,4,32,256]{3,2,1,0:T(8,128)S(1)} collective-permute-done((f32[2,4,32,256]{3,2,1,0:T(8,128)S(1)}, f32[2,4,32,256]{3,2,1,0:T(8,128)S(1)}, u32[]{:S(2)}, u32[]{:S(2)}) %collective-permute-start) | collective-permute-done | bytes 262176 | tf_op jit(solution)/shard_map/ppermute | solution.py:502
  25.0 0.0 collective-permute-done.1.xa2
  25.0 0.2 step0_planes.1
  25.3 0.1 collective-permute-start.8
  25.4 3.0 %collective-permute-start.9 = (f32[4,32,256]{2,1,0:T(8,128)S(1)}, f32[4,32,256]{2,1,0:T(8,128)S(1)}, u32[]{:S(2)}, u32[]{:S(2)}) collective-permute-start(f32[4,32,256]{2,1,0:T(8,128)S(1)} %get-tuple-element.59), channel_id=1, source_target_pairs={{4,8},{5,9},{6,10},{7,11},{8,4},{9,5},{10,6},{11,7},{12,16},{13,17... | collective-permute-start | bytes 393224 | tf_op jit(solution)/shard_map/ppermute | solution.py:502
  28.4 2.1 %collective-permute-start.6 = (f32[8,4,256]{2,1,0:T(4,128)S(1)}, f32[8,4,256]{2,1,0:T(4,128)S(1)}, u32[]{:S(2)}, u32[]{:S(2)}) collective-permute-start(f32[8,4,256]{2,1,0:T(4,128)S(1)} %get-tuple-element.55), channel_id=1, source_target_pairs={{0,1},{1,0},{2,3},{3,2},{4,5},{5,4},{6,7},{7,6},{8,9},{9,8},{10,11... | collective-permute-start | bytes 98312 | tf_op jit(solution)/shard_map/ppermute | solution.py:502
  30.5 0.1 collective-permute-done.4.xf1
  30.7 7.1 %collective-permute-start.7 = (f32[8,4,256]{2,1,0:T(4,128)S(1)}, f32[8,4,256]{2,1,0:T(4,128)S(1)}, u32[]{:S(2)}, u32[]{:S(2)}) collective-permute-start(f32[8,4,256]{2,1,0:T(4,128)S(1)} %get-tuple-element.56), channel_id=1, source_target_pairs={{1,2},{2,1},{5,6},{6,5},{9,10},{10,9},{13,14},{14,13},{17,18},{18,... | collective-permute-start | bytes 98312 | tf_op jit(solution)/shard_map/ppermute | solution.py:502
  37.8 0.0 collective-permute-done.5.xf2
  37.8 0.0 collective-permute-done.6.y1
  37.8 1.6 %collective-permute-done.7.y2 = f32[8,4,256]{2,1,0:T(4,128)S(1)} collective-permute-done((f32[8,4,256]{2,1,0:T(4,128)S(1)}, f32[8,4,256]{2,1,0:T(4,128)S(1)}, u32[]{:S(2)}, u32[]{:S(2)}) %collective-permute-start.7) | collective-permute-done | bytes 32800 | tf_op jit(solution)/shard_map/ppermute | solution.py:502
  39.4 1.4 %images_and_step1_own.1 = (f32[8,32,256]{2,1,0:T(8,128)S(1)}, f32[8,32,256]{2,1,0:T(8,128)S(1)}, f32[8,32,256]{2,1,0:T(8,128)S(1)}, f32[8,32,256]{2,1,0:T(8,128)S(1)}, f32[1,8,32,256]{3,2,1,0:T(8,128)S(1)}) custom-call(f32[1,1,1,8,32,256]{5,4,3,2,1,0:T(8,128)S(1)} %get-tuple-element.68.cur, f32[8,32,256]{2,1,0:T(8,128)S(1)} %get-tuple-element.45.e0, ...), custom_call_target="tpu_custom_call" | custom-call | bytes 15000000 | tf_op jit(solution)/shard_map/images_and_step1_own/pallas_call | solution.py:477
  40.7 0.7 %copy.12 = f32[1,8,32,256]{3,2,1,0:T(8,128)} copy(f32[1,8,32,256]{3,2,1,0:T(8,128)S(1)} %get-tuple-element.69) | data formatting | bytes 524288
  41.4 0.0 collective-permute-done.8.xs1
  41.4 0.0 collective-permute-done.9.xs2
  41.4 1.0 %step1_planes.1 = (f32[1,8,32,256]{3,2,1,0:T(8,128)}, f32[1,2,1,8,32,256]{5,4,3,2,1,0:T(8,128)}) custom-call(f32[4,32,256]{2,1,0:T(8,128)S(1)} %collective-permute-done.8.xs1, f32[4,32,256]{2,1,0:T(8,128)S(1)} %collective-permute-done.9.xs2, f32[8,32,256]{2,1,0:T(8,128)S(1)} %get-tuple-element.60.rest, f32[8,32,256]{2,1,0:T(8,128)S(1)} %get-tuple-element.61.sx_own, ...), custom_call_target="tpu_custom_call" | custom-call | bytes 3000000 | tf_op jit(solution)/shard_map/step1_planes/pallas_call | solution.py:477
  (1 shorter events, 0.0 us)
Async XLA Ops:
  0.6 4.3 %copy-start = (f32[1,4,1,8,32,256]{5,4,3,2,1,0:T(8,128)S(1)}, f32[1,4,1,8,32,256]{5,4,3,2,1,0:T(8,128)}, u32[]{:S(2)}) copy-start(f32[1,4,1,8,32,256]{5,4,3,2,1,0:T(8,128)} %fwd.3) | copy-start | bytes 3145732
  0.6 1.0 %copy-start.1 = (f32[1,8,32,256]{3,2,1,0:T(8,128)S(1)}, f32[1,8,32,256]{3,2,1,0:T(8,128)}, u32[]{:S(2)}) copy-start(f32[1,8,32,256]{3,2,1,0:T(8,128)} %buoy.5) | copy-start | bytes 786436
  1.7 0.9 %copy-start.3 = (f32[1,8,32,256]{3,2,1,0:T(8,128)S(1)}, f32[1,8,32,256]{3,2,1,0:T(8,128)}, u32[]{:S(2)}) copy-start(f32[1,8,32,256]{3,2,1,0:T(8,128)} %mod.5) | copy-start | bytes 786436
  2.6 1.0 %copy-start.5 = (f32[1,2,1,8,32,256]{5,4,3,2,1,0:T(8,128)S(1)}, f32[1,2,1,8,32,256]{5,4,3,2,1,0:T(8,128)}, u32[]{:S(2)}) copy-start(f32[1,2,1,8,32,256]{5,4,3,2,1,0:T(8,128)} %adj.1) | copy-start | bytes 1572868
  3.7 0.7 %copy-start.11 = (s32[1,8,32]{2,1,0:T(8,128)S(1)}, s32[1,8,32]{2,1,0:T(8,128)}, u32[]{:S(2)}) copy-start(s32[1,8,32]{2,1,0:T(8,128)} %topo.3) | copy-start | bytes 3076
  5.0 12.3 %copy-start.6 = (f32[1,2,1,8,32,256]{5,4,3,2,1,0:T(8,128)S(1)}, f32[1,2,1,8,32,256]{5,4,3,2,1,0:T(8,128)}, u32[]{:S(2)}) copy-start(f32[1,2,1,8,32,256]{5,4,3,2,1,0:T(8,128)} %adj.1) | copy-start | bytes 1572868
  5.2 7.7 %collective-permute-start.2 = (f32[4,8,4,256]{3,2,1,0:T(4,128)S(1)}, f32[4,8,4,256]{3,2,1,0:T(4,128)S(1)}, u32[]{:S(2)}, u32[]{:S(2)}) collective-permute-start(f32[4,8,4,256]{3,2,1,0:T(4,128)S(1)} %get-tuple-element.38), channel_id=1, source_target_pairs={{0,1},{1,0},{2,3},{3,2},{4,5},{5,4},{6,7},{7,6},{8,9},{9,8},{10,11... | collective-permute-start | bytes 393224 | tf_op jit(solution)/shard_map/ppermute | solution.py:502
  5.9 19.1 %collective-permute-start = (f32[2,4,32,256]{3,2,1,0:T(8,128)S(1)}, f32[2,4,32,256]{3,2,1,0:T(8,128)S(1)}, u32[]{:S(2)}, u32[]{:S(2)}) collective-permute-start(f32[2,4,32,256]{3,2,1,0:T(8,128)S(1)} %get-tuple-element.35), channel_id=1, source_target_pairs={{0,4},{1,5},{2,6},{3,7},{4,0},{5,1},{6,2},{7,3},{8,12},{9,13},{10,... | collective-permute-start | bytes 786440 | tf_op jit(solution)/shard_map/ppermute | solution.py:502
  7.2 17.9 %collective-permute-start.1 = (f32[2,4,32,256]{3,2,1,0:T(8,128)S(1)}, f32[2,4,32,256]{3,2,1,0:T(8,128)S(1)}, u32[]{:S(2)}, u32[]{:S(2)}) collective-permute-start(f32[2,4,32,256]{3,2,1,0:T(8,128)S(1)} %get-tuple-element.36), channel_id=1, source_target_pairs={{4,8},{5,9},{6,10},{7,11},{8,4},{9,5},{10,6},{11,7},{12,16},{13,17... | collective-permute-start | bytes 786440 | tf_op jit(solution)/shard_map/ppermute | solution.py:502
  9.2 8.2 %collective-permute-start.3 = (f32[4,8,4,256]{3,2,1,0:T(4,128)S(1)}, f32[4,8,4,256]{3,2,1,0:T(4,128)S(1)}, u32[]{:S(2)}, u32[]{:S(2)}) collective-permute-start(f32[4,8,4,256]{3,2,1,0:T(4,128)S(1)} %get-tuple-element.39), channel_id=1, source_target_pairs={{1,2},{2,1},{5,6},{6,5},{9,10},{10,9},{13,14},{14,13},{17,18},{18,... | collective-permute-start | bytes 393224 | tf_op jit(solution)/shard_map/ppermute | solution.py:502
  12.8 17.8 %collective-permute-start.4 = (f32[2,4,32,256]{3,2,1,0:T(8,128)S(1)}, f32[2,4,32,256]{3,2,1,0:T(8,128)S(1)}, u32[]{:S(2)}, u32[]{:S(2)}) collective-permute-start(f32[2,4,32,256]{3,2,1,0:T(8,128)S(1)} %get-tuple-element.53), channel_id=1, source_target_pairs={{0,4},{1,5},{2,6},{3,7},{4,0},{5,1},{6,2},{7,3},{8,12},{9,13},{10,... | collective-permute-start | bytes 786440 | tf_op jit(solution)/shard_map/ppermute | solution.py:502
  12.9 4.5 %copy-start.2 = (f32[1,8,32,256]{3,2,1,0:T(8,128)S(1)}, f32[1,8,32,256]{3,2,1,0:T(8,128)}, u32[]{:S(2)}) copy-start(f32[1,8,32,256]{3,2,1,0:T(8,128)} %buoy.5) | copy-start | bytes 786436
  12.9 4.5 %copy-start.4 = (f32[1,8,32,256]{3,2,1,0:T(8,128)S(1)}, f32[1,8,32,256]{3,2,1,0:T(8,128)}, u32[]{:S(2)}) copy-start(f32[1,8,32,256]{3,2,1,0:T(8,128)} %mod.5) | copy-start | bytes 786436
  12.9 4.4 %copy-start.7 = (bf16[256,512]{1,0:T(8,128)(2,1)S(1)}, bf16[256,512]{1,0:T(8,128)(2,1)}, u32[]{:S(2)}) copy-start(bf16[256,512]{1,0:T(8,128)(2,1)} %constant.4.clone.zf) | copy-start | bytes 786436
  13.0 4.4 %copy-start.8 = (bf16[2,64,80]{2,1,0:T(8,128)(2,1)S(1)}, bf16[2,64,80]{2,1,0:T(8,128)(2,1)}, u32[]{:S(2)}) copy-start(bf16[2,64,80]{2,1,0:T(8,128)(2,1)} %constant.5.clone.yf) | copy-start | bytes 61444
  13.0 4.4 %copy-start.9 = (s32[4096,2]{0,1:T(2,128)S(1)}, s32[4096,2]{0,1:T(2,128)}, u32[]{:S(2)}) copy-start(s32[4096,2]{0,1:T(2,128)} %param.14) | copy-start | bytes 98308
  13.0 4.4 %copy-start.10 = (f32[1,2,4096]{2,1,0:T(2,128)S(1)}, f32[1,2,4096]{2,1,0:T(2,128)}, u32[]{:S(2)}) copy-start(f32[1,2,4096]{2,1,0:T(2,128)} %res.1) | copy-start | bytes 98308
  13.0 24.8 %collective-permute-start.5 = (f32[2,4,32,256]{3,2,1,0:T(8,128)S(1)}, f32[2,4,32,256]{3,2,1,0:T(8,128)S(1)}, u32[]{:S(2)}, u32[]{:S(2)}) collective-permute-start(f32[2,4,32,256]{3,2,1,0:T(8,128)S(1)} %get-tuple-element.54), channel_id=1, source_target_pairs={{4,8},{5,9},{6,10},{7,11},{8,4},{9,5},{10,6},{11,7},{12,16},{13,17... | collective-permute-start | bytes 786440 | tf_op jit(solution)/shard_map/ppermute | solution.py:502
  17.3 0.7 %copy-start.12 = (s32[1,8,32]{2,1,0:T(8,128)S(1)}, s32[1,8,32]{2,1,0:T(8,128)}, u32[]{:S(2)}) copy-start(s32[1,8,32]{2,1,0:T(8,128)} %topo.3) | copy-start | bytes 3076
  25.3 16.2 %collective-permute-start.8 = (f32[4,32,256]{2,1,0:T(8,128)S(1)}, f32[4,32,256]{2,1,0:T(8,128)S(1)}, u32[]{:S(2)}, u32[]{:S(2)}) collective-permute-start(f32[4,32,256]{2,1,0:T(8,128)S(1)} %get-tuple-element.58), channel_id=1, source_target_pairs={{0,4},{1,5},{2,6},{3,7},{4,0},{5,1},{6,2},{7,3},{8,12},{9,13},{10,... | collective-permute-start | bytes 393224 | tf_op jit(solution)/shard_map/ppermute | solution.py:502
  25.4 16.1 %collective-permute-start.9 = (f32[4,32,256]{2,1,0:T(8,128)S(1)}, f32[4,32,256]{2,1,0:T(8,128)S(1)}, u32[]{:S(2)}, u32[]{:S(2)}) collective-permute-start(f32[4,32,256]{2,1,0:T(8,128)S(1)} %get-tuple-element.59), channel_id=1, source_target_pairs={{4,8},{5,9},{6,10},{7,11},{8,4},{9,5},{10,6},{11,7},{12,16},{13,17... | collective-permute-start | bytes 393224 | tf_op jit(solution)/shard_map/ppermute | solution.py:502
  28.4 9.4 %collective-permute-start.6 = (f32[8,4,256]{2,1,0:T(4,128)S(1)}, f32[8,4,256]{2,1,0:T(4,128)S(1)}, u32[]{:S(2)}, u32[]{:S(2)}) collective-permute-start(f32[8,4,256]{2,1,0:T(4,128)S(1)} %get-tuple-element.55), channel_id=1, source_target_pairs={{0,1},{1,0},{2,3},{3,2},{4,5},{5,4},{6,7},{7,6},{8,9},{9,8},{10,11... | collective-permute-start | bytes 98312 | tf_op jit(solution)/shard_map/ppermute | solution.py:502
  30.7 8.7 %collective-permute-start.7 = (f32[8,4,256]{2,1,0:T(4,128)S(1)}, f32[8,4,256]{2,1,0:T(4,128)S(1)}, u32[]{:S(2)}, u32[]{:S(2)}) collective-permute-start(f32[8,4,256]{2,1,0:T(4,128)S(1)} %get-tuple-element.56), channel_id=1, source_target_pairs={{1,2},{2,1},{5,6},{6,5},{9,10},{10,9},{13,14},{14,13},{17,18},{18,... | collective-permute-start | bytes 98312 | tf_op jit(solution)/shard_map/ppermute | solution.py:502

commit v3 on v2

--- a/solution.py
+++ b/solution.py
@@ -78,6 +78,11 @@
     return np.stack(out)
 
 
+def edge_rows(factor, height):
+    rows = np.concatenate([np.arange(8), np.arange(height - 8, height)])
+    return factor[:, np.concatenate([rows, height + rows]), 2 * height :]
+
+
 def parts(value):
     lead = value.astype(BF16)
     return lead, (value - lead.astype(F32)).astype(BF16)
@@ -94,12 +99,15 @@
     return out.reshape(planes, height, out.shape[1])
 
 
+def edge_parts(first, second):
+    edge = jnp.concatenate([first, second], axis=0)
+    lead = edge.astype(BF16).astype(F32)
+    return jnp.concatenate([lead, edge - lead], axis=0).astype(BF16)
+
+
 def y_product(plane, first, second, factor):
     lead, trail = parts(plane)
-    edge = jnp.concatenate([first, second], axis=0)
-    edge_lead = edge.astype(BF16).astype(F32)
-    edges = jnp.concatenate([edge_lead, edge - edge_lead], axis=0).astype(BF16)
-    return dot(factor, jnp.concatenate([lead, trail, edges], axis=0))
+    return dot(factor, jnp.concatenate([lead, trail, edge_parts(first, second)], axis=0))
 
 
 def x_slope(own):
@@ -183,46 +191,38 @@
     return copies
 
 
-def first_kernel(adj, mod, buoy, topo, x1, x2, s0, cur_v, mod_v, sem):
+def first_kernel(
+    adj, mod, buoy, topo_in, fwd,
+    x1, x2, f1, f2, y1, y2, s0,
+    cur_v, mod_v, topo, buoy_v, fields_v, sem,
+):
     width, height, depth = s0.shape
     parity = row_parity()
-    high_first = (1 - parity) * HALO
-    low_first = parity * HALO
+    first = pl.ds((1 - parity) * HALO, HALO)
+    second = pl.ds(parity * HALO, HALO)
     copies = copy_all(
         [
+            (topo_in, topo),
             (adj.at[0, 1, 0], cur_v),
             (mod.at[0], mod_v),
-            (buoy.at[0, pl.ds(high_first, HALO)], x1.at[0]),
-            (buoy.at[0, pl.ds(low_first, HALO)], x2.at[0]),
+            (buoy.at[0], buoy_v),
+            (fwd.at[0, pl.ds(1, 2), 0], fields_v),
+            (buoy.at[0, first], x1.at[0]),
+            (buoy.at[0, second], x2.at[0]),
+            (fwd.at[0, pl.ds(1, 2), 0, first], f1),
+            (fwd.at[0, pl.ds(1, 2), 0, second], f2),
         ],
         sem,
     )
     lanes = lax.broadcasted_iota(jnp.int32, (height, depth), 1)
+    copies[0].wait()
     masks = [lanes >= depth_of_surface(topo[0, i : i + 1, :], height) for i in range(width)]
-    copies[0].wait()
     copies[1].wait()
+    copies[2].wait()
     for i in range(width):
         s0[i] = jnp.where(masks[i], mod_v[i] * cur_v[i], 0.0)
-    x1[1] = s0[pl.ds(high_first, HALO)]
-    x2[1] = s0[pl.ds(low_first, HALO)]
-    copies[2].wait()
-    copies[3].wait()
-
-
-def second_kernel(buoy, fwd, s0, x1, x2, y1, y2, buoy_v, fields_v, sem):
-    width, height, depth = s0.shape
-    parity = row_parity()
-    high_first = (1 - parity) * HALO
-    low_first = parity * HALO
-    copies = copy_all(
-        [
-            (buoy.at[0], buoy_v),
-            (fwd.at[0, pl.ds(1, 2), 0], fields_v),
-            (fwd.at[0, pl.ds(1, 2), 0, pl.ds(high_first, HALO)], x1),
-            (fwd.at[0, pl.ds(1, 2), 0, pl.ds(low_first, HALO)], x2),
-        ],
-        sem,
-    )
+    x1[1] = s0[first]
+    x2[1] = s0[second]
     even = column_parity() == 0
 
     def pack(n, value):
@@ -231,18 +231,18 @@
         y1[n] = jnp.where(even, high, low)
         y2[n] = jnp.where(even, low, high)
 
-    pack(1, s0[...])
-    copies[0].wait()
-    pack(0, buoy_v[...])
-    copies[1].wait()
-    pack(2, fields_v[0])
-    pack(3, fields_v[1])
-    copies[2].wait()
+    pack(1, s0)
     copies[3].wait()
+    pack(0, buoy_v)
+    copies[4].wait()
+    pack(2, fields_v.at[0])
+    pack(3, fields_v.at[1])
+    for c in copies[5:]:
+        c.wait()
 
 
 def early_kernel(
-    cur, later, mod, buoy, topo, s0, rec, res, y1, y2, zf, yf,
+    adj, buoy, topo, s0, rec, res, y1, y2, zf, yf,
     rest, sx_own, sy, sz, gx_own, gy, gz, weight, scale, source,
     zs, zb, ys, yb,
 ):
@@ -305,14 +305,14 @@
             gz[i, rows] = g_z
             sy[i, rows] = s_y
             sz[i, rows] = s_z
-            moved = 2.0 * cur[0, 0, 0, i, rows] - later[0, 0, 0, i, rows] + source[0, i, rows]
+            moved = 2.0 * adj[0, 1, 0, i, rows] - adj[0, 0, 0, i, rows] + source[0, i, rows]
             moved = jnp.where(w > 0.0, moved, 0.0)
             rest[i, rows] = moved + b * laplace[i] + g_y * s_y + g_z * s_z
 
 
 def finish_kernel(
     xa1, xa2, rest, sx_own, gx_own, weight, scale, mod,
-    e0, s1, sx, gx, x1, x2, y1, y2,
+    e0, s1, sx, gx, x1, x2, y2,
 ):
     width, height, depth = e0.shape
 
@@ -350,26 +350,33 @@
         body(xa1, xa2, x1, x2)
 
     even = column_parity() == 0
-    low = s1[:, :HALO]
-    high = s1[:, height - HALO :]
-    y1[...] = jnp.where(even, high, low)
-    y2[...] = jnp.where(even, low, high)
+    y2[...] = jnp.where(even, s1[:, :HALO], s1[:, height - HALO :])
 
 
 def middle_kernel(
-    cur, e0, s1, sx0, sy0, sz0, gy, gz, weight, scale, source, fwd, xf1, xf2, yf1, yf2, y1, y2, zf, yf,
-    rest, sx_own, image, fx, image_mod,
-    zs, ys, z1, z2, ya, yb,
+    adj, e0, s1, sx0, sy0, sz0, gy, gz, weight, scale, source, fwd, xf1, xf2, yf1, yf2, zf, yf, ys2,
+    rest, sx_own, image, fx, fy, y1, image_mod, states,
+    zs, ys, z1, z2, ya, image_v, sem,
 ):
     width, height, depth = e0.shape
+    first = pltpu.make_async_copy(e0, states.at[0, 0, 0], sem.at[0])
+    first.start()
+    even = column_parity() == 0
+    y1[...] = jnp.where(even, s1[:, height - HALO :], s1[:, :HALO])
+    for i in range(width):
+        f0, f1, f2, f3 = (fwd[0, n, 0, i] for n in range(4))
+        image_v[i] = adj[0, 1, 0, i] * (f0 - 2.0 * f1 + f2) + e0[i] * (f1 - 2.0 * f2 + f3)
+    second = pltpu.make_async_copy(image_v, image_mod.at[0], sem.at[1])
+    second.start()
     factor_y = yf[column_parity()]
+    factor_own = factor_y[:, : 2 * height]
     zs[...] = z_product(s1[...], zf[...])
     z1[...] = z_product(fwd[0, 1, 0], zf[:, :depth])
     z2[...] = z_product(fwd[0, 2, 0], zf[:, :depth])
     for i in range(width):
-        ys[i] = y_product(s1[i], y1[i], y2[i], factor_y)
+        ys[i] = dot(factor_own, jnp.concatenate(parts(s1[i]), axis=0))
         ya[i] = y_product(fwd[0, 1, 0, i], yf1[2, i], yf2[2, i], factor_y[:height])
-        yb[i] = y_product(fwd[0, 2, 0, i], yf1[3, i], yf2[3, i], factor_y[:height])
+        fy[i] = y_product(fwd[0, 2, 0, i], yf1[3, i], yf2[3, i], factor_y[:height])
 
     def body(low_ref, high_ref):
         for t in range(height // 8):
@@ -386,7 +393,7 @@
             low2 = [low_ref[1, i, rows] for i in range(HALO)]
             high2 = [high_ref[1, i, rows] for i in range(HALO)]
             for i in range(width):
-                now, before = cur[0, 0, 0, i, rows], e0[i, rows]
+                now, before = adj[0, 1, 0, i, rows], e0[i, rows]
                 s_y = C_UNIT * ys[i, rows]
                 s_z = C_UNIT * zs[i, rows, :depth]
                 edge = ys[i, pl.ds(height + 8 * t, 8)] + zs[i, rows, depth:]
@@ -405,14 +412,10 @@
                     * (
                         ya[i, rows] * sy0[i, rows]
                         + z1[i, rows] * sz0[i, rows]
-                        + yb[i, rows] * s_y
+                        + fy[i, rows] * s_y
                         + z2[i, rows] * s_z
                     )
                 )
-                f0, f3 = fwd[0, 0, 0, i, rows], fwd[0, 3, 0, i, rows]
-                image_mod[0, i, rows] = now * (f0 - 2.0 * own1[i] + own2[i]) + before * (
-                    own1[i] - 2.0 * own2[i] + f3
-                )
 
     @pl.when(row_parity() == 0)
     def _():
@@ -422,29 +425,48 @@
     def _():
         body(xf1, xf2)
 
+    first.wait()
+    second.wait()
+
 
 def last_kernel(
-    xs1, xs2, rest, sx_own, image, fx, gx, weight, e0,
+    xs1, xs2, ys1, ys2, rest, sx_own, image, fx, fy, gx, gy, weight, ye, states_in,
     image_out, states_out,
     image_v, e1_v, sem,
 ):
-    width, height, depth = e0.shape
-    first = pltpu.make_async_copy(e0, states_out.at[0, 0, 0], sem.at[0])
-    first.start()
+    width, height, depth = rest.shape
+    tiles = height // 8
+    factor = ye[column_parity()]
+
+    def leave(t):
+        rows = pl.ds(8 * t, 8)
+        return (
+            pltpu.make_async_copy(e1_v.at[:, rows], states_out.at[0, 1, 0, :, rows], sem.at[t]),
+            pltpu.make_async_copy(image_v.at[:, rows], image_out.at[0, :, rows], sem.at[tiles + t]),
+        )
+
+    edges = [dot(factor, edge_parts(ys1[i], ys2[i])) for i in range(width)]
 
     def body(low_ref, high_ref):
-        for t in range(height // 8):
+        for t in range(tiles):
             rows = pl.ds(8 * t, 8)
             low = [low_ref[i, rows] for i in range(HALO)]
             high = [high_ref[i, rows] for i in range(HALO)]
             for i in range(width):
                 s_x = sx_own[i, rows] + edge_slope(i, width, low, high)
-                e1_v[i, rows] = (
-                    rest[i, rows]
-                    + weight[i, rows] * edge_laplace(i, width, low, high)
-                    + gx[i, rows] * s_x
-                )
-                image_v[i, rows] = image[i, rows] + fx[i, rows] * s_x
+                lap = edge_laplace(i, width, low, high)
+                add = gx[i, rows] * s_x
+                shown = fx[i, rows] * s_x
+                if t == 0 or t == tiles - 1:
+                    n = 0 if t == 0 else 8
+                    s_y = C_UNIT * edges[i][n : n + 8]
+                    lap = lap + A_UNIT * edges[i][16 + n : 24 + n]
+                    add = add + gy[i, rows] * s_y
+                    shown = shown + C_UNIT * (fy[i, rows] * s_y)
+                e1_v[i, rows] = rest[i, rows] + weight[i, rows] * lap + add
+                image_v[i, rows] = image[i, rows] + shown
+            for c in leave(t):
+                c.start()
 
     @pl.when(row_parity() == 0)
     def _():
@@ -454,26 +476,22 @@
     def _():
         body(xs1, xs2)
 
-    second = pltpu.make_async_copy(e1_v, states_out.at[0, 1, 0], sem.at[1])
-    third = pltpu.make_async_copy(image_v, image_out.at[0], sem.at[2])
-    second.start()
-    third.start()
-    first.wait()
-    second.wait()
-    third.wait()
-
-
-def call(kernel, name, inputs, outputs, scratch=(), us=1.0):
+    for t in range(tiles):
+        for c in leave(t):
+            c.wait()
+
+
+def call(kernel, name, inputs, outputs, scratch=(), us=1.0, aliases=None):
     arrays, in_specs = [], []
     for array, near in inputs:
-        if near:
-            array = pltpu.with_memory_space_constraint(array, VMEM)
-        arrays.append(array)
-        in_specs.append(pl.BlockSpec(memory_space=VMEM if near else pl.ANY))
+        place = VMEM if near else pltpu.HBM
+        arrays.append(pltpu.with_memory_space_constraint(array, place))
+        in_specs.append(pl.BlockSpec(memory_space=place))
     shapes, out_specs = [], []
     for shape, near in outputs:
-        shapes.append(VMEM(shape, F32) if near else jax.ShapeDtypeStruct(shape, F32))
-        out_specs.append(pl.BlockSpec(memory_space=VMEM if near else pl.ANY))
+        place = VMEM if near else pltpu.HBM
+        shapes.append(place(shape, F32))
+        out_specs.append(pl.BlockSpec(memory_space=place))
     return pl.pallas_call(
         kernel,
         name=name,
@@ -481,6 +499,7 @@
         out_specs=out_specs,
         out_shape=shapes,
         scratch_shapes=list(scratch),
+        input_output_aliases=aliases or {},
         compiler_params=pltpu.CompilerParams(vmem_limit_bytes=16 * 1024 * 1024),
         cost_estimate=pl.CostEstimate(
             flops=0, bytes_accessed=int(us * 3.0e6), transcendentals=0
@@ -496,38 +515,31 @@
     cols1, cols2 = column_pairs(size)
     zf = jnp.asarray(along_z(depth), BF16)
     yf = jnp.asarray(along_y(height), BF16)
+    ye = jnp.asarray(edge_rows(along_y(height), height), BF16)
     dma = pltpu.SemaphoreType.DMA
 
     def swap(value, pairs):
         return lax.ppermute(value, "blk", pairs)
 
     ahead = (2, HALO, height, depth)
-    xa1, xa2, s0 = call(
+    edge = (4, width, HALO, depth)
+    xa1, xa2, xf1, xf2, ya1, ya2, s0 = call(
         first_kernel,
-        "scaled_and_planes",
-        [(adjoint_in, False), (modulus, False), (buoyancy, False), (topography, True)],
-        [(ahead, True), (ahead, True), (block, True)],
-        [VMEM(block, F32), VMEM(block, F32), dma((4,))],
+        "scaled_and_edges",
+        [(adjoint_in, False), (modulus, False), (buoyancy, False), (topography, False), (forward, False)],
+        [(ahead, True)] * 4 + [(edge, True)] * 2 + [(block, True)],
+        [VMEM(block, F32), VMEM(block, F32), VMEM(topography.shape, jnp.int32), VMEM(block, F32),
+         VMEM((2,) + block, F32), dma((9,))],
     )
     xa1, xa2 = swap(xa1, rows1), swap(xa2, rows2)
-    edge = (4, width, HALO, depth)
-    xf1, xf2, ya1, ya2 = call(
-        second_kernel,
-        "edges",
-        [(buoyancy, False), (forward, False), (s0, True)],
-        [(ahead, True), (ahead, True), (edge, True), (edge, True)],
-        [VMEM(block, F32), VMEM((2,) + block, F32), dma((4,))],
-    )
     ya1, ya2 = swap(ya1, cols1), swap(ya2, cols2)
     xf1, xf2 = swap(xf1, rows1), swap(xf2, rows2)
-    later = adjoint_in[:, :1]
-    current = adjoint_in[:, 1:]
     z_out = (width, height, 2 * depth)
     y_out = (width, 2 * height, depth)
     rest, sx_own, sy, sz, gx_own, gy, gz, weight, scale, source = call(
         early_kernel,
         "step0_own",
-        [(current, True), (later, True), (modulus, True), (buoyancy, True), (topography, True), (s0, True),
+        [(adjoint_in, True), (buoyancy, True), (topography, True), (s0, True),
          (receivers.T, True), (residuals, True), (ya1, True), (ya2, True), (zf, True), (yf, True)],
         [(block, True)] * 9 + [((STEPS,) + block, True)],
         [VMEM(z_out, F32), VMEM(block, F32), VMEM(y_out, F32), VMEM(block, F32)],
@@ -535,32 +547,33 @@
     )
     half = (HALO, height, depth)
     side = (width, HALO, depth)
-    e0, s1, sx, gx, xs1, xs2, ys1, ys2 = call(
+    e0, s1, sx, gx, xs1, xs2, ys2 = call(
         finish_kernel,
         "step0_planes",
         [(xa1, True), (xa2, True), (rest, True), (sx_own, True), (gx_own, True), (weight, True), (scale, True),
          (modulus, True)],
-        [(block, True)] * 4 + [(half, True)] * 2 + [(side, True)] * 2,
-    )
-    xs1, xs2 = swap(xs1, rows1), swap(xs2, rows2)
-    ys1, ys2 = swap(ys1, cols1), swap(ys2, cols2)
-    rest, sx_own, image, fx, image_mod = call(
+        [(block, True)] * 4 + [(half, True)] * 2 + [(side, True)],
+    )
+    xs1, xs2, ys2 = swap(xs1, rows1), swap(xs2, rows2), swap(ys2, cols2)
+    rest, sx_own, image, fx, fy, ys1, image_mod, states = call(
         middle_kernel,
         "images_and_step1_own",
-        [(current, True), (e0, True), (s1, True), (sx, True), (sy, True), (sz, True), (gy, True), (gz, True),
+        [(adjoint_in, True), (e0, True), (s1, True), (sx, True), (sy, True), (sz, True), (gy, True), (gz, True),
          (weight, True), (scale, True), (source, True), (forward, True), (xf1, True), (xf2, True), (ya1, True),
-         (ya2, True), (ys1, True), (ys2, True), (zf, True), (yf, True)],
-        [(block, True)] * 4 + [((1,) + block, True)],
-        [VMEM(z_out, F32), VMEM(y_out, F32)] + [VMEM(block, F32)] * 4,
+         (ya2, True), (zf, True), (yf, True), (ys2, True)],
+        [(block, True)] * 5 + [(side, True), ((1,) + block, False), ((1, STEPS, 1) + block, False)],
+        [VMEM(z_out, F32), VMEM(y_out, F32)] + [VMEM(block, F32)] * 4 + [dma((2,))],
         us=5.0,
     )
+    ys1 = swap(ys1, cols1)
     image_buo, states = call(
         last_kernel,
         "step1_planes",
-        [(xs1, True), (xs2, True), (rest, True), (sx_own, True), (image, True), (fx, True), (gx, True),
-         (weight, True), (e0, True)],
+        [(xs1, True), (xs2, True), (ys1, True), (ys2, True), (rest, True), (sx_own, True), (image, True), (fx, True),
+         (fy, True), (gx, True), (gy, True), (weight, True), (ye, True), (states, False)],
         [((1,) + block, False), ((1, STEPS, 1) + block, False)],
-        [VMEM(block, F32), VMEM(block, F32), dma((3,))],
+        [VMEM(block, F32), VMEM(block, F32), dma((2 * (height // 8),))],
+        aliases={13: 1},
     )
     if lax.axis_size("shot") > 1:
         image_mod, image_buo = lax.psum((image_mod, image_buo), "shot")

time: 42.8 us -> 37.7 us (0.88)
  the two profiles are of different devices: /device:TPU:25 before, /device:TPU:5 now
where the time goes in v3:
time: 37.7 us; the launch traced here: 37.4 us
  starting transfers between devices  23.1 us (61%)
  waiting for transfers between devices  7.64 us (20%)
  Pallas kernels  5.73 us (15%)
  between operations  0.86 us (2%)
    ppermute x10, starting transfers between devices, swap(): return lax.ppermute(value, 'blk', pairs)  23.1 us
    ppermute x10, waiting for transfers between devices, swap(): return lax.ppermute(value, 'blk', pairs)  7.64 us
    pallas_call x5, Pallas kernels, call(): pl.pallas_call(kernel, name=name, in_specs=in_specs, out_specs=out_specs,...  5.73 us
  transfers between devices with their start and end apart: 10, of which 4 were waited for; matrix products, arithmetic and copies ran while one was open for 0% of the time, Pallas kernels for 8%

profile of v3, /device:TPU:5, one launch (start us, length us, event | category | flops | bytes accessed | tf_op | source)
XLA Modules:
  0.0 37.4 jit_solution(12609966338170172105)
XLA Ops:
  0.6 0.0 copy-start.2
  0.6 0.0 copy-start
  0.7 0.0 copy-start.3
  0.7 0.0 copy-start.5
  0.7 0.0 copy-start.6
  0.7 0.0 copy-start.7
  0.7 1.7 %scaled_and_edges.1 = (f32[2,4,32,256]{3,2,1,0:T(8,128)S(1)}, f32[2,4,32,256]{3,2,1,0:T(8,128)S(1)}, f32[2,4,32,256]{3,2,1,0:T(8,128)S(1)}, f32[2,4,32,256]{3,2,...) custom-call(f32[1,2,1,8,32,256]{5,4,3,2,1,0:T(8,128)} %adj.5, ...), custom_call_target="tpu_custom_call" | custom-call | bytes 3000000 | tf_op jit(solution)/shard_map/scaled_and_edges/pallas_call | solution.py:495
  2.4 0.7 %collective-permute-start.2 = (f32[4,8,4,256]{3,2,1,0:T(4,128)S(1)}, f32[4,8,4,256]{3,2,1,0:T(4,128)S(1)}, u32[]{:S(2)}, u32[]{:S(2)}) collective-permute-start(f32[4,8,4,256]{3,2,1,0:T(4,128)S(1)} %get-tuple-element.40), channel_id=1, source_target_pairs={{0,1},{1,0},{2,3},{3,2},{4,5},{5,4},{6,7},{7,6},{8,9},{9,8},{10,11... | collective-permute-start | bytes 393224 | tf_op jit(solution)/shard_map/ppermute | solution.py:522
  3.1 0.0 collective-permute-start
  3.1 4.4 %collective-permute-start.1 = (f32[2,4,32,256]{3,2,1,0:T(8,128)S(1)}, f32[2,4,32,256]{3,2,1,0:T(8,128)S(1)}, u32[]{:S(2)}, u32[]{:S(2)}) collective-permute-start(f32[2,4,32,256]{3,2,1,0:T(8,128)S(1)} %get-tuple-element.38), channel_id=1, source_target_pairs={{4,8},{5,9},{6,10},{7,11},{8,4},{9,5},{10,6},{11,7},{12,16},{13,17... | collective-permute-start | bytes 786440 | tf_op jit(solution)/shard_map/ppermute | solution.py:522
  7.5 0.0 copy-start.9
  7.5 0.1 collective-permute-start.4
  7.6 4.4 %collective-permute-start.5 = (f32[2,4,32,256]{3,2,1,0:T(8,128)S(1)}, f32[2,4,32,256]{3,2,1,0:T(8,128)S(1)}, u32[]{:S(2)}, u32[]{:S(2)}) collective-permute-start(f32[2,4,32,256]{3,2,1,0:T(8,128)S(1)} %get-tuple-element.56), channel_id=1, source_target_pairs={{4,8},{5,9},{6,10},{7,11},{8,4},{9,5},{10,6},{11,7},{12,16},{13,17... | collective-permute-start | bytes 786440 | tf_op jit(solution)/shard_map/ppermute | solution.py:522
  12.0 0.0 collective-permute-done.2.y1.yf1
  12.0 4.2 %collective-permute-start.3 = (f32[4,8,4,256]{3,2,1,0:T(4,128)S(1)}, f32[4,8,4,256]{3,2,1,0:T(4,128)S(1)}, u32[]{:S(2)}, u32[]{:S(2)}) collective-permute-start(f32[4,8,4,256]{3,2,1,0:T(4,128)S(1)} %get-tuple-element.41), channel_id=1, source_target_pairs={{1,2},{2,1},{5,6},{6,5},{9,10},{10,9},{13,14},{14,13},{17,18},{18,... | collective-permute-start | bytes 393224 | tf_op jit(solution)/shard_map/ppermute | solution.py:522
  16.2 2.9 %collective-permute-done.3.y2.yf2 = f32[4,8,4,256]{3,2,1,0:T(4,128)S(1)} collective-permute-done((f32[4,8,4,256]{3,2,1,0:T(4,128)S(1)}, f32[4,8,4,256]{3,2,1,0:T(4,128)S(1)}, u32[]{:S(2)}, u32[]{:S(2)}) %collective-permute-start.3) | collective-permute-done | bytes 131104 | tf_op jit(solution)/shard_map/ppermute | solution.py:522
  19.1 0.0 copy-done.2
  19.1 0.0 copy-done
  19.1 0.0 copy-done.3
  19.1 0.0 copy-done.5
  19.1 0.0 copy-done.6
  19.2 0.0 copy-done.7
  19.2 0.0 copy-done.9
  19.2 0.0 copy-start.4
  19.2 1.4 %step0_own.1 = (f32[8,32,256]{2,1,0:T(8,128)S(1)}, f32[8,32,256]{2,1,0:T(8,128)S(1)}, f32[8,32,256]{2,1,0:T(8,128)S(1)}, f32[8,32,256]{2,1,0:T(8,128)S(1)}, f32[...) custom-call(f32[1,2,1,8,32,256]{5,4,3,2,1,0:T(8,128)S(1)} %copy-done, ...), custom_call_target="tpu_custom_call" | custom-call | bytes 12000000 | tf_op jit(solution)/shard_map/step0_own/pallas_call | solution.py:495
  20.6 1.6 %collective-permute-done.xa1 = f32[2,4,32,256]{3,2,1,0:T(8,128)S(1)} collective-permute-done((f32[2,4,32,256]{3,2,1,0:T(8,128)S(1)}, f32[2,4,32,256]{3,2,1,0:T(8,128)S(1)}, u32[]{:S(2)}, u32[]{:S(2)}) %collective-permute-start) | collective-permute-done | bytes 262176 | tf_op jit(solution)/shard_map/ppermute | solution.py:522
  22.2 0.0 collective-permute-done.1.xa2
  22.2 0.0 copy-done.4
  22.2 0.0 copy-start.1
  22.3 0.3 step0_planes.1
  22.5 0.1 collective-permute-start.7
  22.6 4.4 %collective-permute-start.8 = (f32[4,32,256]{2,1,0:T(8,128)S(1)}, f32[4,32,256]{2,1,0:T(8,128)S(1)}, u32[]{:S(2)}, u32[]{:S(2)}) collective-permute-start(f32[4,32,256]{2,1,0:T(8,128)S(1)} %get-tuple-element.60), channel_id=1, source_target_pairs={{4,8},{5,9},{6,10},{7,11},{8,4},{9,5},{10,6},{11,7},{12,16},{13,17... | collective-permute-start | bytes 393224 | tf_op jit(solution)/shard_map/ppermute | solution.py:522
  27.0 4.9 %collective-permute-start.6 = (f32[8,4,256]{2,1,0:T(4,128)S(1)}, f32[8,4,256]{2,1,0:T(4,128)S(1)}, u32[]{:S(2)}, u32[]{:S(2)}) collective-permute-start(f32[8,4,256]{2,1,0:T(4,128)S(1)} %get-tuple-element.57), channel_id=1, source_target_pairs={{1,2},{2,1},{5,6},{6,5},{9,10},{10,9},{13,14},{14,13},{17,18},{18,... | collective-permute-start | bytes 98312 | tf_op jit(solution)/shard_map/ppermute | solution.py:522
  31.8 0.0 collective-permute-done.4.xf1
  31.9 0.0 collective-permute-done.5.xf2
  31.9 1.9 %collective-permute-done.6.ys2 = f32[8,4,256]{2,1,0:T(4,128)S(1)} collective-permute-done((f32[8,4,256]{2,1,0:T(4,128)S(1)}, f32[8,4,256]{2,1,0:T(4,128)S(1)}, u32[]{:S(2)}, u32[]{:S(2)}) %collective-permute-start.6) | collective-permute-done | bytes 32800 | tf_op jit(solution)/shard_map/ppermute | solution.py:522
  33.7 0.0 copy-done.1
  33.7 0.0 copy-start.8
  33.7 1.3 %images_and_step1_own.1 = (f32[8,32,256]{2,1,0:T(8,128)S(1)}, f32[8,32,256]{2,1,0:T(8,128)S(1)}, f32[8,32,256]{2,1,0:T(8,128)S(1)}, f32[8,32,256]{2,1,0:T(8,128)...) custom-call(f32[1,2,1,8,32,256]{5,4,3,2,1,0:T(8,128)S(1)} %copy-done, ...), custom_call_target="tpu_custom_call" | custom-call | bytes 15000000 | tf_op jit(solution)/shard_map/images_and_step1_own/pallas_call | solution.py:495
  35.1 0.1 collective-permute-start.9
  35.1 1.2 %collective-permute-done.9.ys1 = f32[8,4,256]{2,1,0:T(4,128)S(1)} collective-permute-done((f32[8,4,256]{2,1,0:T(4,128)S(1)}, f32[8,4,256]{2,1,0:T(4,128)S(1)}, u32[]{:S(2)}, u32[]{:S(2)}) %collective-permute-start.9) | collective-permute-done | bytes 32800 | tf_op jit(solution)/shard_map/ppermute | solution.py:522
  36.3 0.0 collective-permute-done.7.xs1
  36.3 0.0 collective-permute-done.8.xs2
  36.3 0.0 copy-done.8
  36.3 1.1 %step1_planes.1 = (f32[1,8,32,256]{3,2,1,0:T(8,128)}, f32[1,2,1,8,32,256]{5,4,3,2,1,0:T(8,128)}) custom-call(f32[4,32,256]{2,1,0:T(8,128)S(1)} %collective-permute-done.7.xs1, f32[4,32,256]{2,1,0:T(8,128)S(1)} %collective-permute-done.8.xs2, f32[8,4,256]{2,1,0:T(4,128)S(1)} %collective-permute-done.9.ys1, ...), custom_call_target="tpu_custom_call", output_to_operand_aliasing={{1}: (13, {})} | custom-call | bytes 3000000 | tf_op jit(solution)/shard_map/step1_planes/pallas_call | solution.py:495
Async XLA Ops:
  0.6 18.5 %copy-start.2 = (bf16[256,512]{1,0:T(8,128)(2,1)S(1)}, bf16[256,512]{1,0:T(8,128)(2,1)}, u32[]{:S(2)}) copy-start(bf16[256,512]{1,0:T(8,128)(2,1)} %constant.6.clone.zf) | copy-start | bytes 786436
  0.6 18.5 %copy-start = (f32[1,2,1,8,32,256]{5,4,3,2,1,0:T(8,128)S(1)}, f32[1,2,1,8,32,256]{5,4,3,2,1,0:T(8,128)}, u32[]{:S(2)}) copy-start(f32[1,2,1,8,32,256]{5,4,3,2,1,0:T(8,128)} %adj.5) | copy-start | bytes 1572868
  0.7 18.5 %copy-start.3 = (f32[1,8,32,256]{3,2,1,0:T(8,128)S(1)}, f32[1,8,32,256]{3,2,1,0:T(8,128)}, u32[]{:S(2)}) copy-start(f32[1,8,32,256]{3,2,1,0:T(8,128)} %buoy.3) | copy-start | bytes 786436
  0.7 18.5 %copy-start.5 = (bf16[2,64,80]{2,1,0:T(8,128)(2,1)S(1)}, bf16[2,64,80]{2,1,0:T(8,128)(2,1)}, u32[]{:S(2)}) copy-start(bf16[2,64,80]{2,1,0:T(8,128)(2,1)} %constant.7.clone.yf) | copy-start | bytes 61444
  0.7 18.5 %copy-start.6 = (s32[4096,2]{0,1:T(2,128)S(1)}, s32[4096,2]{0,1:T(2,128)}, u32[]{:S(2)}) copy-start(s32[4096,2]{0,1:T(2,128)} %param.15) | copy-start | bytes 98308
  0.7 18.5 %copy-start.7 = (f32[1,2,4096]{2,1,0:T(2,128)S(1)}, f32[1,2,4096]{2,1,0:T(2,128)}, u32[]{:S(2)}) copy-start(f32[1,2,4096]{2,1,0:T(2,128)} %res.1) | copy-start | bytes 98308
  2.4 9.6 %collective-permute-start.2 = (f32[4,8,4,256]{3,2,1,0:T(4,128)S(1)}, f32[4,8,4,256]{3,2,1,0:T(4,128)S(1)}, u32[]{:S(2)}, u32[]{:S(2)}) collective-permute-start(f32[4,8,4,256]{3,2,1,0:T(4,128)S(1)} %get-tuple-element.40), channel_id=1, source_target_pairs={{0,1},{1,0},{2,3},{3,2},{4,5},{5,4},{6,7},{7,6},{8,9},{9,8},{10,11... | collective-permute-start | bytes 393224 | tf_op jit(solution)/shard_map/ppermute | solution.py:522
  3.1 19.1 %collective-permute-start = (f32[2,4,32,256]{3,2,1,0:T(8,128)S(1)}, f32[2,4,32,256]{3,2,1,0:T(8,128)S(1)}, u32[]{:S(2)}, u32[]{:S(2)}) collective-permute-start(f32[2,4,32,256]{3,2,1,0:T(8,128)S(1)} %get-tuple-element.37), channel_id=1, source_target_pairs={{0,4},{1,5},{2,6},{3,7},{4,0},{5,1},{6,2},{7,3},{8,12},{9,13},{10,... | collective-permute-start | bytes 786440 | tf_op jit(solution)/shard_map/ppermute | solution.py:522
  3.1 19.1 %collective-permute-start.1 = (f32[2,4,32,256]{3,2,1,0:T(8,128)S(1)}, f32[2,4,32,256]{3,2,1,0:T(8,128)S(1)}, u32[]{:S(2)}, u32[]{:S(2)}) collective-permute-start(f32[2,4,32,256]{3,2,1,0:T(8,128)S(1)} %get-tuple-element.38), channel_id=1, source_target_pairs={{4,8},{5,9},{6,10},{7,11},{8,4},{9,5},{10,6},{11,7},{12,16},{13,17... | collective-permute-start | bytes 786440 | tf_op jit(solution)/shard_map/ppermute | solution.py:522
  7.5 11.6 %copy-start.9 = (s32[1,8,32]{2,1,0:T(8,128)S(1)}, s32[1,8,32]{2,1,0:T(8,128)}, u32[]{:S(2)}) copy-start(s32[1,8,32]{2,1,0:T(8,128)} %topo.1) | copy-start | bytes 3076
  7.5 24.3 %collective-permute-start.4 = (f32[2,4,32,256]{3,2,1,0:T(8,128)S(1)}, f32[2,4,32,256]{3,2,1,0:T(8,128)S(1)}, u32[]{:S(2)}, u32[]{:S(2)}) collective-permute-start(f32[2,4,32,256]{3,2,1,0:T(8,128)S(1)} %get-tuple-element.55), channel_id=1, source_target_pairs={{0,4},{1,5},{2,6},{3,7},{4,0},{5,1},{6,2},{7,3},{8,12},{9,13},{10,... | collective-permute-start | bytes 786440 | tf_op jit(solution)/shard_map/ppermute | solution.py:522
  7.6 24.2 %collective-permute-start.5 = (f32[2,4,32,256]{3,2,1,0:T(8,128)S(1)}, f32[2,4,32,256]{3,2,1,0:T(8,128)S(1)}, u32[]{:S(2)}, u32[]{:S(2)}) collective-permute-start(f32[2,4,32,256]{3,2,1,0:T(8,128)S(1)} %get-tuple-element.56), channel_id=1, source_target_pairs={{4,8},{5,9},{6,10},{7,11},{8,4},{9,5},{10,6},{11,7},{12,16},{13,17... | collective-permute-start | bytes 786440 | tf_op jit(solution)/shard_map/ppermute | solution.py:522
  12.0 7.1 %collective-permute-start.3 = (f32[4,8,4,256]{3,2,1,0:T(4,128)S(1)}, f32[4,8,4,256]{3,2,1,0:T(4,128)S(1)}, u32[]{:S(2)}, u32[]{:S(2)}) collective-permute-start(f32[4,8,4,256]{3,2,1,0:T(4,128)S(1)} %get-tuple-element.41), channel_id=1, source_target_pairs={{1,2},{2,1},{5,6},{6,5},{9,10},{10,9},{13,14},{14,13},{17,18},{18,... | collective-permute-start | bytes 393224 | tf_op jit(solution)/shard_map/ppermute | solution.py:522
  19.2 3.1 %copy-start.4 = (f32[1,8,32,256]{3,2,1,0:T(8,128)S(1)}, f32[1,8,32,256]{3,2,1,0:T(8,128)}, u32[]{:S(2)}) copy-start(f32[1,8,32,256]{3,2,1,0:T(8,128)} %mod.3) | copy-start | bytes 786436
  22.2 11.5 %copy-start.1 = (f32[1,4,1,8,32,256]{5,4,3,2,1,0:T(8,128)S(1)}, f32[1,4,1,8,32,256]{5,4,3,2,1,0:T(8,128)}, u32[]{:S(2)}) copy-start(f32[1,4,1,8,32,256]{5,4,3,2,1,0:T(8,128)} %fwd.3) | copy-start | bytes 3145732
  22.5 13.8 %collective-permute-start.7 = (f32[4,32,256]{2,1,0:T(8,128)S(1)}, f32[4,32,256]{2,1,0:T(8,128)S(1)}, u32[]{:S(2)}, u32[]{:S(2)}) collective-permute-start(f32[4,32,256]{2,1,0:T(8,128)S(1)} %get-tuple-element.59), channel_id=1, source_target_pairs={{0,4},{1,5},{2,6},{3,7},{4,0},{5,1},{6,2},{7,3},{8,12},{9,13},{10,... | collective-permute-start | bytes 393224 | tf_op jit(solution)/shard_map/ppermute | solution.py:522
  22.6 13.7 %collective-permute-start.8 = (f32[4,32,256]{2,1,0:T(8,128)S(1)}, f32[4,32,256]{2,1,0:T(8,128)S(1)}, u32[]{:S(2)}, u32[]{:S(2)}) collective-permute-start(f32[4,32,256]{2,1,0:T(8,128)S(1)} %get-tuple-element.60), channel_id=1, source_target_pairs={{4,8},{5,9},{6,10},{7,11},{8,4},{9,5},{10,6},{11,7},{12,16},{13,17... | collective-permute-start | bytes 393224 | tf_op jit(solution)/shard_map/ppermute | solution.py:522
  27.0 6.8 %collective-permute-start.6 = (f32[8,4,256]{2,1,0:T(4,128)S(1)}, f32[8,4,256]{2,1,0:T(4,128)S(1)}, u32[]{:S(2)}, u32[]{:S(2)}) collective-permute-start(f32[8,4,256]{2,1,0:T(4,128)S(1)} %get-tuple-element.57), channel_id=1, source_target_pairs={{1,2},{2,1},{5,6},{6,5},{9,10},{10,9},{13,14},{14,13},{17,18},{18,... | collective-permute-start | bytes 98312 | tf_op jit(solution)/shard_map/ppermute | solution.py:522
  33.7 2.6 %copy-start.8 = (bf16[2,32,16]{2,1,0:T(8,128)(2,1)S(1)}, bf16[2,32,16]{2,1,0:T(8,128)(2,1)}, u32[]{:S(2)}) copy-start(bf16[2,32,16]{2,1,0:T(8,128)(2,1)} %constant.8.clone.ye) | copy-start | bytes 6148
  35.1 1.3 %collective-permute-start.9 = (f32[8,4,256]{2,1,0:T(4,128)S(1)}, f32[8,4,256]{2,1,0:T(4,128)S(1)}, u32[]{:S(2)}, u32[]{:S(2)}) collective-permute-start(f32[8,4,256]{2,1,0:T(4,128)S(1)} %get-tuple-element.61), channel_id=1, source_target_pairs={{0,1},{1,0},{2,3},{3,2},{4,5},{5,4},{6,7},{7,6},{8,9},{9,8},{10,11... | collective-permute-start | bytes 98312 | tf_op jit(solution)/shard_map/ppermute | solution.py:522

commit v4 on v3

--- a/solution.py
+++ b/solution.py
@@ -146,9 +146,9 @@
 def edge_terms(i, count, low, high):
     terms = []
     for k in range(1, HALO + 1):
-        if i - k < 0:
+        if i - k < 0 and low is not None:
             terms.append((k, -1.0, low[HALO + i - k]))
-        if i + k >= count:
+        if i + k >= count and high is not None:
             terms.append((k, 1.0, high[i + k - count]))
     return terms
 
@@ -161,6 +161,12 @@
     return total
 
 
+def plus(value, *terms):
+    for term in terms:
+        value = value if term is None else value + term
+    return value
+
+
 def edge_laplace(i, count, low, high):
     total = None
     for k, _, value in edge_terms(i, count, low, high):
@@ -176,6 +182,10 @@
     return jnp.sum(picked, axis=1, keepdims=True).astype(jnp.int32)
 
 
+def planes(ref, n, rows):
+    return None if ref is None else [ref[n, i, rows] for i in range(HALO)]
+
+
 def row_parity():
     return lax.rem(lax.axis_index("blk") // YBLOCKS, 2)
 
@@ -193,7 +203,7 @@
 
 def first_kernel(
     adj, mod, buoy, topo_in, fwd,
-    x1, x2, f1, f2, y1, y2, s0,
+    x1, x2, y1, y2, s0,
     cur_v, mod_v, topo, buoy_v, fields_v, sem,
 ):
     width, height, depth = s0.shape
@@ -209,8 +219,6 @@
             (fwd.at[0, pl.ds(1, 2), 0], fields_v),
             (buoy.at[0, first], x1.at[0]),
             (buoy.at[0, second], x2.at[0]),
-            (fwd.at[0, pl.ds(1, 2), 0, first], f1),
-            (fwd.at[0, pl.ds(1, 2), 0, second], f2),
         ],
         sem,
     )
@@ -241,16 +249,19 @@
         c.wait()
 
 
-def early_kernel(
-    adj, buoy, topo, s0, rec, res, y1, y2, zf, yf,
-    rest, sx_own, sy, sz, gx_own, gy, gz, weight, scale, source,
-    zs, zb, ys, yb,
-):
-    width, height, depth = s0.shape
-    size = lax.axis_index("blk")
-    anchor_x = size // YBLOCKS * width
-    anchor_y = lax.rem(size, YBLOCKS) * height
-    factor_y = yf[column_parity()]
+def source_kernel(topo, rec, res, fwd, _, scale, source, x1, x2, sem):
+    width, height, depth = scale.shape
+    parity = row_parity()
+    copies = copy_all(
+        [
+            (fwd.at[0, pl.ds(1, 2), 0, pl.ds((1 - parity) * HALO, HALO)], x1),
+            (fwd.at[0, pl.ds(1, 2), 0, pl.ds(parity * HALO, HALO)], x2),
+        ],
+        sem,
+    )
+    index = lax.axis_index("blk")
+    anchor_x = index // YBLOCKS * width
+    anchor_y = lax.rem(index, YBLOCKS) * height
     count = rec.shape[1]
     rx = rec[0:1, :] - anchor_x
     ry = rec[1:2, :] - anchor_y
@@ -267,11 +278,6 @@
         precision=lax.Precision.HIGHEST,
         preferred_element_type=F32,
     )
-    zs[...] = z_product(s0[...], zf[...])
-    zb[...] = z_product(buoy[0], zf[:, :depth])
-    for i in range(width):
-        ys[i] = y_product(s0[i], y1[1, i], y2[1, i], factor_y)
-        yb[i] = y_product(buoy[0, i], y1[0, i], y2[0, i], factor_y[:height])
     lanes = lax.broadcasted_iota(jnp.int32, (height, depth), 1)
     for i in range(width):
         surface = depth_of_surface(topo[0, i : i + 1, :], height)
@@ -281,6 +287,22 @@
         for s in range(STEPS):
             n = s * width + i
             source[s, i] = jnp.where(at, plane[:, n : n + 1], 0.0)
+    for c in copies:
+        c.wait()
+
+
+def early_kernel(
+    adj, buoy, s0, y1, y2, zf, yf, scale, source,
+    rest, sx_own, sy, sz, gx_own, gy, gz, weight,
+    zs, zb, ys, yb,
+):
+    width, height, depth = s0.shape
+    factor_y = yf[column_parity()]
+    zs[...] = z_product(s0[...], zf[...])
+    zb[...] = z_product(buoy[0], zf[:, :depth])
+    for i in range(width):
+        ys[i] = y_product(s0[i], y1[1, i], y2[1, i], factor_y)
+        yb[i] = y_product(buoy[0, i], y1[0, i], y2[0, i], factor_y[:height])
     for t in range(height // 8):
         rows = pl.ds(8 * t, 8)
         own = [s0[i, rows] for i in range(width)]
@@ -311,8 +333,8 @@
 
 
 def finish_kernel(
-    xa1, xa2, rest, sx_own, gx_own, weight, scale, mod,
-    e0, s1, sx, gx, x1, x2, y2,
+    xa1, xa2, rest, sx_own, gx_own, weight, scale, mod, _,
+    e0, s1, sx, gx, x1, x2, y1, y2, f2,
 ):
     width, height, depth = e0.shape
 
@@ -350,19 +372,18 @@
         body(xa1, xa2, x1, x2)
 
     even = column_parity() == 0
-    y2[...] = jnp.where(even, s1[:, :HALO], s1[:, height - HALO :])
+    y1[...] = jnp.where(even, s1[:, height - HALO :], s1[:, :HALO])
+    y2[...] = jnp.where(even, s1[:, :8], s1[:, height - 8 :])
 
 
 def middle_kernel(
-    adj, e0, s1, sx0, sy0, sz0, gy, gz, weight, scale, source, fwd, xf1, xf2, yf1, yf2, zf, yf, ys2,
-    rest, sx_own, image, fx, fy, y1, image_mod, states,
+    adj, e0, s1, sx0, sy0, sz0, gy, gz, weight, scale, source, fwd, xf, yf1, yf2, zf, yf,
+    rest, sx_own, image, fx, fy, image_mod, states,
     zs, ys, z1, z2, ya, image_v, sem,
 ):
     width, height, depth = e0.shape
     first = pltpu.make_async_copy(e0, states.at[0, 0, 0], sem.at[0])
     first.start()
-    even = column_parity() == 0
-    y1[...] = jnp.where(even, s1[:, height - HALO :], s1[:, :HALO])
     for i in range(width):
         f0, f1, f2, f3 = (fwd[0, n, 0, i] for n in range(4))
         image_v[i] = adj[0, 1, 0, i] * (f0 - 2.0 * f1 + f2) + e0[i] * (f1 - 2.0 * f2 + f3)
@@ -388,10 +409,8 @@
             own2 = [fwd[0, 2, 0, i, rows] for i in range(width)]
             slope1 = x_slope(own1)
             slope2 = x_slope(own2)
-            low1 = [low_ref[0, i, rows] for i in range(HALO)]
-            high1 = [high_ref[0, i, rows] for i in range(HALO)]
-            low2 = [low_ref[1, i, rows] for i in range(HALO)]
-            high2 = [high_ref[1, i, rows] for i in range(HALO)]
+            low1, low2 = planes(low_ref, 0, rows), planes(low_ref, 1, rows)
+            high1, high2 = planes(high_ref, 0, rows), planes(high_ref, 1, rows)
             for i in range(width):
                 now, before = adj[0, 1, 0, i, rows], e0[i, rows]
                 s_y = C_UNIT * ys[i, rows]
@@ -404,8 +423,8 @@
                     moved + weight[i, rows] * lap + gy[i, rows] * s_y + gz[i, rows] * s_z
                 )
                 sx_own[i, rows] = slope[i]
-                f1x = slope1[i] + edge_slope(i, width, low1, high1)
-                fx[i, rows] = slope2[i] + edge_slope(i, width, low2, high2)
+                f1x = plus(slope1[i], edge_slope(i, width, low1, high1))
+                fx[i, rows] = plus(slope2[i], edge_slope(i, width, low2, high2))
                 image[i, rows] = (
                     f1x * sx0[i, rows]
                     + C_UNIT
@@ -419,18 +438,18 @@
 
     @pl.when(row_parity() == 0)
     def _():
-        body(xf2, xf1)
+        body(None, xf)
 
     @pl.when(row_parity() == 1)
     def _():
-        body(xf1, xf2)
+        body(xf, None)
 
     first.wait()
     second.wait()
 
 
 def last_kernel(
-    xs1, xs2, ys1, ys2, rest, sx_own, image, fx, fy, gx, gy, weight, ye, states_in,
+    xs1, xs2, ys1, ys2, rest, sx_own, image, fx, fy, gx, gy, weight, ye, sx0, xf2, states_in,
     image_out, states_out,
     image_v, e1_v, sem,
 ):
@@ -445,18 +464,28 @@
             pltpu.make_async_copy(image_v.at[:, rows], image_out.at[0, :, rows], sem.at[tiles + t]),
         )
 
-    edges = [dot(factor, edge_parts(ys1[i], ys2[i])) for i in range(width)]
-
-    def body(low_ref, high_ref):
+    even = column_parity() == 0
+    edges = []
+    for i in range(width):
+        second = jnp.where(even, ys2[i, 8 - HALO :], ys2[i, :HALO])
+        edges.append(dot(factor, edge_parts(ys1[i], second)))
+
+    def body(low_ref, high_ref, low_fields, high_fields):
         for t in range(tiles):
             rows = pl.ds(8 * t, 8)
             low = [low_ref[i, rows] for i in range(HALO)]
             high = [high_ref[i, rows] for i in range(HALO)]
+            low1, low2 = planes(low_fields, 0, rows), planes(low_fields, 1, rows)
+            high1, high2 = planes(high_fields, 0, rows), planes(high_fields, 1, rows)
             for i in range(width):
                 s_x = sx_own[i, rows] + edge_slope(i, width, low, high)
                 lap = edge_laplace(i, width, low, high)
                 add = gx[i, rows] * s_x
-                shown = fx[i, rows] * s_x
+                f_x = plus(fx[i, rows], edge_slope(i, width, low2, high2))
+                shown = image[i, rows] + f_x * s_x
+                f_x = edge_slope(i, width, low1, high1)
+                if f_x is not None:
+                    shown = shown + f_x * sx0[i, rows]
                 if t == 0 or t == tiles - 1:
                     n = 0 if t == 0 else 8
                     s_y = C_UNIT * edges[i][n : n + 8]
@@ -464,17 +493,17 @@
                     add = add + gy[i, rows] * s_y
                     shown = shown + C_UNIT * (fy[i, rows] * s_y)
                 e1_v[i, rows] = rest[i, rows] + weight[i, rows] * lap + add
-                image_v[i, rows] = image[i, rows] + shown
+                image_v[i, rows] = shown
             for c in leave(t):
                 c.start()
 
     @pl.when(row_parity() == 0)
     def _():
-        body(xs2, xs1)
+        body(xs2, xs1, xf2, None)
 
     @pl.when(row_parity() == 1)
     def _():
-        body(xs1, xs2)
+        body(xs1, xs2, None, xf2)
 
     for t in range(tiles):
         for c in leave(t):
@@ -523,57 +552,66 @@
 
     ahead = (2, HALO, height, depth)
     edge = (4, width, HALO, depth)
-    xa1, xa2, xf1, xf2, ya1, ya2, s0 = call(
+    xa1, xa2, ya1, ya2, s0 = call(
         first_kernel,
         "scaled_and_edges",
         [(adjoint_in, False), (modulus, False), (buoyancy, False), (topography, False), (forward, False)],
-        [(ahead, True)] * 4 + [(edge, True)] * 2 + [(block, True)],
+        [(ahead, True)] * 2 + [(edge, True)] * 2 + [(block, True)],
         [VMEM(block, F32), VMEM(block, F32), VMEM(topography.shape, jnp.int32), VMEM(block, F32),
-         VMEM((2,) + block, F32), dma((9,))],
+         VMEM((2,) + block, F32), dma((7,))],
     )
     xa1, xa2 = swap(xa1, rows1), swap(xa2, rows2)
     ya1, ya2 = swap(ya1, cols1), swap(ya2, cols2)
-    xf1, xf2 = swap(xf1, rows1), swap(xf2, rows2)
     z_out = (width, height, 2 * depth)
     y_out = (width, 2 * height, depth)
-    rest, sx_own, sy, sz, gx_own, gy, gz, weight, scale, source = call(
+    scale, source, xf1, xf2 = call(
+        source_kernel,
+        "sources_and_planes",
+        [(topography, True), (receivers.T, True), (residuals, True), (forward, False), (ya1, True)],
+        [(block, True), ((STEPS,) + block, True), (ahead, True), (ahead, True)],
+        [dma((2,))],
+    )
+    xf1 = swap(xf1, rows1)
+    rest, sx_own, sy, sz, gx_own, gy, gz, weight = call(
         early_kernel,
         "step0_own",
-        [(adjoint_in, True), (buoyancy, True), (topography, True), (s0, True),
-         (receivers.T, True), (residuals, True), (ya1, True), (ya2, True), (zf, True), (yf, True)],
-        [(block, True)] * 9 + [((STEPS,) + block, True)],
+        [(adjoint_in, True), (buoyancy, True), (s0, True), (ya1, True), (ya2, True), (zf, True), (yf, True),
+         (scale, True), (source, True)],
+        [(block, True)] * 8,
         [VMEM(z_out, F32), VMEM(block, F32), VMEM(y_out, F32), VMEM(block, F32)],
         us=4.0,
     )
     half = (HALO, height, depth)
     side = (width, HALO, depth)
-    e0, s1, sx, gx, xs1, xs2, ys2 = call(
+    rows8 = (width, 8, depth)
+    e0, s1, sx, gx, xs1, xs2, ys1, ys2, xf2 = call(
         finish_kernel,
         "step0_planes",
         [(xa1, True), (xa2, True), (rest, True), (sx_own, True), (gx_own, True), (weight, True), (scale, True),
-         (modulus, True)],
-        [(block, True)] * 4 + [(half, True)] * 2 + [(side, True)],
-    )
-    xs1, xs2, ys2 = swap(xs1, rows1), swap(xs2, rows2), swap(ys2, cols2)
-    rest, sx_own, image, fx, fy, ys1, image_mod, states = call(
+         (modulus, True), (xf2, True)],
+        [(block, True)] * 4 + [(half, True)] * 2 + [(side, True), (rows8, True)] + [(ahead, True)],
+        aliases={8: 8},
+    )
+    xf2, xs1, xs2 = swap(xf2, rows2), swap(xs1, rows1), swap(xs2, rows2)
+    ys1, ys2 = swap(ys1, cols1), swap(ys2, cols2)
+    rest, sx_own, image, fx, fy, image_mod, states = call(
         middle_kernel,
         "images_and_step1_own",
         [(adjoint_in, True), (e0, True), (s1, True), (sx, True), (sy, True), (sz, True), (gy, True), (gz, True),
-         (weight, True), (scale, True), (source, True), (forward, True), (xf1, True), (xf2, True), (ya1, True),
-         (ya2, True), (zf, True), (yf, True), (ys2, True)],
-        [(block, True)] * 5 + [(side, True), ((1,) + block, False), ((1, STEPS, 1) + block, False)],
+         (weight, True), (scale, True), (source, True), (forward, True), (xf1, True), (ya1, True),
+         (ya2, True), (zf, True), (yf, True)],
+        [(block, True)] * 5 + [((1,) + block, False), ((1, STEPS, 1) + block, False)],
         [VMEM(z_out, F32), VMEM(y_out, F32)] + [VMEM(block, F32)] * 4 + [dma((2,))],
-        us=5.0,
-    )
-    ys1 = swap(ys1, cols1)
+        us=20.0,
+    )
     image_buo, states = call(
         last_kernel,
         "step1_planes",
         [(xs1, True), (xs2, True), (ys1, True), (ys2, True), (rest, True), (sx_own, True), (image, True), (fx, True),
-         (fy, True), (gx, True), (gy, True), (weight, True), (ye, True), (states, False)],
+         (fy, True), (gx, True), (gy, True), (weight, True), (ye, True), (sx, True), (xf2, True), (states, False)],
         [((1,) + block, False), ((1, STEPS, 1) + block, False)],
         [VMEM(block, F32), VMEM(block, F32), dma((2 * (height // 8),))],
-        aliases={13: 1},
+        aliases={15: 1},
     )
     if lax.axis_size("shot") > 1:
         image_mod, image_buo = lax.psum((image_mod, image_buo), "shot")

time: 37.7 us -> 34.6 us (0.918)
  the two profiles are of different devices: /device:TPU:5 before, /device:TPU:0 now
where the time goes in v4:
time: 34.6 us; the launch traced here: 34.3 us
  starting transfers between devices  16.2 us (47%)
  waiting for transfers between devices  11.2 us (32%)
  Pallas kernels  6 us (17%)
  between operations  0.83 us (2%)
    ppermute x10, starting transfers between devices, swap(): return lax.ppermute(value, 'blk', pairs)  16.2 us
    ppermute x10, waiting for transfers between devices, swap(): return lax.ppermute(value, 'blk', pairs)  11.2 us
    pallas_call x6, Pallas kernels, call(): pl.pallas_call(kernel, name=name, in_specs=in_specs, out_specs=out_specs,...  6 us
  transfers between devices with their start and end apart: 10, of which 4 were waited for; matrix products, arithmetic and copies ran while one was open for 0% of the time, Pallas kernels for 10%

profile of v4, /device:TPU:0, one launch (start us, length us, event | category | flops | bytes accessed | tf_op | source)
XLA Modules:
  0.0 34.3 jit_solution(10971012194926590640)
XLA Ops:
  0.6 0.0 copy-start.7
  0.6 0.0 copy-start.6
  0.7 1.4 %scaled_and_edges.1 = (f32[2,4,32,256]{3,2,1,0:T(8,128)S(1)}, f32[2,4,32,256]{3,2,1,0:T(8,128)S(1)}, f32[4,8,4,256]{3,2,1,0:T(4,128)S(1)}, f32[4,8,4,256]{3,2,1,0:T(4,128)S(1)}, f32[8,32,256]{2,1,0:T(8,128)S(1)}) custom-call(f32[1,2,1,8,32,256]{5,4,3,2,1,0:T(8,128)} %adj.5, f32[1,8,32,256]{3,2,1,0:T(8,128)} %mod.3, f32[1,8,32,256]{3,2,1,0:T(8,128)} %buoy.3, ...), custom_call_target="tpu_custom_call" | custom-call | bytes 3000000 | tf_op jit(solution)/shard_map/scaled_and_edges/pallas_call | solution.py:524
  2.1 0.0 copy-start.9
  2.1 3.0 %collective-permute-start = (f32[2,4,32,256]{3,2,1,0:T(8,128)S(1)}, f32[2,4,32,256]{3,2,1,0:T(8,128)S(1)}, u32[]{:S(2)}, u32[]{:S(2)}) collective-permute-start(f32[2,4,32,256]{3,2,1,0:T(8,128)S(1)} %get-tuple-element.38), channel_id=1, source_target_pairs={{0,4},{1,5},{2,6},{3,7},{4,0},{5,1},{6,2},{7,3},{8,12},{9,13},{10,... | collective-permute-start | bytes 786440 | tf_op jit(solution)/shard_map/ppermute | solution.py:551
  5.1 0.7 %collective-permute-start.1 = (f32[2,4,32,256]{3,2,1,0:T(8,128)S(1)}, f32[2,4,32,256]{3,2,1,0:T(8,128)S(1)}, u32[]{:S(2)}, u32[]{:S(2)}) collective-permute-start(f32[2,4,32,256]{3,2,1,0:T(8,128)S(1)} %get-tuple-element.39), channel_id=1, source_target_pairs={{4,8},{5,9},{6,10},{7,11},{8,4},{9,5},{10,6},{11,7},{12,16},{13,17... | collective-permute-start | bytes 786440 | tf_op jit(solution)/shard_map/ppermute | solution.py:551
  5.8 0.1 collective-permute-start.2
  5.9 0.7 %collective-permute-start.3 = (f32[4,8,4,256]{3,2,1,0:T(4,128)S(1)}, f32[4,8,4,256]{3,2,1,0:T(4,128)S(1)}, u32[]{:S(2)}, u32[]{:S(2)}) collective-permute-start(f32[4,8,4,256]{3,2,1,0:T(4,128)S(1)} %get-tuple-element.42), channel_id=1, source_target_pairs={{1,2},{2,1},{5,6},{6,5},{9,10},{10,9},{13,14},{14,13},{17,18},{18,... | collective-permute-start | bytes 393224 | tf_op jit(solution)/shard_map/ppermute | solution.py:551
  6.6 0.7 %collective-permute-done.2._.y1.yf1 = f32[4,8,4,256]{3,2,1,0:T(4,128)S(1)} collective-permute-done((f32[4,8,4,256]{3,2,1,0:T(4,128)S(1)}, f32[4,8,4,256]{3,2,1,0:T(4,128)S(1)}, u32[]{:S(2)}, u32[]{:S(2)}) %collective-permute-start.2) | collective-permute-done | bytes 131104 | tf_op jit(solution)/shard_map/ppermute | solution.py:551
  7.2 0.0 copy-done.7
  7.2 0.0 copy-done.6
  7.2 0.0 copy-done.9
  7.2 0.0 copy-start.1
  7.2 0.0 copy-start.2
  7.3 0.0 copy-start.3
  7.3 0.0 copy-start.5
  7.3 1.1 %sources_and_planes.1 = (f32[8,32,256]{2,1,0:T(8,128)S(1)}, f32[2,8,32,256]{3,2,1,0:T(8,128)S(1)}, f32[2,4,32,256]{3,2,1,0:T(8,128)S(1)}, f32[2,4,32,256]{3,2,1,0:T(8,128)S(1)}) custom-call(s32[1,8,32]{2,1,0:T(8,128)S(1)} %copy-done.9, s32[2,4096]{1,0:T(2,128)S(1)} %bitcast.1, f32[1,2,4096]{2,1,0:T(2,128)S(1)} %copy-done.7, f32[1,4,1,8,32,256]{5,4,3,2,1,0:T(8,128)} %fwd.5, ...), custom_call_target="tpu_custom_call" | custom-call | bytes 3000000 | tf_op jit(solution)/shard_map/sources_and_planes/pallas_call | solution.py:524
  8.4 4.3 %collective-permute-start.4 = (f32[2,4,32,256]{3,2,1,0:T(8,128)S(1)}, f32[2,4,32,256]{3,2,1,0:T(8,128)S(1)}, u32[]{:S(2)}, u32[]{:S(2)}) collective-permute-start(f32[2,4,32,256]{3,2,1,0:T(8,128)S(1)} %get-tuple-element.57), channel_id=1, source_target_pairs={{0,4},{1,5},{2,6},{3,7},{4,0},{5,1},{6,2},{7,3},{8,12},{9,13},{10,... | collective-permute-start | bytes 786440 | tf_op jit(solution)/shard_map/ppermute | solution.py:551
  12.8 0.0 collective-permute-done.3.y2.yf2
  12.8 0.0 copy-done.1
  12.8 0.0 copy-done.2
  12.8 0.0 copy-done.3
  12.8 0.0 copy-done.5
  12.8 0.0 copy-start.4
  12.8 0.8 %step0_own.1 = (f32[8,32,256]{2,1,0:T(8,128)S(1)}, f32[8,32,256]{2,1,0:T(8,128)S(1)}, f32[8,32,256]{2,1,0:T(8,128)S(1)}, f32[8,32,256]{2,1,0:T(8,128)S(1)}, f32[...) custom-call(f32[1,2,1,8,32,256]{5,4,3,2,1,0:T(8,128)S(1)} %copy-done.1, ...), custom_call_target="tpu_custom_call" | custom-call | bytes 12000000 | tf_op jit(solution)/shard_map/step0_own/pallas_call | solution.py:524
  13.6 3.9 %collective-permute-done.xa1 = f32[2,4,32,256]{3,2,1,0:T(8,128)S(1)} collective-permute-done((f32[2,4,32,256]{3,2,1,0:T(8,128)S(1)}, f32[2,4,32,256]{3,2,1,0:T(8,128)S(1)}, u32[]{:S(2)}, u32[]{:S(2)}) %collective-permute-start) | collective-permute-done | bytes 262176 | tf_op jit(solution)/shard_map/ppermute | solution.py:551
  17.5 0.0 collective-permute-done.1.xa2
  17.5 0.0 copy-done.4
  17.5 0.0 copy-start
  17.5 0.2 step0_planes.1
  17.7 0.8 %collective-permute-start.9 = (f32[2,4,32,256]{3,2,1,0:T(8,128)S(1)}, f32[2,4,32,256]{3,2,1,0:T(8,128)S(1)}, u32[]{:S(2)}, u32[]{:S(2)}) collective-permute-start(f32[2,4,32,256]{3,2,1,0:T(8,128)S(1)} %get-tuple-element.69), channel_id=1, source_target_pairs={{4,8},{5,9},{6,10},{7,11},{8,4},{9,5},{10,6},{11,7},{12,16},{13,17... | collective-permute-start | bytes 786440 | tf_op jit(solution)/shard_map/ppermute | solution.py:551
  18.5 5.3 %collective-permute-start.5 = (f32[4,32,256]{2,1,0:T(8,128)S(1)}, f32[4,32,256]{2,1,0:T(8,128)S(1)}, u32[]{:S(2)}, u32[]{:S(2)}) collective-permute-start(f32[4,32,256]{2,1,0:T(8,128)S(1)} %get-tuple-element.59), channel_id=1, source_target_pairs={{0,4},{1,5},{2,6},{3,7},{4,0},{5,1},{6,2},{7,3},{8,12},{9,13},{10,... | collective-permute-start | bytes 393224 | tf_op jit(solution)/shard_map/ppermute | solution.py:551
  23.8 0.7 %collective-permute-start.6 = (f32[4,32,256]{2,1,0:T(8,128)S(1)}, f32[4,32,256]{2,1,0:T(8,128)S(1)}, u32[]{:S(2)}, u32[]{:S(2)}) collective-permute-start(f32[4,32,256]{2,1,0:T(8,128)S(1)} %get-tuple-element.60), channel_id=1, source_target_pairs={{4,8},{5,9},{6,10},{7,11},{8,4},{9,5},{10,6},{11,7},{12,16},{13,17... | collective-permute-start | bytes 393224 | tf_op jit(solution)/shard_map/ppermute | solution.py:551
  24.5 0.7 %collective-permute-start.8 = (f32[8,8,256]{2,1,0:T(8,128)S(1)}, f32[8,8,256]{2,1,0:T(8,128)S(1)}, u32[]{:S(2)}, u32[]{:S(2)}) collective-permute-start(f32[8,8,256]{2,1,0:T(8,128)S(1)} %get-tuple-element.62), channel_id=1, source_target_pairs={{1,2},{2,1},{5,6},{6,5},{9,10},{10,9},{13,14},{14,13},{17,18},{18,... | collective-permute-start | bytes 196616 | tf_op jit(solution)/shard_map/ppermute | solution.py:551
  25.2 5.4 %collective-permute-done.4.xf = f32[2,4,32,256]{3,2,1,0:T(8,128)S(1)} collective-permute-done((f32[2,4,32,256]{3,2,1,0:T(8,128)S(1)}, f32[2,4,32,256]{3,2,1,0:T(8,128)S(1)}, u32[]{:S(2)}, u32[]{:S(2)}) %collective-permute-start.4) | collective-permute-done | bytes 262176 | tf_op jit(solution)/shard_map/ppermute | solution.py:551
  30.6 0.0 collective-permute-start.7
  30.6 0.0 copy-done
  30.6 0.0 copy-start.8
  30.6 1.3 %images_and_step1_own.1 = (f32[8,32,256]{2,1,0:T(8,128)S(1)}, f32[8,32,256]{2,1,0:T(8,128)S(1)}, f32[8,32,256]{2,1,0:T(8,128)S(1)}, f32[8,32,256]{2,1,0:T(8,128)...) custom-call(f32[1,2,1,8,32,256]{5,4,3,2,1,0:T(8,128)S(1)} %copy-done.1, ...), custom_call_target="tpu_custom_call" | custom-call | bytes 60000000 | tf_op jit(solution)/shard_map/images_and_step1_own/pallas_call | solution.py:524
  31.9 0.0 collective-permute-done.7.ys1
  31.9 0.0 collective-permute-done.8.ys2
  31.9 1.2 %collective-permute-done.5.xs1 = f32[4,32,256]{2,1,0:T(8,128)S(1)} collective-permute-done((f32[4,32,256]{2,1,0:T(8,128)S(1)}, f32[4,32,256]{2,1,0:T(8,128)S(1)}, u32[]{:S(2)}, u32[]{:S(2)}) %collective-permute-start.5) | collective-permute-done | bytes 131104 | tf_op jit(solution)/shard_map/ppermute | solution.py:551
  33.2 0.0 collective-permute-done.6.xs2
  33.2 0.0 collective-permute-done.9.xf2
  33.2 0.0 copy-done.8
  33.2 1.1 %step1_planes.1 = (f32[1,8,32,256]{3,2,1,0:T(8,128)}, f32[1,2,1,8,32,256]{5,4,3,2,1,0:T(8,128)}) custom-call(f32[4,32,256]{2,1,0:T(8,128)S(1)} %collective-permute-done.5.xs1, f32[4,32,256]{2,1,0:T(8,128)S(1)} %collective-permute-done.6.xs2, f32[8,4,256]{2,1,0:T(4,128)S(1)} %collective-permute-done.7.ys1, ...), custom_call_target="tpu_custom_call", output_to_operand_aliasing={{1}: (15, {})} | custom-call | bytes 3000000 | tf_op jit(solution)/shard_map/step1_planes/pallas_call | solution.py:524
Async XLA Ops:
  0.6 6.6 %copy-start.7 = (f32[1,2,4096]{2,1,0:T(2,128)S(1)}, f32[1,2,4096]{2,1,0:T(2,128)}, u32[]{:S(2)}) copy-start(f32[1,2,4096]{2,1,0:T(2,128)} %res.1) | copy-start | bytes 98308
  0.6 6.6 %copy-start.6 = (s32[4096,2]{0,1:T(2,128)S(1)}, s32[4096,2]{0,1:T(2,128)}, u32[]{:S(2)}) copy-start(s32[4096,2]{0,1:T(2,128)} %param.15) | copy-start | bytes 98308
  2.1 5.1 %copy-start.9 = (s32[1,8,32]{2,1,0:T(8,128)S(1)}, s32[1,8,32]{2,1,0:T(8,128)}, u32[]{:S(2)}) copy-start(s32[1,8,32]{2,1,0:T(8,128)} %topo.1) | copy-start | bytes 3076
  2.1 15.4 %collective-permute-start = (f32[2,4,32,256]{3,2,1,0:T(8,128)S(1)}, f32[2,4,32,256]{3,2,1,0:T(8,128)S(1)}, u32[]{:S(2)}, u32[]{:S(2)}) collective-permute-start(f32[2,4,32,256]{3,2,1,0:T(8,128)S(1)} %get-tuple-element.38), channel_id=1, source_target_pairs={{0,4},{1,5},{2,6},{3,7},{4,0},{5,1},{6,2},{7,3},{8,12},{9,13},{10,... | collective-permute-start | bytes 786440 | tf_op jit(solution)/shard_map/ppermute | solution.py:551
  5.1 12.3 %collective-permute-start.1 = (f32[2,4,32,256]{3,2,1,0:T(8,128)S(1)}, f32[2,4,32,256]{3,2,1,0:T(8,128)S(1)}, u32[]{:S(2)}, u32[]{:S(2)}) collective-permute-start(f32[2,4,32,256]{3,2,1,0:T(8,128)S(1)} %get-tuple-element.39), channel_id=1, source_target_pairs={{4,8},{5,9},{6,10},{7,11},{8,4},{9,5},{10,6},{11,7},{12,16},{13,17... | collective-permute-start | bytes 786440 | tf_op jit(solution)/shard_map/ppermute | solution.py:551
  5.8 1.4 %collective-permute-start.2 = (f32[4,8,4,256]{3,2,1,0:T(4,128)S(1)}, f32[4,8,4,256]{3,2,1,0:T(4,128)S(1)}, u32[]{:S(2)}, u32[]{:S(2)}) collective-permute-start(f32[4,8,4,256]{3,2,1,0:T(4,128)S(1)} %get-tuple-element.41), channel_id=1, source_target_pairs={{0,1},{1,0},{2,3},{3,2},{4,5},{5,4},{6,7},{7,6},{8,9},{9,8},{10,11... | collective-permute-start | bytes 393224 | tf_op jit(solution)/shard_map/ppermute | solution.py:551
  5.9 6.9 %collective-permute-start.3 = (f32[4,8,4,256]{3,2,1,0:T(4,128)S(1)}, f32[4,8,4,256]{3,2,1,0:T(4,128)S(1)}, u32[]{:S(2)}, u32[]{:S(2)}) collective-permute-start(f32[4,8,4,256]{3,2,1,0:T(4,128)S(1)} %get-tuple-element.42), channel_id=1, source_target_pairs={{1,2},{2,1},{5,6},{6,5},{9,10},{10,9},{13,14},{14,13},{17,18},{18,... | collective-permute-start | bytes 393224 | tf_op jit(solution)/shard_map/ppermute | solution.py:551
  7.2 5.5 %copy-start.1 = (f32[1,2,1,8,32,256]{5,4,3,2,1,0:T(8,128)S(1)}, f32[1,2,1,8,32,256]{5,4,3,2,1,0:T(8,128)}, u32[]{:S(2)}) copy-start(f32[1,2,1,8,32,256]{5,4,3,2,1,0:T(8,128)} %adj.5) | copy-start | bytes 1572868
  7.2 5.5 %copy-start.2 = (bf16[256,512]{1,0:T(8,128)(2,1)S(1)}, bf16[256,512]{1,0:T(8,128)(2,1)}, u32[]{:S(2)}) copy-start(bf16[256,512]{1,0:T(8,128)(2,1)} %constant.6.clone.zf) | copy-start | bytes 786436
  7.3 5.5 %copy-start.3 = (f32[1,8,32,256]{3,2,1,0:T(8,128)S(1)}, f32[1,8,32,256]{3,2,1,0:T(8,128)}, u32[]{:S(2)}) copy-start(f32[1,8,32,256]{3,2,1,0:T(8,128)} %buoy.3) | copy-start | bytes 786436
  7.3 5.5 %copy-start.5 = (bf16[2,64,80]{2,1,0:T(8,128)(2,1)S(1)}, bf16[2,64,80]{2,1,0:T(8,128)(2,1)}, u32[]{:S(2)}) copy-start(bf16[2,64,80]{2,1,0:T(8,128)(2,1)} %constant.7.clone.yf) | copy-start | bytes 61444
  8.4 22.2 %collective-permute-start.4 = (f32[2,4,32,256]{3,2,1,0:T(8,128)S(1)}, f32[2,4,32,256]{3,2,1,0:T(8,128)S(1)}, u32[]{:S(2)}, u32[]{:S(2)}) collective-permute-start(f32[2,4,32,256]{3,2,1,0:T(8,128)S(1)} %get-tuple-element.57), channel_id=1, source_target_pairs={{0,4},{1,5},{2,6},{3,7},{4,0},{5,1},{6,2},{7,3},{8,12},{9,13},{10,... | collective-permute-start | bytes 786440 | tf_op jit(solution)/shard_map/ppermute | solution.py:551
  12.8 4.7 %copy-start.4 = (f32[1,8,32,256]{3,2,1,0:T(8,128)S(1)}, f32[1,8,32,256]{3,2,1,0:T(8,128)}, u32[]{:S(2)}) copy-start(f32[1,8,32,256]{3,2,1,0:T(8,128)} %mod.3) | copy-start | bytes 786436
  17.5 13.1 %copy-start = (f32[1,4,1,8,32,256]{5,4,3,2,1,0:T(8,128)S(1)}, f32[1,4,1,8,32,256]{5,4,3,2,1,0:T(8,128)}, u32[]{:S(2)}) copy-start(f32[1,4,1,8,32,256]{5,4,3,2,1,0:T(8,128)} %fwd.5) | copy-start | bytes 3145732
  17.7 15.5 %collective-permute-start.9 = (f32[2,4,32,256]{3,2,1,0:T(8,128)S(1)}, f32[2,4,32,256]{3,2,1,0:T(8,128)S(1)}, u32[]{:S(2)}, u32[]{:S(2)}) collective-permute-start(f32[2,4,32,256]{3,2,1,0:T(8,128)S(1)} %get-tuple-element.69), channel_id=1, source_target_pairs={{4,8},{5,9},{6,10},{7,11},{8,4},{9,5},{10,6},{11,7},{12,16},{13,17... | collective-permute-start | bytes 786440 | tf_op jit(solution)/shard_map/ppermute | solution.py:551
  18.5 14.6 %collective-permute-start.5 = (f32[4,32,256]{2,1,0:T(8,128)S(1)}, f32[4,32,256]{2,1,0:T(8,128)S(1)}, u32[]{:S(2)}, u32[]{:S(2)}) collective-permute-start(f32[4,32,256]{2,1,0:T(8,128)S(1)} %get-tuple-element.59), channel_id=1, source_target_pairs={{0,4},{1,5},{2,6},{3,7},{4,0},{5,1},{6,2},{7,3},{8,12},{9,13},{10,... | collective-permute-start | bytes 393224 | tf_op jit(solution)/shard_map/ppermute | solution.py:551
  23.8 9.3 %collective-permute-start.6 = (f32[4,32,256]{2,1,0:T(8,128)S(1)}, f32[4,32,256]{2,1,0:T(8,128)S(1)}, u32[]{:S(2)}, u32[]{:S(2)}) collective-permute-start(f32[4,32,256]{2,1,0:T(8,128)S(1)} %get-tuple-element.60), channel_id=1, source_target_pairs={{4,8},{5,9},{6,10},{7,11},{8,4},{9,5},{10,6},{11,7},{12,16},{13,17... | collective-permute-start | bytes 393224 | tf_op jit(solution)/shard_map/ppermute | solution.py:551
  24.5 7.4 %collective-permute-start.8 = (f32[8,8,256]{2,1,0:T(8,128)S(1)}, f32[8,8,256]{2,1,0:T(8,128)S(1)}, u32[]{:S(2)}, u32[]{:S(2)}) collective-permute-start(f32[8,8,256]{2,1,0:T(8,128)S(1)} %get-tuple-element.62), channel_id=1, source_target_pairs={{1,2},{2,1},{5,6},{6,5},{9,10},{10,9},{13,14},{14,13},{17,18},{18,... | collective-permute-start | bytes 196616 | tf_op jit(solution)/shard_map/ppermute | solution.py:551
  30.6 1.3 %collective-permute-start.7 = (f32[8,4,256]{2,1,0:T(4,128)S(1)}, f32[8,4,256]{2,1,0:T(4,128)S(1)}, u32[]{:S(2)}, u32[]{:S(2)}) collective-permute-start(f32[8,4,256]{2,1,0:T(4,128)S(1)} %get-tuple-element.61), channel_id=1, source_target_pairs={{0,1},{1,0},{2,3},{3,2},{4,5},{5,4},{6,7},{7,6},{8,9},{9,8},{10,11... | collective-permute-start | bytes 98312 | tf_op jit(solution)/shard_map/ppermute | solution.py:551
  30.6 2.6 %copy-start.8 = (bf16[2,32,16]{2,1,0:T(8,128)(2,1)S(1)}, bf16[2,32,16]{2,1,0:T(8,128)(2,1)}, u32[]{:S(2)}) copy-start(bf16[2,32,16]{2,1,0:T(8,128)(2,1)} %constant.8.clone.ye) | copy-start | bytes 6148

commit v5 on v4

--- a/solution.py
+++ b/solution.py
@@ -201,11 +201,7 @@
     return copies
 
 
-def first_kernel(
-    adj, mod, buoy, topo_in, fwd,
-    x1, x2, y1, y2, s0,
-    cur_v, mod_v, topo, buoy_v, fields_v, sem,
-):
+def first_kernel(adj, mod, buoy, topo_in, x1, x2, s0, cur_v, mod_v, topo, sem):
     width, height, depth = s0.shape
     parity = row_parity()
     first = pl.ds((1 - parity) * HALO, HALO)
@@ -215,8 +211,6 @@
             (topo_in, topo),
             (adj.at[0, 1, 0], cur_v),
             (mod.at[0], mod_v),
-            (buoy.at[0], buoy_v),
-            (fwd.at[0, pl.ds(1, 2), 0], fields_v),
             (buoy.at[0, first], x1.at[0]),
             (buoy.at[0, second], x2.at[0]),
         ],
@@ -231,22 +225,33 @@
         s0[i] = jnp.where(masks[i], mod_v[i] * cur_v[i], 0.0)
     x1[1] = s0[first]
     x2[1] = s0[second]
+    for c in copies[3:]:
+        c.wait()
+
+
+def edge_kernel(buoy, fwd, s0, y1, y2, low_v, high_v, sem):
+    width, height, depth = s0.shape
+    low, high = pl.ds(0, 8), pl.ds(height - 8, 8)
+    copies = copy_all(
+        [
+            (buoy.at[0, :, low], low_v.at[0]),
+            (buoy.at[0, :, high], high_v.at[0]),
+            (fwd.at[0, pl.ds(1, 2), 0, :, low], low_v.at[pl.ds(1, 2)]),
+            (fwd.at[0, pl.ds(1, 2), 0, :, high], high_v.at[pl.ds(1, 2)]),
+        ],
+        sem,
+    )
     even = column_parity() == 0
 
-    def pack(n, value):
-        low = value[:, :HALO]
-        high = value[:, height - HALO :]
+    def pack(n, low, high):
         y1[n] = jnp.where(even, high, low)
         y2[n] = jnp.where(even, low, high)
 
-    pack(1, s0)
-    copies[3].wait()
-    pack(0, buoy_v)
-    copies[4].wait()
-    pack(2, fields_v.at[0])
-    pack(3, fields_v.at[1])
-    for c in copies[5:]:
+    pack(1, s0[:, :HALO], s0[:, height - HALO :])
+    for c in copies:
         c.wait()
+    for n, m in ((0, 0), (2, 1), (3, 2)):
+        pack(n, low_v[m, :, :HALO], high_v[m, :, 8 - HALO :])
 
 
 def source_kernel(topo, rec, res, fwd, _, scale, source, x1, x2, sem):
@@ -465,13 +470,14 @@
         )
 
     even = column_parity() == 0
-    edges = []
-    for i in range(width):
+
+    def edge_of(i):
         second = jnp.where(even, ys2[i, 8 - HALO :], ys2[i, :HALO])
-        edges.append(dot(factor, edge_parts(ys1[i], second)))
+        return dot(factor, edge_parts(ys1[i], second))
 
     def body(low_ref, high_ref, low_fields, high_fields):
-        for t in range(tiles):
+        edges = [edge_of(i) for i in range(width)]
+        for t in list(range(1, tiles - 1)) + [0, tiles - 1]:
             rows = pl.ds(8 * t, 8)
             low = [low_ref[i, rows] for i in range(HALO)]
             high = [high_ref[i, rows] for i in range(HALO)]
@@ -552,15 +558,21 @@
 
     ahead = (2, HALO, height, depth)
     edge = (4, width, HALO, depth)
-    xa1, xa2, ya1, ya2, s0 = call(
+    xa1, xa2, s0 = call(
         first_kernel,
-        "scaled_and_edges",
-        [(adjoint_in, False), (modulus, False), (buoyancy, False), (topography, False), (forward, False)],
-        [(ahead, True)] * 2 + [(edge, True)] * 2 + [(block, True)],
-        [VMEM(block, F32), VMEM(block, F32), VMEM(topography.shape, jnp.int32), VMEM(block, F32),
-         VMEM((2,) + block, F32), dma((7,))],
+        "scaled_and_planes",
+        [(adjoint_in, False), (modulus, False), (buoyancy, False), (topography, False)],
+        [(ahead, True)] * 2 + [(block, True)],
+        [VMEM(block, F32), VMEM(block, F32), VMEM(topography.shape, jnp.int32), dma((5,))],
     )
     xa1, xa2 = swap(xa1, rows1), swap(xa2, rows2)
+    ya1, ya2 = call(
+        edge_kernel,
+        "edges",
+        [(buoyancy, False), (forward, False), (s0, True)],
+        [(edge, True)] * 2,
+        [VMEM((3, width, 8, depth), F32), VMEM((3, width, 8, depth), F32), dma((4,))],
+    )
     ya1, ya2 = swap(ya1, cols1), swap(ya2, cols2)
     z_out = (width, height, 2 * depth)
     y_out = (width, 2 * height, depth)

time: 34.6 us -> 34.4 us (level)
  waiting for transfers between devices: 11.2 us -> 6.04 us
  starting transfers between devices: 16.2 us -> 20.3 us
  Pallas kernels: 6 us -> 6.87 us
    ppermute x10, waiting for transfers between devices: 11.2 us -> 6.04 us  [swap(): return lax.ppermute(value, 'blk', pairs)]
    ppermute x10, starting transfers between devices: 16.2 us -> 20.3 us  [swap(): return lax.ppermute(value, 'blk', pairs)]
    pallas_call x6 -> x7, Pallas kernels: 6 us -> 6.87 us  [call(): pl.pallas_call(kernel, name=name, in_specs=in_specs, out_specs=out_specs,...]
  transfers between devices with their start and end apart: 10 -> 10, of which waited for: 4 -> 3; matrix products, arithmetic and copies ran while one was open for 0% -> 0% of each run, Pallas kernels for 10% -> 14%
where the time goes in v5:
time: 34.4 us; the launch traced here: 34.1 us
  starting transfers between devices  20.3 us (59%)
  Pallas kernels  6.87 us (20%)
  waiting for transfers between devices  6.04 us (18%)
  between operations  0.84 us (2%)
    ppermute x10, starting transfers between devices, swap(): return lax.ppermute(value, 'blk', pairs)  20.3 us
    pallas_call x7, Pallas kernels, call(): pl.pallas_call(kernel, name=name, in_specs=in_specs, out_specs=out_specs,...  6.87 us
    ppermute x10, waiting for transfers between devices, swap(): return lax.ppermute(value, 'blk', pairs)  6.04 us
  transfers between devices with their start and end apart: 10, of which 3 were waited for; matrix products, arithmetic and copies ran while one was open for 0% of the time, Pallas kernels for 14%

profile of v5, /device:TPU:0, one launch (start us, length us, event | category | flops | bytes accessed | tf_op | source)
XLA Modules:
  0.0 34.1 jit_solution(17093875819677909875)
XLA Ops:
  0.6 1.2 %scaled_and_planes.1 = (f32[2,4,32,256]{3,2,1,0:T(8,128)S(1)}, f32[2,4,32,256]{3,2,1,0:T(8,128)S(1)}, f32[8,32,256]{2,1,0:T(8,128)S(1)}) custom-call(f32[1,2,1,8,32,256]{5,4,3,2,1,0:T(8,128)} %adj.5, f32[1,8,32,256]{3,2,1,0:T(8,128)} %mod.3, f32[1,8,32,256]{3,2,1,0:T(8,128)} %buoy.5, s32[1,8,32]{2,1,0:T(8,128)} %topo.1), custom_call_target="tpu_custom_call" | custom-call | bytes 3000000 | tf_op jit(solution)/shard_map/scaled_and_planes/pallas_call | solution.py:530
  1.8 3.0 %collective-permute-start = (f32[2,4,32,256]{3,2,1,0:T(8,128)S(1)}, f32[2,4,32,256]{3,2,1,0:T(8,128)S(1)}, u32[]{:S(2)}, u32[]{:S(2)}) collective-permute-start(f32[2,4,32,256]{3,2,1,0:T(8,128)S(1)} %get-tuple-element.38), channel_id=1, source_target_pairs={{0,4},{1,5},{2,6},{3,7},{4,0},{5,1},{6,2},{7,3},{8,12},{9,13},{10,... | collective-permute-start | bytes 786440 | tf_op jit(solution)/shard_map/ppermute | solution.py:557
  4.8 0.7 %collective-permute-start.1 = (f32[2,4,32,256]{3,2,1,0:T(8,128)S(1)}, f32[2,4,32,256]{3,2,1,0:T(8,128)S(1)}, u32[]{:S(2)}, u32[]{:S(2)}) collective-permute-start(f32[2,4,32,256]{3,2,1,0:T(8,128)S(1)} %get-tuple-element.39), channel_id=1, source_target_pairs={{4,8},{5,9},{6,10},{7,11},{8,4},{9,5},{10,6},{11,7},{12,16},{13,17... | collective-permute-start | bytes 786440 | tf_op jit(solution)/shard_map/ppermute | solution.py:557
  5.5 0.0 copy-start.6
  5.5 0.0 copy-start.7
  5.5 1.1 %edges.1 = (f32[4,8,4,256]{3,2,1,0:T(4,128)S(1)}, f32[4,8,4,256]{3,2,1,0:T(4,128)S(1)}) custom-call(f32[1,8,32,256]{3,2,1,0:T(8,128)} %buoy.5, f32[1,4,1,8,32,256]{5,4,3,2,1,0:T(8,128)} %fwd.5, f32[8,32,256]{2,1,0:T(8,128)S(1)} %get-tuple-element.40.s0), custom_call_target="tpu_custom_call" | custom-call | bytes 3000000 | tf_op jit(solution)/shard_map/edges/pallas_call | solution.py:530
  6.7 0.0 copy-start.9
  6.7 0.1 collective-permute-start.2
  6.8 0.7 %collective-permute-start.3 = (f32[4,8,4,256]{3,2,1,0:T(4,128)S(1)}, f32[4,8,4,256]{3,2,1,0:T(4,128)S(1)}, u32[]{:S(2)}, u32[]{:S(2)}) collective-permute-start(f32[4,8,4,256]{3,2,1,0:T(4,128)S(1)} %get-tuple-element.42), channel_id=1, source_target_pairs={{1,2},{2,1},{5,6},{6,5},{9,10},{10,9},{13,14},{14,13},{17,18},{18,... | collective-permute-start | bytes 393224 | tf_op jit(solution)/shard_map/ppermute | solution.py:557
  7.4 0.7 %collective-permute-done.2._.y1.yf1 = f32[4,8,4,256]{3,2,1,0:T(4,128)S(1)} collective-permute-done((f32[4,8,4,256]{3,2,1,0:T(4,128)S(1)}, f32[4,8,4,256]{3,2,1,0:T(4,128)S(1)}, u32[]{:S(2)}, u32[]{:S(2)}) %collective-permute-start.2) | collective-permute-done | bytes 131104 | tf_op jit(solution)/shard_map/ppermute | solution.py:557
  8.1 0.0 copy-done.6
  8.1 0.0 copy-done.7
  8.1 0.0 copy-done.9
  8.1 0.0 copy-start.1
  8.1 0.0 copy-start.2
  8.1 0.0 copy-start.3
  8.1 0.0 copy-start.5
  8.1 1.1 %sources_and_planes.1 = (f32[8,32,256]{2,1,0:T(8,128)S(1)}, f32[2,8,32,256]{3,2,1,0:T(8,128)S(1)}, f32[2,4,32,256]{3,2,1,0:T(8,128)S(1)}, f32[2,4,32,256]{3,2,1,0:T(8,128)S(1)}) custom-call(s32[1,8,32]{2,1,0:T(8,128)S(1)} %copy-done.9, s32[2,4096]{1,0:T(2,128)S(1)} %bitcast.1, f32[1,2,4096]{2,1,0:T(2,128)S(1)} %copy-done.7, f32[1,4,1,8,32,256]{5,4,3,2,1,0:T(8,128)} %fwd.5, ...), custom_call_target="tpu_custom_call" | custom-call | bytes 3000000 | tf_op jit(solution)/shard_map/sources_and_planes/pallas_call | solution.py:530
  9.3 4.3 %collective-permute-start.4 = (f32[2,4,32,256]{3,2,1,0:T(8,128)S(1)}, f32[2,4,32,256]{3,2,1,0:T(8,128)S(1)}, u32[]{:S(2)}, u32[]{:S(2)}) collective-permute-start(f32[2,4,32,256]{3,2,1,0:T(8,128)S(1)} %get-tuple-element.57), channel_id=1, source_target_pairs={{0,4},{1,5},{2,6},{3,7},{4,0},{5,1},{6,2},{7,3},{8,12},{9,13},{10,... | collective-permute-start | bytes 786440 | tf_op jit(solution)/shard_map/ppermute | solution.py:557
  13.6 0.0 collective-permute-done.3.y2.yf2
  13.6 0.0 copy-done.1
  13.6 0.0 copy-done.2
  13.6 0.0 copy-done.3
  13.7 0.0 copy-done.5
  13.7 0.0 copy-start.4
  13.7 0.8 %step0_own.1 = (f32[8,32,256]{2,1,0:T(8,128)S(1)}, f32[8,32,256]{2,1,0:T(8,128)S(1)}, f32[8,32,256]{2,1,0:T(8,128)S(1)}, f32[8,32,256]{2,1,0:T(8,128)S(1)}, f32[...) custom-call(f32[1,2,1,8,32,256]{5,4,3,2,1,0:T(8,128)S(1)} %copy-done.1, ...), custom_call_target="tpu_custom_call" | custom-call | bytes 12000000 | tf_op jit(solution)/shard_map/step0_own/pallas_call | solution.py:530
  14.5 1.5 %collective-permute-done.xa1 = f32[2,4,32,256]{3,2,1,0:T(8,128)S(1)} collective-permute-done((f32[2,4,32,256]{3,2,1,0:T(8,128)S(1)}, f32[2,4,32,256]{3,2,1,0:T(8,128)S(1)}, u32[]{:S(2)}, u32[]{:S(2)}) %collective-permute-start) | collective-permute-done | bytes 262176 | tf_op jit(solution)/shard_map/ppermute | solution.py:557
  16.0 0.0 collective-permute-done.1.xa2
  16.0 0.0 copy-done.4
  16.0 0.0 copy-start
  16.0 0.2 step0_planes.1
  16.3 0.8 %collective-permute-start.9 = (f32[2,4,32,256]{3,2,1,0:T(8,128)S(1)}, f32[2,4,32,256]{3,2,1,0:T(8,128)S(1)}, u32[]{:S(2)}, u32[]{:S(2)}) collective-permute-start(f32[2,4,32,256]{3,2,1,0:T(8,128)S(1)} %get-tuple-element.69), channel_id=1, source_target_pairs={{4,8},{5,9},{6,10},{7,11},{8,4},{9,5},{10,6},{11,7},{12,16},{13,17... | collective-permute-start | bytes 786440 | tf_op jit(solution)/shard_map/ppermute | solution.py:557
  17.1 5.5 %collective-permute-start.5 = (f32[4,32,256]{2,1,0:T(8,128)S(1)}, f32[4,32,256]{2,1,0:T(8,128)S(1)}, u32[]{:S(2)}, u32[]{:S(2)}) collective-permute-start(f32[4,32,256]{2,1,0:T(8,128)S(1)} %get-tuple-element.59), channel_id=1, source_target_pairs={{0,4},{1,5},{2,6},{3,7},{4,0},{5,1},{6,2},{7,3},{8,12},{9,13},{10,... | collective-permute-start | bytes 393224 | tf_op jit(solution)/shard_map/ppermute | solution.py:557
  22.6 0.7 %collective-permute-start.6 = (f32[4,32,256]{2,1,0:T(8,128)S(1)}, f32[4,32,256]{2,1,0:T(8,128)S(1)}, u32[]{:S(2)}, u32[]{:S(2)}) collective-permute-start(f32[4,32,256]{2,1,0:T(8,128)S(1)} %get-tuple-element.60), channel_id=1, source_target_pairs={{4,8},{5,9},{6,10},{7,11},{8,4},{9,5},{10,6},{11,7},{12,16},{13,17... | collective-permute-start | bytes 393224 | tf_op jit(solution)/shard_map/ppermute | solution.py:557
  23.3 0.7 %collective-permute-start.8 = (f32[8,8,256]{2,1,0:T(8,128)S(1)}, f32[8,8,256]{2,1,0:T(8,128)S(1)}, u32[]{:S(2)}, u32[]{:S(2)}) collective-permute-start(f32[8,8,256]{2,1,0:T(8,128)S(1)} %get-tuple-element.62), channel_id=1, source_target_pairs={{1,2},{2,1},{5,6},{6,5},{9,10},{10,9},{13,14},{14,13},{17,18},{18,... | collective-permute-start | bytes 196616 | tf_op jit(solution)/shard_map/ppermute | solution.py:557
  24.0 0.0 collective-permute-done.4.xf
  24.0 3.9 %collective-permute-start.7 = (f32[8,4,256]{2,1,0:T(4,128)S(1)}, f32[8,4,256]{2,1,0:T(4,128)S(1)}, u32[]{:S(2)}, u32[]{:S(2)}) collective-permute-start(f32[8,4,256]{2,1,0:T(4,128)S(1)} %get-tuple-element.61), channel_id=1, source_target_pairs={{0,1},{1,0},{2,3},{3,2},{4,5},{5,4},{6,7},{7,6},{8,9},{9,8},{10,11... | collective-permute-start | bytes 98312 | tf_op jit(solution)/shard_map/ppermute | solution.py:557
  27.8 0.0 copy-done
  27.8 0.0 copy-start.8
  27.8 1.3 %images_and_step1_own.1 = (f32[8,32,256]{2,1,0:T(8,128)S(1)}, f32[8,32,256]{2,1,0:T(8,128)S(1)}, f32[8,32,256]{2,1,0:T(8,128)S(1)}, f32[8,32,256]{2,1,0:T(8,128)...) custom-call(f32[1,2,1,8,32,256]{5,4,3,2,1,0:T(8,128)S(1)} %copy-done.1, ...), custom_call_target="tpu_custom_call" | custom-call | bytes 60000000 | tf_op jit(solution)/shard_map/images_and_step1_own/pallas_call | solution.py:530
  29.1 0.0 collective-permute-done.7.ys1
  29.2 0.0 collective-permute-done.8.ys2
  29.2 3.9 %collective-permute-done.5.xs1 = f32[4,32,256]{2,1,0:T(8,128)S(1)} collective-permute-done((f32[4,32,256]{2,1,0:T(8,128)S(1)}, f32[4,32,256]{2,1,0:T(8,128)S(1)}, u32[]{:S(2)}, u32[]{:S(2)}) %collective-permute-start.5) | collective-permute-done | bytes 131104 | tf_op jit(solution)/shard_map/ppermute | solution.py:557
  33.0 0.0 collective-permute-done.6.xs2
  33.0 0.0 collective-permute-done.9.xf2
  33.0 0.0 copy-done.8
  33.0 1.1 %step1_planes.1 = (f32[1,8,32,256]{3,2,1,0:T(8,128)}, f32[1,2,1,8,32,256]{5,4,3,2,1,0:T(8,128)}) custom-call(f32[4,32,256]{2,1,0:T(8,128)S(1)} %collective-permute-done.5.xs1, f32[4,32,256]{2,1,0:T(8,128)S(1)} %collective-permute-done.6.xs2, f32[8,4,256]{2,1,0:T(4,128)S(1)} %collective-permute-done.7.ys1, ...), custom_call_target="tpu_custom_call", output_to_operand_aliasing={{1}: (15, {})} | custom-call | bytes 3000000 | tf_op jit(solution)/shard_map/step1_planes/pallas_call | solution.py:530
Async XLA Ops:
  1.8 14.2 %collective-permute-start = (f32[2,4,32,256]{3,2,1,0:T(8,128)S(1)}, f32[2,4,32,256]{3,2,1,0:T(8,128)S(1)}, u32[]{:S(2)}, u32[]{:S(2)}) collective-permute-start(f32[2,4,32,256]{3,2,1,0:T(8,128)S(1)} %get-tuple-element.38), channel_id=1, source_target_pairs={{0,4},{1,5},{2,6},{3,7},{4,0},{5,1},{6,2},{7,3},{8,12},{9,13},{10,... | collective-permute-start | bytes 786440 | tf_op jit(solution)/shard_map/ppermute | solution.py:557
  4.8 11.2 %collective-permute-start.1 = (f32[2,4,32,256]{3,2,1,0:T(8,128)S(1)}, f32[2,4,32,256]{3,2,1,0:T(8,128)S(1)}, u32[]{:S(2)}, u32[]{:S(2)}) collective-permute-start(f32[2,4,32,256]{3,2,1,0:T(8,128)S(1)} %get-tuple-element.39), channel_id=1, source_target_pairs={{4,8},{5,9},{6,10},{7,11},{8,4},{9,5},{10,6},{11,7},{12,16},{13,17... | collective-permute-start | bytes 786440 | tf_op jit(solution)/shard_map/ppermute | solution.py:557
  5.5 2.6 %copy-start.6 = (s32[4096,2]{0,1:T(2,128)S(1)}, s32[4096,2]{0,1:T(2,128)}, u32[]{:S(2)}) copy-start(s32[4096,2]{0,1:T(2,128)} %param.15) | copy-start | bytes 98308
  5.5 2.6 %copy-start.7 = (f32[1,2,4096]{2,1,0:T(2,128)S(1)}, f32[1,2,4096]{2,1,0:T(2,128)}, u32[]{:S(2)}) copy-start(f32[1,2,4096]{2,1,0:T(2,128)} %res.1) | copy-start | bytes 98308
  6.7 1.4 %copy-start.9 = (s32[1,8,32]{2,1,0:T(8,128)S(1)}, s32[1,8,32]{2,1,0:T(8,128)}, u32[]{:S(2)}) copy-start(s32[1,8,32]{2,1,0:T(8,128)} %topo.1) | copy-start | bytes 3076
  6.7 1.4 %collective-permute-start.2 = (f32[4,8,4,256]{3,2,1,0:T(4,128)S(1)}, f32[4,8,4,256]{3,2,1,0:T(4,128)S(1)}, u32[]{:S(2)}, u32[]{:S(2)}) collective-permute-start(f32[4,8,4,256]{3,2,1,0:T(4,128)S(1)} %get-tuple-element.41), channel_id=1, source_target_pairs={{0,1},{1,0},{2,3},{3,2},{4,5},{5,4},{6,7},{7,6},{8,9},{9,8},{10,11... | collective-permute-start | bytes 393224 | tf_op jit(solution)/shard_map/ppermute | solution.py:557
  6.8 6.9 %collective-permute-start.3 = (f32[4,8,4,256]{3,2,1,0:T(4,128)S(1)}, f32[4,8,4,256]{3,2,1,0:T(4,128)S(1)}, u32[]{:S(2)}, u32[]{:S(2)}) collective-permute-start(f32[4,8,4,256]{3,2,1,0:T(4,128)S(1)} %get-tuple-element.42), channel_id=1, source_target_pairs={{1,2},{2,1},{5,6},{6,5},{9,10},{10,9},{13,14},{14,13},{17,18},{18,... | collective-permute-start | bytes 393224 | tf_op jit(solution)/shard_map/ppermute | solution.py:557
  8.1 5.5 %copy-start.1 = (f32[1,2,1,8,32,256]{5,4,3,2,1,0:T(8,128)S(1)}, f32[1,2,1,8,32,256]{5,4,3,2,1,0:T(8,128)}, u32[]{:S(2)}) copy-start(f32[1,2,1,8,32,256]{5,4,3,2,1,0:T(8,128)} %adj.5) | copy-start | bytes 1572868
  8.1 5.5 %copy-start.2 = (f32[1,8,32,256]{3,2,1,0:T(8,128)S(1)}, f32[1,8,32,256]{3,2,1,0:T(8,128)}, u32[]{:S(2)}) copy-start(f32[1,8,32,256]{3,2,1,0:T(8,128)} %buoy.5) | copy-start | bytes 786436
  8.1 5.5 %copy-start.3 = (bf16[256,512]{1,0:T(8,128)(2,1)S(1)}, bf16[256,512]{1,0:T(8,128)(2,1)}, u32[]{:S(2)}) copy-start(bf16[256,512]{1,0:T(8,128)(2,1)} %constant.6.clone.zf) | copy-start | bytes 786436
  8.1 5.5 %copy-start.5 = (bf16[2,64,80]{2,1,0:T(8,128)(2,1)S(1)}, bf16[2,64,80]{2,1,0:T(8,128)(2,1)}, u32[]{:S(2)}) copy-start(bf16[2,64,80]{2,1,0:T(8,128)(2,1)} %constant.7.clone.yf) | copy-start | bytes 61444
  9.3 14.7 %collective-permute-start.4 = (f32[2,4,32,256]{3,2,1,0:T(8,128)S(1)}, f32[2,4,32,256]{3,2,1,0:T(8,128)S(1)}, u32[]{:S(2)}, u32[]{:S(2)}) collective-permute-start(f32[2,4,32,256]{3,2,1,0:T(8,128)S(1)} %get-tuple-element.57), channel_id=1, source_target_pairs={{0,4},{1,5},{2,6},{3,7},{4,0},{5,1},{6,2},{7,3},{8,12},{9,13},{10,... | collective-permute-start | bytes 786440 | tf_op jit(solution)/shard_map/ppermute | solution.py:557
  13.7 2.4 %copy-start.4 = (f32[1,8,32,256]{3,2,1,0:T(8,128)S(1)}, f32[1,8,32,256]{3,2,1,0:T(8,128)}, u32[]{:S(2)}) copy-start(f32[1,8,32,256]{3,2,1,0:T(8,128)} %mod.3) | copy-start | bytes 786436
  16.0 11.8 %copy-start = (f32[1,4,1,8,32,256]{5,4,3,2,1,0:T(8,128)S(1)}, f32[1,4,1,8,32,256]{5,4,3,2,1,0:T(8,128)}, u32[]{:S(2)}) copy-start(f32[1,4,1,8,32,256]{5,4,3,2,1,0:T(8,128)} %fwd.5) | copy-start | bytes 3145732
  16.3 16.8 %collective-permute-start.9 = (f32[2,4,32,256]{3,2,1,0:T(8,128)S(1)}, f32[2,4,32,256]{3,2,1,0:T(8,128)S(1)}, u32[]{:S(2)}, u32[]{:S(2)}) collective-permute-start(f32[2,4,32,256]{3,2,1,0:T(8,128)S(1)} %get-tuple-element.69), channel_id=1, source_target_pairs={{4,8},{5,9},{6,10},{7,11},{8,4},{9,5},{10,6},{11,7},{12,16},{13,17... | collective-permute-start | bytes 786440 | tf_op jit(solution)/shard_map/ppermute | solution.py:557
  17.1 15.9 %collective-permute-start.5 = (f32[4,32,256]{2,1,0:T(8,128)S(1)}, f32[4,32,256]{2,1,0:T(8,128)S(1)}, u32[]{:S(2)}, u32[]{:S(2)}) collective-permute-start(f32[4,32,256]{2,1,0:T(8,128)S(1)} %get-tuple-element.59), channel_id=1, source_target_pairs={{0,4},{1,5},{2,6},{3,7},{4,0},{5,1},{6,2},{7,3},{8,12},{9,13},{10,... | collective-permute-start | bytes 393224 | tf_op jit(solution)/shard_map/ppermute | solution.py:557
  22.6 10.4 %collective-permute-start.6 = (f32[4,32,256]{2,1,0:T(8,128)S(1)}, f32[4,32,256]{2,1,0:T(8,128)S(1)}, u32[]{:S(2)}, u32[]{:S(2)}) collective-permute-start(f32[4,32,256]{2,1,0:T(8,128)S(1)} %get-tuple-element.60), channel_id=1, source_target_pairs={{4,8},{5,9},{6,10},{7,11},{8,4},{9,5},{10,6},{11,7},{12,16},{13,17... | collective-permute-start | bytes 393224 | tf_op jit(solution)/shard_map/ppermute | solution.py:557
  23.3 5.9 %collective-permute-start.8 = (f32[8,8,256]{2,1,0:T(8,128)S(1)}, f32[8,8,256]{2,1,0:T(8,128)S(1)}, u32[]{:S(2)}, u32[]{:S(2)}) collective-permute-start(f32[8,8,256]{2,1,0:T(8,128)S(1)} %get-tuple-element.62), channel_id=1, source_target_pairs={{1,2},{2,1},{5,6},{6,5},{9,10},{10,9},{13,14},{14,13},{17,18},{18,... | collective-permute-start | bytes 196616 | tf_op jit(solution)/shard_map/ppermute | solution.py:557
  24.0 5.2 %collective-permute-start.7 = (f32[8,4,256]{2,1,0:T(4,128)S(1)}, f32[8,4,256]{2,1,0:T(4,128)S(1)}, u32[]{:S(2)}, u32[]{:S(2)}) collective-permute-start(f32[8,4,256]{2,1,0:T(4,128)S(1)} %get-tuple-element.61), channel_id=1, source_target_pairs={{0,1},{1,0},{2,3},{3,2},{4,5},{5,4},{6,7},{7,6},{8,9},{9,8},{10,11... | collective-permute-start | bytes 98312 | tf_op jit(solution)/shard_map/ppermute | solution.py:557
  27.8 5.2 %copy-start.8 = (bf16[2,32,16]{2,1,0:T(8,128)(2,1)S(1)}, bf16[2,32,16]{2,1,0:T(8,128)(2,1)}, u32[]{:S(2)}) copy-start(bf16[2,32,16]{2,1,0:T(8,128)(2,1)} %constant.8.clone.ye) | copy-start | bytes 6148

commit v6 on v5

--- a/solution.py
+++ b/solution.py
@@ -182,8 +182,12 @@
     return jnp.sum(picked, axis=1, keepdims=True).astype(jnp.int32)
 
 
-def planes(ref, n, rows):
-    return None if ref is None else [ref[n, i, rows] for i in range(HALO)]
+def four(ref, rows):
+    return None if ref is None else [ref[i, rows] for i in range(HALO)]
+
+
+def two_and_two(first, second, rows):
+    return [ref[HALO + i, rows] for ref in (first, second) for i in range(2)]
 
 
 def row_parity():
@@ -254,16 +258,17 @@
         pack(n, low_v[m, :, :HALO], high_v[m, :, 8 - HALO :])
 
 
-def source_kernel(topo, rec, res, fwd, _, scale, source, x1, x2, sem):
+def source_kernel(topo, rec, res, fwd, _, scale, source, x1, x2, s1, s2, sem):
     width, height, depth = scale.shape
     parity = row_parity()
-    copies = copy_all(
-        [
-            (fwd.at[0, pl.ds(1, 2), 0, pl.ds((1 - parity) * HALO, HALO)], x1),
-            (fwd.at[0, pl.ds(1, 2), 0, pl.ds(parity * HALO, HALO)], x2),
-        ],
-        sem,
-    )
+    pairs = []
+    for out, rest, at in ((x1, s1, (1 - parity) * HALO), (x2, s2, parity * HALO)):
+        pairs += [
+            (fwd.at[0, 1, 0, pl.ds(at, HALO)], out.at[pl.ds(0, HALO)]),
+            (fwd.at[0, 2, 0, pl.ds(at, 2)], out.at[pl.ds(HALO, 2)]),
+            (fwd.at[0, 2, 0, pl.ds(at + 2, 2)], rest.at[pl.ds(HALO, 2)]),
+        ]
+    copies = copy_all(pairs, sem)
     index = lax.axis_index("blk")
     anchor_x = index // YBLOCKS * width
     anchor_y = lax.rem(index, YBLOCKS) * height
@@ -338,7 +343,7 @@
 
 
 def finish_kernel(
-    xa1, xa2, rest, sx_own, gx_own, weight, scale, mod, _,
+    xa1, xa2, rest, sx_own, gx_own, weight, scale, mod, _f2, _x1, _x2,
     e0, s1, sx, gx, x1, x2, y1, y2, f2,
 ):
     width, height, depth = e0.shape
@@ -414,8 +419,7 @@
             own2 = [fwd[0, 2, 0, i, rows] for i in range(width)]
             slope1 = x_slope(own1)
             slope2 = x_slope(own2)
-            low1, low2 = planes(low_ref, 0, rows), planes(low_ref, 1, rows)
-            high1, high2 = planes(high_ref, 0, rows), planes(high_ref, 1, rows)
+            low1, high1 = four(low_ref, rows), four(high_ref, rows)
             for i in range(width):
                 now, before = adj[0, 1, 0, i, rows], e0[i, rows]
                 s_y = C_UNIT * ys[i, rows]
@@ -429,7 +433,7 @@
                 )
                 sx_own[i, rows] = slope[i]
                 f1x = plus(slope1[i], edge_slope(i, width, low1, high1))
-                fx[i, rows] = plus(slope2[i], edge_slope(i, width, low2, high2))
+                fx[i, rows] = slope2[i]
                 image[i, rows] = (
                     f1x * sx0[i, rows]
                     + C_UNIT
@@ -454,7 +458,7 @@
 
 
 def last_kernel(
-    xs1, xs2, ys1, ys2, rest, sx_own, image, fx, fy, gx, gy, weight, ye, sx0, xf2, states_in,
+    xs1, xs2, ys1, ys2, rest, sx_own, image, fx, fy, gx, gy, weight, ye, sx0, xf1, xf2, states_in,
     image_out, states_out,
     image_v, e1_v, sem,
 ):
@@ -475,14 +479,15 @@
         second = jnp.where(even, ys2[i, 8 - HALO :], ys2[i, :HALO])
         return dot(factor, edge_parts(ys1[i], second))
 
-    def body(low_ref, high_ref, low_fields, high_fields):
+    def body(low_ref, high_ref, low_fields, high_fields, low_one, high_one):
         edges = [edge_of(i) for i in range(width)]
         for t in list(range(1, tiles - 1)) + [0, tiles - 1]:
             rows = pl.ds(8 * t, 8)
             low = [low_ref[i, rows] for i in range(HALO)]
             high = [high_ref[i, rows] for i in range(HALO)]
-            low1, low2 = planes(low_fields, 0, rows), planes(low_fields, 1, rows)
-            high1, high2 = planes(high_fields, 0, rows), planes(high_fields, 1, rows)
+            low1, high1 = four(low_one, rows), four(high_one, rows)
+            low2 = two_and_two(low_fields, low_ref, rows)
+            high2 = two_and_two(high_fields, high_ref, rows)
             for i in range(width):
                 s_x = sx_own[i, rows] + edge_slope(i, width, low, high)
                 lap = edge_laplace(i, width, low, high)
@@ -505,11 +510,11 @@
 
     @pl.when(row_parity() == 0)
     def _():
-        body(xs2, xs1, xf2, None)
+        body(xs2, xs1, xf2, xf1, xf2, None)
 
     @pl.when(row_parity() == 1)
     def _():
-        body(xs1, xs2, None, xf2)
+        body(xs1, xs2, xf1, xf2, None, xf2)
 
     for t in range(tiles):
         for c in leave(t):
@@ -557,6 +562,7 @@
         return lax.ppermute(value, "blk", pairs)
 
     ahead = (2, HALO, height, depth)
+    six = (HALO + 2, height, depth)
     edge = (4, width, HALO, depth)
     xa1, xa2, s0 = call(
         first_kernel,
@@ -576,12 +582,12 @@
     ya1, ya2 = swap(ya1, cols1), swap(ya2, cols2)
     z_out = (width, height, 2 * depth)
     y_out = (width, 2 * height, depth)
-    scale, source, xf1, xf2 = call(
+    scale, source, xf1, xf2, xs1, xs2 = call(
         source_kernel,
         "sources_and_planes",
         [(topography, True), (receivers.T, True), (residuals, True), (forward, False), (ya1, True)],
-        [(block, True), ((STEPS,) + block, True), (ahead, True), (ahead, True)],
-        [dma((2,))],
+        [(block, True), ((STEPS,) + block, True)] + [(six, True)] * 4,
+        [dma((6,))],
     )
     xf1 = swap(xf1, rows1)
     rest, sx_own, sy, sz, gx_own, gy, gz, weight = call(
@@ -593,18 +599,17 @@
         [VMEM(z_out, F32), VMEM(block, F32), VMEM(y_out, F32), VMEM(block, F32)],
         us=4.0,
     )
-    half = (HALO, height, depth)
     side = (width, HALO, depth)
     rows8 = (width, 8, depth)
     e0, s1, sx, gx, xs1, xs2, ys1, ys2, xf2 = call(
         finish_kernel,
         "step0_planes",
         [(xa1, True), (xa2, True), (rest, True), (sx_own, True), (gx_own, True), (weight, True), (scale, True),
-         (modulus, True), (xf2, True)],
-        [(block, True)] * 4 + [(half, True)] * 2 + [(side, True), (rows8, True)] + [(ahead, True)],
-        aliases={8: 8},
-    )
-    xf2, xs1, xs2 = swap(xf2, rows2), swap(xs1, rows1), swap(xs2, rows2)
+         (modulus, True), (xf2, True), (xs1, True), (xs2, True)],
+        [(block, True)] * 4 + [(six, True)] * 2 + [(side, True), (rows8, True), (six, True)],
+        aliases={8: 8, 9: 4, 10: 5},
+    )
+    xs1, xf2, xs2 = swap(xs1, rows1), swap(xf2, rows2), swap(xs2, rows2)
     ys1, ys2 = swap(ys1, cols1), swap(ys2, cols2)
     rest, sx_own, image, fx, fy, image_mod, states = call(
         middle_kernel,
@@ -620,10 +625,10 @@
         last_kernel,
         "step1_planes",
         [(xs1, True), (xs2, True), (ys1, True), (ys2, True), (rest, True), (sx_own, True), (image, True), (fx, True),
-         (fy, True), (gx, True), (gy, True), (weight, True), (ye, True), (sx, True), (xf2, True), (states, False)],
+         (fy, True), (gx, True), (gy, True), (weight, True), (ye, True), (sx, True), (xf1, True), (xf2, True), (states, False)],
         [((1,) + block, False), ((1, STEPS, 1) + block, False)],
         [VMEM(block, F32), VMEM(block, F32), dma((2 * (height // 8),))],
-        aliases={15: 1},
+        aliases={16: 1},
     )
     if lax.axis_size("shot") > 1:
         image_mod, image_buo = lax.psum((image_mod, image_buo), "shot")

time: 34.4 us -> 34 us (0.988)
  starting transfers between devices: 20.3 us -> 17.4 us
  waiting for transfers between devices: 6.04 us -> 8.14 us
  Pallas kernels: 6.87 us -> 7.28 us
    ppermute x10, starting transfers between devices: 20.3 us -> 17.4 us  [swap(): return lax.ppermute(value, 'blk', pairs)]
    ppermute x10, waiting for transfers between devices: 6.04 us -> 8.14 us  [swap(): return lax.ppermute(value, 'blk', pairs)]
    pallas_call x7, Pallas kernels: 6.87 us -> 7.28 us  [call(): pl.pallas_call(kernel, name=name, in_specs=in_specs, out_specs=out_specs,...]
  transfers between devices with their start and end apart: 10 -> 10, of which waited for: 3 -> 3; matrix products, arithmetic and copies ran while one was open for 0% -> 0% of each run, Pallas kernels for 14% -> 15%
where the time goes in v6:
time: 34 us; the launch traced here: 33.7 us
  starting transfers between devices  17.4 us (51%)
  waiting for transfers between devices  8.14 us (24%)
  Pallas kernels  7.28 us (21%)
  between operations  0.84 us (2%)
    ppermute x10, starting transfers between devices, swap(): return lax.ppermute(value, 'blk', pairs)  17.4 us
    ppermute x10, waiting for transfers between devices, swap(): return lax.ppermute(value, 'blk', pairs)  8.14 us
    pallas_call x7, Pallas kernels, call(): pl.pallas_call(kernel, name=name, in_specs=in_specs, out_specs=out_specs,...  7.28 us
  transfers between devices with their start and end apart: 10, of which 3 were waited for; matrix products, arithmetic and copies ran while one was open for 0% of the time, Pallas kernels for 15%

profile of v6, /device:TPU:0, one launch (start us, length us, event | category | flops | bytes accessed | tf_op | source)
XLA Modules:
  0.0 33.7 jit_solution(17563780213505875159)
XLA Ops:
  0.6 1.2 %scaled_and_planes.1 = (f32[2,4,32,256]{3,2,1,0:T(8,128)S(1)}, f32[2,4,32,256]{3,2,1,0:T(8,128)S(1)}, f32[8,32,256]{2,1,0:T(8,128)S(1)}) custom-call(f32[1,2,1,8,32,256]{5,4,3,2,1,0:T(8,128)} %adj.5, f32[1,8,32,256]{3,2,1,0:T(8,128)} %mod.3, f32[1,8,32,256]{3,2,1,0:T(8,128)} %buoy.5, s32[1,8,32]{2,1,0:T(8,128)} %topo.1), custom_call_target="tpu_custom_call" | custom-call | bytes 3000000 | tf_op jit(solution)/shard_map/scaled_and_planes/pallas_call | solution.py:535
  1.8 3.0 %collective-permute-start = (f32[2,4,32,256]{3,2,1,0:T(8,128)S(1)}, f32[2,4,32,256]{3,2,1,0:T(8,128)S(1)}, u32[]{:S(2)}, u32[]{:S(2)}) collective-permute-start(f32[2,4,32,256]{3,2,1,0:T(8,128)S(1)} %get-tuple-element.40), channel_id=1, source_target_pairs={{0,4},{1,5},{2,6},{3,7},{4,0},{5,1},{6,2},{7,3},{8,12},{9,13},{10,... | collective-permute-start | bytes 786440 | tf_op jit(solution)/shard_map/ppermute | solution.py:562
  4.8 0.7 %collective-permute-start.1 = (f32[2,4,32,256]{3,2,1,0:T(8,128)S(1)}, f32[2,4,32,256]{3,2,1,0:T(8,128)S(1)}, u32[]{:S(2)}, u32[]{:S(2)}) collective-permute-start(f32[2,4,32,256]{3,2,1,0:T(8,128)S(1)} %get-tuple-element.41), channel_id=1, source_target_pairs={{4,8},{5,9},{6,10},{7,11},{8,4},{9,5},{10,6},{11,7},{12,16},{13,17... | collective-permute-start | bytes 786440 | tf_op jit(solution)/shard_map/ppermute | solution.py:562
  5.5 0.0 copy-start.6
  5.5 0.0 copy-start.7
  5.5 1.1 %edges.1 = (f32[4,8,4,256]{3,2,1,0:T(4,128)S(1)}, f32[4,8,4,256]{3,2,1,0:T(4,128)S(1)}) custom-call(f32[1,8,32,256]{3,2,1,0:T(8,128)} %buoy.5, f32[1,4,1,8,32,256]{5,4,3,2,1,0:T(8,128)} %fwd.5, f32[8,32,256]{2,1,0:T(8,128)S(1)} %get-tuple-element.42.s0), custom_call_target="tpu_custom_call" | custom-call | bytes 3000000 | tf_op jit(solution)/shard_map/edges/pallas_call | solution.py:535
  6.7 0.0 copy-start.8
  6.7 0.1 collective-permute-start.2
  6.8 0.7 %collective-permute-start.3 = (f32[4,8,4,256]{3,2,1,0:T(4,128)S(1)}, f32[4,8,4,256]{3,2,1,0:T(4,128)S(1)}, u32[]{:S(2)}, u32[]{:S(2)}) collective-permute-start(f32[4,8,4,256]{3,2,1,0:T(4,128)S(1)} %get-tuple-element.44), channel_id=1, source_target_pairs={{1,2},{2,1},{5,6},{6,5},{9,10},{10,9},{13,14},{14,13},{17,18},{18,... | collective-permute-start | bytes 393224 | tf_op jit(solution)/shard_map/ppermute | solution.py:562
  7.4 0.7 %collective-permute-done.2._.y1.yf1 = f32[4,8,4,256]{3,2,1,0:T(4,128)S(1)} collective-permute-done((f32[4,8,4,256]{3,2,1,0:T(4,128)S(1)}, f32[4,8,4,256]{3,2,1,0:T(4,128)S(1)}, u32[]{:S(2)}, u32[]{:S(2)}) %collective-permute-start.2) | collective-permute-done | bytes 131104 | tf_op jit(solution)/shard_map/ppermute | solution.py:562
  8.1 0.0 copy-done.6
  8.1 0.0 copy-done.7
  8.1 0.0 copy-done.8
  8.1 0.0 copy-start.1
  8.1 0.0 copy-start.2
  8.1 0.0 copy-start.3
  8.1 0.0 copy-start.5
  8.1 1.6 %sources_and_planes.1 = (f32[8,32,256]{2,1,0:T(8,128)S(1)}, f32[2,8,32,256]{3,2,1,0:T(8,128)S(1)}, f32[6,32,256]{2,1,0:T(8,128)S(1)}, f32[6,32,256]{2,1,0:T(8,12...) custom-call(s32[1,8,32]{2,1,0:T(8,128)S(1)} %copy-done.8, s32[2,4096]{1,0:T(2,128)S(1)} %bitcast.1, ...), custom_call_target="tpu_custom_call" | custom-call | bytes 3000000 | tf_op jit(solution)/shard_map/sources_and_planes/pallas_call | solution.py:535
  9.7 4.3 %collective-permute-start.4 = (f32[6,32,256]{2,1,0:T(8,128)S(1)}, f32[6,32,256]{2,1,0:T(8,128)S(1)}, u32[]{:S(2)}, u32[]{:S(2)}) collective-permute-start(f32[6,32,256]{2,1,0:T(8,128)S(1)} %get-tuple-element.61), channel_id=1, source_target_pairs={{0,4},{1,5},{2,6},{3,7},{4,0},{5,1},{6,2},{7,3},{8,12},{9,13},{10,... | collective-permute-start | bytes 589832 | tf_op jit(solution)/shard_map/ppermute | solution.py:562
  14.1 0.0 collective-permute-done.3.y2.yf2
  14.1 0.0 copy-done.1
  14.1 0.0 copy-done.2
  14.1 0.0 copy-done.3
  14.1 0.0 copy-done.5
  14.1 0.0 copy-start.4
  14.1 0.8 %step0_own.1 = (f32[8,32,256]{2,1,0:T(8,128)S(1)}, f32[8,32,256]{2,1,0:T(8,128)S(1)}, f32[8,32,256]{2,1,0:T(8,128)S(1)}, f32[8,32,256]{2,1,0:T(8,128)S(1)}, f32[...) custom-call(f32[1,2,1,8,32,256]{5,4,3,2,1,0:T(8,128)S(1)} %copy-done.1, ...), custom_call_target="tpu_custom_call" | custom-call | bytes 12000000 | tf_op jit(solution)/shard_map/step0_own/pallas_call | solution.py:535
  14.9 1.1 %collective-permute-done.xa1 = f32[2,4,32,256]{3,2,1,0:T(8,128)S(1)} collective-permute-done((f32[2,4,32,256]{3,2,1,0:T(8,128)S(1)}, f32[2,4,32,256]{3,2,1,0:T(8,128)S(1)}, u32[]{:S(2)}, u32[]{:S(2)}) %collective-permute-start) | collective-permute-done | bytes 262176 | tf_op jit(solution)/shard_map/ppermute | solution.py:562
  16.0 0.0 collective-permute-done.1.xa2
  16.0 0.0 copy-done.4
  16.0 0.0 copy-start
  16.0 0.2 step0_planes.1
  16.3 2.6 %collective-permute-start.5 = (f32[6,32,256]{2,1,0:T(8,128)S(1)}, f32[6,32,256]{2,1,0:T(8,128)S(1)}, u32[]{:S(2)}, u32[]{:S(2)}) collective-permute-start(f32[6,32,256]{2,1,0:T(8,128)S(1)} %get-tuple-element.63), channel_id=1, source_target_pairs={{0,4},{1,5},{2,6},{3,7},{4,0},{5,1},{6,2},{7,3},{8,12},{9,13},{10,... | collective-permute-start | bytes 589832 | tf_op jit(solution)/shard_map/ppermute | solution.py:562
  18.8 0.7 %collective-permute-start.6 = (f32[6,32,256]{2,1,0:T(8,128)S(1)}, f32[6,32,256]{2,1,0:T(8,128)S(1)}, u32[]{:S(2)}, u32[]{:S(2)}) collective-permute-start(f32[6,32,256]{2,1,0:T(8,128)S(1)} %get-tuple-element.64), channel_id=1, source_target_pairs={{4,8},{5,9},{6,10},{7,11},{8,4},{9,5},{10,6},{11,7},{12,16},{13,17... | collective-permute-start | bytes 589832 | tf_op jit(solution)/shard_map/ppermute | solution.py:562
  19.5 0.7 %collective-permute-start.9 = (f32[6,32,256]{2,1,0:T(8,128)S(1)}, f32[6,32,256]{2,1,0:T(8,128)S(1)}, u32[]{:S(2)}, u32[]{:S(2)}) collective-permute-start(f32[6,32,256]{2,1,0:T(8,128)S(1)} %get-tuple-element.73), channel_id=1, source_target_pairs={{4,8},{5,9},{6,10},{7,11},{8,4},{9,5},{10,6},{11,7},{12,16},{13,17... | collective-permute-start | bytes 589832 | tf_op jit(solution)/shard_map/ppermute | solution.py:562
  20.2 0.7 %collective-permute-start.8 = (f32[8,8,256]{2,1,0:T(8,128)S(1)}, f32[8,8,256]{2,1,0:T(8,128)S(1)}, u32[]{:S(2)}, u32[]{:S(2)}) collective-permute-start(f32[8,8,256]{2,1,0:T(8,128)S(1)} %get-tuple-element.66), channel_id=1, source_target_pairs={{1,2},{2,1},{5,6},{6,5},{9,10},{10,9},{13,14},{14,13},{17,18},{18,... | collective-permute-start | bytes 196616 | tf_op jit(solution)/shard_map/ppermute | solution.py:562
  20.9 0.0 collective-permute-done.4.xf.xf1
  20.9 4.1 %collective-permute-start.7 = (f32[8,4,256]{2,1,0:T(4,128)S(1)}, f32[8,4,256]{2,1,0:T(4,128)S(1)}, u32[]{:S(2)}, u32[]{:S(2)}) collective-permute-start(f32[8,4,256]{2,1,0:T(4,128)S(1)} %get-tuple-element.65), channel_id=1, source_target_pairs={{0,1},{1,0},{2,3},{3,2},{4,5},{5,4},{6,7},{7,6},{8,9},{9,8},{10,11... | collective-permute-start | bytes 98312 | tf_op jit(solution)/shard_map/ppermute | solution.py:562
  24.9 0.0 copy-done
  24.9 0.0 copy-start.9
  24.9 1.3 %images_and_step1_own.1 = (f32[8,32,256]{2,1,0:T(8,128)S(1)}, f32[8,32,256]{2,1,0:T(8,128)S(1)}, f32[8,32,256]{2,1,0:T(8,128)S(1)}, f32[8,32,256]{2,1,0:T(8,128)...) custom-call(f32[1,2,1,8,32,256]{5,4,3,2,1,0:T(8,128)S(1)} %copy-done.1, ...), custom_call_target="tpu_custom_call" | custom-call | bytes 60000000 | tf_op jit(solution)/shard_map/images_and_step1_own/pallas_call | solution.py:535
  26.3 0.0 collective-permute-done.7.ys1
  26.3 0.0 collective-permute-done.8.ys2
  26.3 6.3 %collective-permute-done.5.xs1 = f32[6,32,256]{2,1,0:T(8,128)S(1)} collective-permute-done((f32[6,32,256]{2,1,0:T(8,128)S(1)}, f32[6,32,256]{2,1,0:T(8,128)S(1)}, u32[]{:S(2)}, u32[]{:S(2)}) %collective-permute-start.5) | collective-permute-done | bytes 196640 | tf_op jit(solution)/shard_map/ppermute | solution.py:562
  32.6 0.0 collective-permute-done.6.xs2
  32.6 0.0 collective-permute-done.9.xf2
  32.6 0.0 copy-done.9
  32.6 1.1 %step1_planes.1 = (f32[1,8,32,256]{3,2,1,0:T(8,128)}, f32[1,2,1,8,32,256]{5,4,3,2,1,0:T(8,128)}) custom-call(f32[6,32,256]{2,1,0:T(8,128)S(1)} %collective-permute-done.5.xs1, f32[6,32,256]{2,1,0:T(8,128)S(1)} %collective-permute-done.6.xs2, f32[8,4,256]{2,1,0:T(4,128)S(1)} %collective-permute-done.7.ys1, ...), custom_call_target="tpu_custom_call", output_to_operand_aliasing={{1}: (16, {})} | custom-call | bytes 3000000 | tf_op jit(solution)/shard_map/step1_planes/pallas_call | solution.py:535
Async XLA Ops:
  1.8 14.2 %collective-permute-start = (f32[2,4,32,256]{3,2,1,0:T(8,128)S(1)}, f32[2,4,32,256]{3,2,1,0:T(8,128)S(1)}, u32[]{:S(2)}, u32[]{:S(2)}) collective-permute-start(f32[2,4,32,256]{3,2,1,0:T(8,128)S(1)} %get-tuple-element.40), channel_id=1, source_target_pairs={{0,4},{1,5},{2,6},{3,7},{4,0},{5,1},{6,2},{7,3},{8,12},{9,13},{10,... | collective-permute-start | bytes 786440 | tf_op jit(solution)/shard_map/ppermute | solution.py:562
  4.8 11.2 %collective-permute-start.1 = (f32[2,4,32,256]{3,2,1,0:T(8,128)S(1)}, f32[2,4,32,256]{3,2,1,0:T(8,128)S(1)}, u32[]{:S(2)}, u32[]{:S(2)}) collective-permute-start(f32[2,4,32,256]{3,2,1,0:T(8,128)S(1)} %get-tuple-element.41), channel_id=1, source_target_pairs={{4,8},{5,9},{6,10},{7,11},{8,4},{9,5},{10,6},{11,7},{12,16},{13,17... | collective-permute-start | bytes 786440 | tf_op jit(solution)/shard_map/ppermute | solution.py:562
  5.5 2.6 %copy-start.6 = (s32[4096,2]{0,1:T(2,128)S(1)}, s32[4096,2]{0,1:T(2,128)}, u32[]{:S(2)}) copy-start(s32[4096,2]{0,1:T(2,128)} %param.15) | copy-start | bytes 98308
  5.5 2.6 %copy-start.7 = (f32[1,2,4096]{2,1,0:T(2,128)S(1)}, f32[1,2,4096]{2,1,0:T(2,128)}, u32[]{:S(2)}) copy-start(f32[1,2,4096]{2,1,0:T(2,128)} %res.1) | copy-start | bytes 98308
  6.7 1.4 %copy-start.8 = (s32[1,8,32]{2,1,0:T(8,128)S(1)}, s32[1,8,32]{2,1,0:T(8,128)}, u32[]{:S(2)}) copy-start(s32[1,8,32]{2,1,0:T(8,128)} %topo.1) | copy-start | bytes 3076
  6.7 1.4 %collective-permute-start.2 = (f32[4,8,4,256]{3,2,1,0:T(4,128)S(1)}, f32[4,8,4,256]{3,2,1,0:T(4,128)S(1)}, u32[]{:S(2)}, u32[]{:S(2)}) collective-permute-start(f32[4,8,4,256]{3,2,1,0:T(4,128)S(1)} %get-tuple-element.43), channel_id=1, source_target_pairs={{0,1},{1,0},{2,3},{3,2},{4,5},{5,4},{6,7},{7,6},{8,9},{9,8},{10,11... | collective-permute-start | bytes 393224 | tf_op jit(solution)/shard_map/ppermute | solution.py:562
  6.8 7.3 %collective-permute-start.3 = (f32[4,8,4,256]{3,2,1,0:T(4,128)S(1)}, f32[4,8,4,256]{3,2,1,0:T(4,128)S(1)}, u32[]{:S(2)}, u32[]{:S(2)}) collective-permute-start(f32[4,8,4,256]{3,2,1,0:T(4,128)S(1)} %get-tuple-element.44), channel_id=1, source_target_pairs={{1,2},{2,1},{5,6},{6,5},{9,10},{10,9},{13,14},{14,13},{17,18},{18,... | collective-permute-start | bytes 393224 | tf_op jit(solution)/shard_map/ppermute | solution.py:562
  8.1 6.0 %copy-start.1 = (f32[1,2,1,8,32,256]{5,4,3,2,1,0:T(8,128)S(1)}, f32[1,2,1,8,32,256]{5,4,3,2,1,0:T(8,128)}, u32[]{:S(2)}) copy-start(f32[1,2,1,8,32,256]{5,4,3,2,1,0:T(8,128)} %adj.5) | copy-start | bytes 1572868
  8.1 6.0 %copy-start.2 = (f32[1,8,32,256]{3,2,1,0:T(8,128)S(1)}, f32[1,8,32,256]{3,2,1,0:T(8,128)}, u32[]{:S(2)}) copy-start(f32[1,8,32,256]{3,2,1,0:T(8,128)} %buoy.5) | copy-start | bytes 786436
  8.1 6.0 %copy-start.3 = (bf16[256,512]{1,0:T(8,128)(2,1)S(1)}, bf16[256,512]{1,0:T(8,128)(2,1)}, u32[]{:S(2)}) copy-start(bf16[256,512]{1,0:T(8,128)(2,1)} %constant.6.clone.zf) | copy-start | bytes 786436
  8.1 6.0 %copy-start.5 = (bf16[2,64,80]{2,1,0:T(8,128)(2,1)S(1)}, bf16[2,64,80]{2,1,0:T(8,128)(2,1)}, u32[]{:S(2)}) copy-start(bf16[2,64,80]{2,1,0:T(8,128)(2,1)} %constant.7.clone.yf) | copy-start | bytes 61444
  9.7 11.1 %collective-permute-start.4 = (f32[6,32,256]{2,1,0:T(8,128)S(1)}, f32[6,32,256]{2,1,0:T(8,128)S(1)}, u32[]{:S(2)}, u32[]{:S(2)}) collective-permute-start(f32[6,32,256]{2,1,0:T(8,128)S(1)} %get-tuple-element.61), channel_id=1, source_target_pairs={{0,4},{1,5},{2,6},{3,7},{4,0},{5,1},{6,2},{7,3},{8,12},{9,13},{10,... | collective-permute-start | bytes 589832 | tf_op jit(solution)/shard_map/ppermute | solution.py:562
  14.1 1.9 %copy-start.4 = (f32[1,8,32,256]{3,2,1,0:T(8,128)S(1)}, f32[1,8,32,256]{3,2,1,0:T(8,128)}, u32[]{:S(2)}) copy-start(f32[1,8,32,256]{3,2,1,0:T(8,128)} %mod.3) | copy-start | bytes 786436
  16.0 8.9 %copy-start = (f32[1,4,1,8,32,256]{5,4,3,2,1,0:T(8,128)S(1)}, f32[1,4,1,8,32,256]{5,4,3,2,1,0:T(8,128)}, u32[]{:S(2)}) copy-start(f32[1,4,1,8,32,256]{5,4,3,2,1,0:T(8,128)} %fwd.5) | copy-start | bytes 3145732
  16.3 16.4 %collective-permute-start.5 = (f32[6,32,256]{2,1,0:T(8,128)S(1)}, f32[6,32,256]{2,1,0:T(8,128)S(1)}, u32[]{:S(2)}, u32[]{:S(2)}) collective-permute-start(f32[6,32,256]{2,1,0:T(8,128)S(1)} %get-tuple-element.63), channel_id=1, source_target_pairs={{0,4},{1,5},{2,6},{3,7},{4,0},{5,1},{6,2},{7,3},{8,12},{9,13},{10,... | collective-permute-start | bytes 589832 | tf_op jit(solution)/shard_map/ppermute | solution.py:562
  18.8 13.8 %collective-permute-start.6 = (f32[6,32,256]{2,1,0:T(8,128)S(1)}, f32[6,32,256]{2,1,0:T(8,128)S(1)}, u32[]{:S(2)}, u32[]{:S(2)}) collective-permute-start(f32[6,32,256]{2,1,0:T(8,128)S(1)} %get-tuple-element.64), channel_id=1, source_target_pairs={{4,8},{5,9},{6,10},{7,11},{8,4},{9,5},{10,6},{11,7},{12,16},{13,17... | collective-permute-start | bytes 589832 | tf_op jit(solution)/shard_map/ppermute | solution.py:562
  19.5 13.1 %collective-permute-start.9 = (f32[6,32,256]{2,1,0:T(8,128)S(1)}, f32[6,32,256]{2,1,0:T(8,128)S(1)}, u32[]{:S(2)}, u32[]{:S(2)}) collective-permute-start(f32[6,32,256]{2,1,0:T(8,128)S(1)} %get-tuple-element.73), channel_id=1, source_target_pairs={{4,8},{5,9},{6,10},{7,11},{8,4},{9,5},{10,6},{11,7},{12,16},{13,17... | collective-permute-start | bytes 589832 | tf_op jit(solution)/shard_map/ppermute | solution.py:562
  20.2 6.1 %collective-permute-start.8 = (f32[8,8,256]{2,1,0:T(8,128)S(1)}, f32[8,8,256]{2,1,0:T(8,128)S(1)}, u32[]{:S(2)}, u32[]{:S(2)}) collective-permute-start(f32[8,8,256]{2,1,0:T(8,128)S(1)} %get-tuple-element.66), channel_id=1, source_target_pairs={{1,2},{2,1},{5,6},{6,5},{9,10},{10,9},{13,14},{14,13},{17,18},{18,... | collective-permute-start | bytes 196616 | tf_op jit(solution)/shard_map/ppermute | solution.py:562
  20.9 5.4 %collective-permute-start.7 = (f32[8,4,256]{2,1,0:T(4,128)S(1)}, f32[8,4,256]{2,1,0:T(4,128)S(1)}, u32[]{:S(2)}, u32[]{:S(2)}) collective-permute-start(f32[8,4,256]{2,1,0:T(4,128)S(1)} %get-tuple-element.65), channel_id=1, source_target_pairs={{0,1},{1,0},{2,3},{3,2},{4,5},{5,4},{6,7},{7,6},{8,9},{9,8},{10,11... | collective-permute-start | bytes 98312 | tf_op jit(solution)/shard_map/ppermute | solution.py:562
  24.9 7.7 %copy-start.9 = (bf16[2,32,16]{2,1,0:T(8,128)(2,1)S(1)}, bf16[2,32,16]{2,1,0:T(8,128)(2,1)}, u32[]{:S(2)}) copy-start(bf16[2,32,16]{2,1,0:T(8,128)(2,1)} %constant.8.clone.ye) | copy-start | bytes 6148

commit v7 on v6

--- a/solution.py
+++ b/solution.py
@@ -457,14 +457,28 @@
     second.wait()
 
 
+def column_kernel(ys1, ys2, weight, gy, fy, ye, rest_in, image_in, rest, image):
+    width, height, depth = weight.shape
+    factor = ye[column_parity()]
+    even = column_parity() == 0
+    for i in range(width):
+        second = jnp.where(even, ys2[i, 8 - HALO :], ys2[i, :HALO])
+        edge = dot(factor, edge_parts(ys1[i], second))
+        for n, start in ((0, 0), (8, height - 8)):
+            rows = pl.ds(start, 8)
+            s_y = C_UNIT * edge[n : n + 8]
+            lap = A_UNIT * edge[16 + n : 24 + n]
+            rest[i, rows] = rest_in[i, rows] + weight[i, rows] * lap + gy[i, rows] * s_y
+            image[i, rows] = image_in[i, rows] + C_UNIT * (fy[i, rows] * s_y)
+
+
 def last_kernel(
-    xs1, xs2, ys1, ys2, rest, sx_own, image, fx, fy, gx, gy, weight, ye, sx0, xf1, xf2, states_in,
+    xs1, xs2, rest, sx_own, image, fx, gx, weight, sx0, xf1, xf2, states_in,
     image_out, states_out,
     image_v, e1_v, sem,
 ):
     width, height, depth = rest.shape
     tiles = height // 8
-    factor = ye[column_parity()]
 
     def leave(t):
         rows = pl.ds(8 * t, 8)
@@ -473,15 +487,8 @@
             pltpu.make_async_copy(image_v.at[:, rows], image_out.at[0, :, rows], sem.at[tiles + t]),
         )
 
-    even = column_parity() == 0
-
-    def edge_of(i):
-        second = jnp.where(even, ys2[i, 8 - HALO :], ys2[i, :HALO])
-        return dot(factor, edge_parts(ys1[i], second))
-
     def body(low_ref, high_ref, low_fields, high_fields, low_one, high_one):
-        edges = [edge_of(i) for i in range(width)]
-        for t in list(range(1, tiles - 1)) + [0, tiles - 1]:
+        for t in range(tiles):
             rows = pl.ds(8 * t, 8)
             low = [low_ref[i, rows] for i in range(HALO)]
             high = [high_ref[i, rows] for i in range(HALO)]
@@ -497,12 +504,6 @@
                 f_x = edge_slope(i, width, low1, high1)
                 if f_x is not None:
                     shown = shown + f_x * sx0[i, rows]
-                if t == 0 or t == tiles - 1:
-                    n = 0 if t == 0 else 8
-                    s_y = C_UNIT * edges[i][n : n + 8]
-                    lap = lap + A_UNIT * edges[i][16 + n : 24 + n]
-                    add = add + gy[i, rows] * s_y
-                    shown = shown + C_UNIT * (fy[i, rows] * s_y)
                 e1_v[i, rows] = rest[i, rows] + weight[i, rows] * lap + add
                 image_v[i, rows] = shown
             for c in leave(t):
@@ -621,14 +622,21 @@
         [VMEM(z_out, F32), VMEM(y_out, F32)] + [VMEM(block, F32)] * 4 + [dma((2,))],
         us=20.0,
     )
+    rest, image = call(
+        column_kernel,
+        "column_edges",
+        [(ys1, True), (ys2, True), (weight, True), (gy, True), (fy, True), (ye, True), (rest, True), (image, True)],
+        [(block, True)] * 2,
+        aliases={6: 0, 7: 1},
+    )
     image_buo, states = call(
         last_kernel,
         "step1_planes",
-        [(xs1, True), (xs2, True), (ys1, True), (ys2, True), (rest, True), (sx_own, True), (image, True), (fx, True),
-         (fy, True), (gx, True), (gy, True), (weight, True), (ye, True), (sx, True), (xf1, True), (xf2, True), (states, False)],
+        [(xs1, True), (xs2, True), (rest, True), (sx_own, True), (image, True), (fx, True), (gx, True), (weight, True),
+         (sx, True), (xf1, True), (xf2, True), (states, False)],
         [((1,) + block, False), ((1, STEPS, 1) + block, False)],
         [VMEM(block, F32), VMEM(block, F32), dma((2 * (height // 8),))],
-        aliases={16: 1},
+        aliases={11: 1},
     )
     if lax.axis_size("shot") > 1:
         image_mod, image_buo = lax.psum((image_mod, image_buo), "shot")

time: 34 us -> 33.8 us (level)
    pallas_call x7 -> x8, Pallas kernels: 7.28 us -> 7.29 us  [call(): pl.pallas_call(kernel, name=name, in_specs=in_specs, out_specs=out_specs,...]
  transfers between devices with their start and end apart: 10 -> 10, of which waited for: 3 -> 3; matrix products, arithmetic and copies ran while one was open for 0% -> 0% of each run, Pallas kernels for 15% -> 16%
where the time goes in v7:
time: 33.8 us; the launch traced here: 33.5 us
  starting transfers between devices  17.4 us (51%)
  waiting for transfers between devices  7.93 us (23%)
  Pallas kernels  7.29 us (22%)
  between operations  0.86 us (3%)
    ppermute x10, starting transfers between devices, swap(): return lax.ppermute(value, 'blk', pairs)  17.4 us
    ppermute x10, waiting for transfers between devices, swap(): return lax.ppermute(value, 'blk', pairs)  7.93 us
    pallas_call x8, Pallas kernels, call(): pl.pallas_call(kernel, name=name, in_specs=in_specs, out_specs=out_specs,...  7.29 us
  transfers between devices with their start and end apart: 10, of which 3 were waited for; matrix products, arithmetic and copies ran while one was open for 0% of the time, Pallas kernels for 16%

profile of v7, /device:TPU:0, one launch (start us, length us, event | category | flops | bytes accessed | tf_op | source)
XLA Modules:
  0.0 33.5 jit_solution(301592315598991914)
XLA Ops:
  0.6 1.2 %scaled_and_planes.1 = (f32[2,4,32,256]{3,2,1,0:T(8,128)S(1)}, f32[2,4,32,256]{3,2,1,0:T(8,128)S(1)}, f32[8,32,256]{2,1,0:T(8,128)S(1)}) custom-call(f32[1,2,1,8,32,256]{5,4,3,2,1,0:T(8,128)} %adj.5, f32[1,8,32,256]{3,2,1,0:T(8,128)} %mod.3, f32[1,8,32,256]{3,2,1,0:T(8,128)} %buoy.5, s32[1,8,32]{2,1,0:T(8,128)} %topo.1), custom_call_target="tpu_custom_call" | custom-call | bytes 3000000 | tf_op jit(solution)/shard_map/scaled_and_planes/pallas_call | solution.py:536
  1.8 3.0 %collective-permute-start = (f32[2,4,32,256]{3,2,1,0:T(8,128)S(1)}, f32[2,4,32,256]{3,2,1,0:T(8,128)S(1)}, u32[]{:S(2)}, u32[]{:S(2)}) collective-permute-start(f32[2,4,32,256]{3,2,1,0:T(8,128)S(1)} %get-tuple-element.42), channel_id=1, source_target_pairs={{0,4},{1,5},{2,6},{3,7},{4,0},{5,1},{6,2},{7,3},{8,12},{9,13},{10,... | collective-permute-start | bytes 786440 | tf_op jit(solution)/shard_map/ppermute | solution.py:563
  4.8 0.7 %collective-permute-start.1 = (f32[2,4,32,256]{3,2,1,0:T(8,128)S(1)}, f32[2,4,32,256]{3,2,1,0:T(8,128)S(1)}, u32[]{:S(2)}, u32[]{:S(2)}) collective-permute-start(f32[2,4,32,256]{3,2,1,0:T(8,128)S(1)} %get-tuple-element.43), channel_id=1, source_target_pairs={{4,8},{5,9},{6,10},{7,11},{8,4},{9,5},{10,6},{11,7},{12,16},{13,17... | collective-permute-start | bytes 786440 | tf_op jit(solution)/shard_map/ppermute | solution.py:563
  5.5 0.0 copy-start.6
  5.5 0.0 copy-start.7
  5.5 1.1 %edges.1 = (f32[4,8,4,256]{3,2,1,0:T(4,128)S(1)}, f32[4,8,4,256]{3,2,1,0:T(4,128)S(1)}) custom-call(f32[1,8,32,256]{3,2,1,0:T(8,128)} %buoy.5, f32[1,4,1,8,32,256]{5,4,3,2,1,0:T(8,128)} %fwd.5, f32[8,32,256]{2,1,0:T(8,128)S(1)} %get-tuple-element.44.s0), custom_call_target="tpu_custom_call" | custom-call | bytes 3000000 | tf_op jit(solution)/shard_map/edges/pallas_call | solution.py:536
  6.7 0.0 copy-start.9
  6.7 0.1 collective-permute-start.2
  6.8 0.7 %collective-permute-start.3 = (f32[4,8,4,256]{3,2,1,0:T(4,128)S(1)}, f32[4,8,4,256]{3,2,1,0:T(4,128)S(1)}, u32[]{:S(2)}, u32[]{:S(2)}) collective-permute-start(f32[4,8,4,256]{3,2,1,0:T(4,128)S(1)} %get-tuple-element.46), channel_id=1, source_target_pairs={{1,2},{2,1},{5,6},{6,5},{9,10},{10,9},{13,14},{14,13},{17,18},{18,... | collective-permute-start | bytes 393224 | tf_op jit(solution)/shard_map/ppermute | solution.py:563
  7.4 0.7 %collective-permute-done.2._.y1.yf1 = f32[4,8,4,256]{3,2,1,0:T(4,128)S(1)} collective-permute-done((f32[4,8,4,256]{3,2,1,0:T(4,128)S(1)}, f32[4,8,4,256]{3,2,1,0:T(4,128)S(1)}, u32[]{:S(2)}, u32[]{:S(2)}) %collective-permute-start.2) | collective-permute-done | bytes 131104 | tf_op jit(solution)/shard_map/ppermute | solution.py:563
  8.1 0.0 copy-done.6
  8.1 0.0 copy-done.7
  8.1 0.0 copy-done.9
  8.1 0.0 copy-start.1
  8.1 0.0 copy-start.2
  8.1 0.0 copy-start.3
  8.1 0.0 copy-start.5
  8.1 1.6 %sources_and_planes.1 = (f32[8,32,256]{2,1,0:T(8,128)S(1)}, f32[2,8,32,256]{3,2,1,0:T(8,128)S(1)}, f32[6,32,256]{2,1,0:T(8,128)S(1)}, f32[6,32,256]{2,1,0:T(8,12...) custom-call(s32[1,8,32]{2,1,0:T(8,128)S(1)} %copy-done.9, s32[2,4096]{1,0:T(2,128)S(1)} %bitcast.1, ...), custom_call_target="tpu_custom_call" | custom-call | bytes 3000000 | tf_op jit(solution)/shard_map/sources_and_planes/pallas_call | solution.py:536
  9.7 4.3 %collective-permute-start.4 = (f32[6,32,256]{2,1,0:T(8,128)S(1)}, f32[6,32,256]{2,1,0:T(8,128)S(1)}, u32[]{:S(2)}, u32[]{:S(2)}) collective-permute-start(f32[6,32,256]{2,1,0:T(8,128)S(1)} %get-tuple-element.63), channel_id=1, source_target_pairs={{0,4},{1,5},{2,6},{3,7},{4,0},{5,1},{6,2},{7,3},{8,12},{9,13},{10,... | collective-permute-start | bytes 589832 | tf_op jit(solution)/shard_map/ppermute | solution.py:563
  14.1 0.0 collective-permute-done.3.y2.yf2
  14.1 0.0 copy-done.1
  14.1 0.0 copy-done.2
  14.1 0.0 copy-done.3
  14.1 0.0 copy-done.5
  14.1 0.0 copy-start.4
  14.1 0.8 %step0_own.1 = (f32[8,32,256]{2,1,0:T(8,128)S(1)}, f32[8,32,256]{2,1,0:T(8,128)S(1)}, f32[8,32,256]{2,1,0:T(8,128)S(1)}, f32[8,32,256]{2,1,0:T(8,128)S(1)}, f32[...) custom-call(f32[1,2,1,8,32,256]{5,4,3,2,1,0:T(8,128)S(1)} %copy-done.1, ...), custom_call_target="tpu_custom_call" | custom-call | bytes 12000000 | tf_op jit(solution)/shard_map/step0_own/pallas_call | solution.py:536
  14.9 1.1 %collective-permute-done.xa1 = f32[2,4,32,256]{3,2,1,0:T(8,128)S(1)} collective-permute-done((f32[2,4,32,256]{3,2,1,0:T(8,128)S(1)}, f32[2,4,32,256]{3,2,1,0:T(8,128)S(1)}, u32[]{:S(2)}, u32[]{:S(2)}) %collective-permute-start) | collective-permute-done | bytes 262176 | tf_op jit(solution)/shard_map/ppermute | solution.py:563
  16.0 0.0 collective-permute-done.1.xa2
  16.0 0.0 copy-done.4
  16.0 0.0 copy-start
  16.0 0.2 step0_planes.1
  16.3 2.6 %collective-permute-start.5 = (f32[6,32,256]{2,1,0:T(8,128)S(1)}, f32[6,32,256]{2,1,0:T(8,128)S(1)}, u32[]{:S(2)}, u32[]{:S(2)}) collective-permute-start(f32[6,32,256]{2,1,0:T(8,128)S(1)} %get-tuple-element.65), channel_id=1, source_target_pairs={{0,4},{1,5},{2,6},{3,7},{4,0},{5,1},{6,2},{7,3},{8,12},{9,13},{10,... | collective-permute-start | bytes 589832 | tf_op jit(solution)/shard_map/ppermute | solution.py:563
  18.8 0.7 %collective-permute-start.6 = (f32[6,32,256]{2,1,0:T(8,128)S(1)}, f32[6,32,256]{2,1,0:T(8,128)S(1)}, u32[]{:S(2)}, u32[]{:S(2)}) collective-permute-start(f32[6,32,256]{2,1,0:T(8,128)S(1)} %get-tuple-element.66), channel_id=1, source_target_pairs={{4,8},{5,9},{6,10},{7,11},{8,4},{9,5},{10,6},{11,7},{12,16},{13,17... | collective-permute-start | bytes 589832 | tf_op jit(solution)/shard_map/ppermute | solution.py:563
  19.5 0.7 %collective-permute-start.9 = (f32[6,32,256]{2,1,0:T(8,128)S(1)}, f32[6,32,256]{2,1,0:T(8,128)S(1)}, u32[]{:S(2)}, u32[]{:S(2)}) collective-permute-start(f32[6,32,256]{2,1,0:T(8,128)S(1)} %get-tuple-element.77), channel_id=1, source_target_pairs={{4,8},{5,9},{6,10},{7,11},{8,4},{9,5},{10,6},{11,7},{12,16},{13,17... | collective-permute-start | bytes 589832 | tf_op jit(solution)/shard_map/ppermute | solution.py:563
  20.2 0.7 %collective-permute-start.8 = (f32[8,8,256]{2,1,0:T(8,128)S(1)}, f32[8,8,256]{2,1,0:T(8,128)S(1)}, u32[]{:S(2)}, u32[]{:S(2)}) collective-permute-start(f32[8,8,256]{2,1,0:T(8,128)S(1)} %get-tuple-element.68), channel_id=1, source_target_pairs={{1,2},{2,1},{5,6},{6,5},{9,10},{10,9},{13,14},{14,13},{17,18},{18,... | collective-permute-start | bytes 196616 | tf_op jit(solution)/shard_map/ppermute | solution.py:563
  20.9 0.0 collective-permute-done.4.xf.xf1
  20.9 4.1 %collective-permute-start.7 = (f32[8,4,256]{2,1,0:T(4,128)S(1)}, f32[8,4,256]{2,1,0:T(4,128)S(1)}, u32[]{:S(2)}, u32[]{:S(2)}) collective-permute-start(f32[8,4,256]{2,1,0:T(4,128)S(1)} %get-tuple-element.67), channel_id=1, source_target_pairs={{0,1},{1,0},{2,3},{3,2},{4,5},{5,4},{6,7},{7,6},{8,9},{9,8},{10,11... | collective-permute-start | bytes 98312 | tf_op jit(solution)/shard_map/ppermute | solution.py:563
  24.9 0.0 copy-done
  24.9 0.0 copy-start.8
  24.9 1.3 %images_and_step1_own.1 = (f32[8,32,256]{2,1,0:T(8,128)S(1)}, f32[8,32,256]{2,1,0:T(8,128)S(1)}, f32[8,32,256]{2,1,0:T(8,128)S(1)}, f32[8,32,256]{2,1,0:T(8,128)...) custom-call(f32[1,2,1,8,32,256]{5,4,3,2,1,0:T(8,128)S(1)} %copy-done.1, ...), custom_call_target="tpu_custom_call" | custom-call | bytes 60000000 | tf_op jit(solution)/shard_map/images_and_step1_own/pallas_call | solution.py:536
  26.3 0.0 collective-permute-done.7.ys1
  26.3 0.0 collective-permute-done.8.ys2
  26.3 0.0 copy-done.8
  26.3 0.2 column_edges.1
  26.5 6.1 %collective-permute-done.5.xs1 = f32[6,32,256]{2,1,0:T(8,128)S(1)} collective-permute-done((f32[6,32,256]{2,1,0:T(8,128)S(1)}, f32[6,32,256]{2,1,0:T(8,128)S(1)}, u32[]{:S(2)}, u32[]{:S(2)}) %collective-permute-start.5) | collective-permute-done | bytes 196640 | tf_op jit(solution)/shard_map/ppermute | solution.py:563
  32.6 0.0 collective-permute-done.6.xs2
  32.6 0.0 collective-permute-done.9.xf2
  32.6 0.9 %step1_planes.1 = (f32[1,8,32,256]{3,2,1,0:T(8,128)}, f32[1,2,1,8,32,256]{5,4,3,2,1,0:T(8,128)}) custom-call(f32[6,32,256]{2,1,0:T(8,128)S(1)} %collective-permute-done.5.xs1, f32[6,32,256]{2,1,0:T(8,128)S(1)} %collective-permute-done.6.xs2, f32[8,32,256]{2,1,0:T(8,128)S(1)} %get-tuple-element.72.rest, ...), custom_call_target="tpu_custom_call", output_to_operand_aliasing={{1}: (11, {})} | custom-call | bytes 3000000 | tf_op jit(solution)/shard_map/step1_planes/pallas_call | solution.py:536
Async XLA Ops:
  1.8 14.2 %collective-permute-start = (f32[2,4,32,256]{3,2,1,0:T(8,128)S(1)}, f32[2,4,32,256]{3,2,1,0:T(8,128)S(1)}, u32[]{:S(2)}, u32[]{:S(2)}) collective-permute-start(f32[2,4,32,256]{3,2,1,0:T(8,128)S(1)} %get-tuple-element.42), channel_id=1, source_target_pairs={{0,4},{1,5},{2,6},{3,7},{4,0},{5,1},{6,2},{7,3},{8,12},{9,13},{10,... | collective-permute-start | bytes 786440 | tf_op jit(solution)/shard_map/ppermute | solution.py:563
  4.8 11.2 %collective-permute-start.1 = (f32[2,4,32,256]{3,2,1,0:T(8,128)S(1)}, f32[2,4,32,256]{3,2,1,0:T(8,128)S(1)}, u32[]{:S(2)}, u32[]{:S(2)}) collective-permute-start(f32[2,4,32,256]{3,2,1,0:T(8,128)S(1)} %get-tuple-element.43), channel_id=1, source_target_pairs={{4,8},{5,9},{6,10},{7,11},{8,4},{9,5},{10,6},{11,7},{12,16},{13,17... | collective-permute-start | bytes 786440 | tf_op jit(solution)/shard_map/ppermute | solution.py:563
  5.5 2.6 %copy-start.6 = (s32[4096,2]{0,1:T(2,128)S(1)}, s32[4096,2]{0,1:T(2,128)}, u32[]{:S(2)}) copy-start(s32[4096,2]{0,1:T(2,128)} %param.15) | copy-start | bytes 98308
  5.5 2.6 %copy-start.7 = (f32[1,2,4096]{2,1,0:T(2,128)S(1)}, f32[1,2,4096]{2,1,0:T(2,128)}, u32[]{:S(2)}) copy-start(f32[1,2,4096]{2,1,0:T(2,128)} %res.1) | copy-start | bytes 98308
  6.7 1.4 %copy-start.9 = (s32[1,8,32]{2,1,0:T(8,128)S(1)}, s32[1,8,32]{2,1,0:T(8,128)}, u32[]{:S(2)}) copy-start(s32[1,8,32]{2,1,0:T(8,128)} %topo.1) | copy-start | bytes 3076
  6.7 1.4 %collective-permute-start.2 = (f32[4,8,4,256]{3,2,1,0:T(4,128)S(1)}, f32[4,8,4,256]{3,2,1,0:T(4,128)S(1)}, u32[]{:S(2)}, u32[]{:S(2)}) collective-permute-start(f32[4,8,4,256]{3,2,1,0:T(4,128)S(1)} %get-tuple-element.45), channel_id=1, source_target_pairs={{0,1},{1,0},{2,3},{3,2},{4,5},{5,4},{6,7},{7,6},{8,9},{9,8},{10,11... | collective-permute-start | bytes 393224 | tf_op jit(solution)/shard_map/ppermute | solution.py:563
  6.8 7.3 %collective-permute-start.3 = (f32[4,8,4,256]{3,2,1,0:T(4,128)S(1)}, f32[4,8,4,256]{3,2,1,0:T(4,128)S(1)}, u32[]{:S(2)}, u32[]{:S(2)}) collective-permute-start(f32[4,8,4,256]{3,2,1,0:T(4,128)S(1)} %get-tuple-element.46), channel_id=1, source_target_pairs={{1,2},{2,1},{5,6},{6,5},{9,10},{10,9},{13,14},{14,13},{17,18},{18,... | collective-permute-start | bytes 393224 | tf_op jit(solution)/shard_map/ppermute | solution.py:563
  8.1 6.0 %copy-start.1 = (f32[1,2,1,8,32,256]{5,4,3,2,1,0:T(8,128)S(1)}, f32[1,2,1,8,32,256]{5,4,3,2,1,0:T(8,128)}, u32[]{:S(2)}) copy-start(f32[1,2,1,8,32,256]{5,4,3,2,1,0:T(8,128)} %adj.5) | copy-start | bytes 1572868
  8.1 6.0 %copy-start.2 = (f32[1,8,32,256]{3,2,1,0:T(8,128)S(1)}, f32[1,8,32,256]{3,2,1,0:T(8,128)}, u32[]{:S(2)}) copy-start(f32[1,8,32,256]{3,2,1,0:T(8,128)} %buoy.5) | copy-start | bytes 786436
  8.1 6.0 %copy-start.3 = (bf16[256,512]{1,0:T(8,128)(2,1)S(1)}, bf16[256,512]{1,0:T(8,128)(2,1)}, u32[]{:S(2)}) copy-start(bf16[256,512]{1,0:T(8,128)(2,1)} %constant.6.clone.zf) | copy-start | bytes 786436
  8.1 6.0 %copy-start.5 = (bf16[2,64,80]{2,1,0:T(8,128)(2,1)S(1)}, bf16[2,64,80]{2,1,0:T(8,128)(2,1)}, u32[]{:S(2)}) copy-start(bf16[2,64,80]{2,1,0:T(8,128)(2,1)} %constant.7.clone.yf) | copy-start | bytes 61444
  9.7 11.1 %collective-permute-start.4 = (f32[6,32,256]{2,1,0:T(8,128)S(1)}, f32[6,32,256]{2,1,0:T(8,128)S(1)}, u32[]{:S(2)}, u32[]{:S(2)}) collective-permute-start(f32[6,32,256]{2,1,0:T(8,128)S(1)} %get-tuple-element.63), channel_id=1, source_target_pairs={{0,4},{1,5},{2,6},{3,7},{4,0},{5,1},{6,2},{7,3},{8,12},{9,13},{10,... | collective-permute-start | bytes 589832 | tf_op jit(solution)/shard_map/ppermute | solution.py:563
  14.1 1.9 %copy-start.4 = (f32[1,8,32,256]{3,2,1,0:T(8,128)S(1)}, f32[1,8,32,256]{3,2,1,0:T(8,128)}, u32[]{:S(2)}) copy-start(f32[1,8,32,256]{3,2,1,0:T(8,128)} %mod.3) | copy-start | bytes 786436
  16.0 8.9 %copy-start = (f32[1,4,1,8,32,256]{5,4,3,2,1,0:T(8,128)S(1)}, f32[1,4,1,8,32,256]{5,4,3,2,1,0:T(8,128)}, u32[]{:S(2)}) copy-start(f32[1,4,1,8,32,256]{5,4,3,2,1,0:T(8,128)} %fwd.5) | copy-start | bytes 3145732
  16.3 16.4 %collective-permute-start.5 = (f32[6,32,256]{2,1,0:T(8,128)S(1)}, f32[6,32,256]{2,1,0:T(8,128)S(1)}, u32[]{:S(2)}, u32[]{:S(2)}) collective-permute-start(f32[6,32,256]{2,1,0:T(8,128)S(1)} %get-tuple-element.65), channel_id=1, source_target_pairs={{0,4},{1,5},{2,6},{3,7},{4,0},{5,1},{6,2},{7,3},{8,12},{9,13},{10,... | collective-permute-start | bytes 589832 | tf_op jit(solution)/shard_map/ppermute | solution.py:563
  18.8 13.8 %collective-permute-start.6 = (f32[6,32,256]{2,1,0:T(8,128)S(1)}, f32[6,32,256]{2,1,0:T(8,128)S(1)}, u32[]{:S(2)}, u32[]{:S(2)}) collective-permute-start(f32[6,32,256]{2,1,0:T(8,128)S(1)} %get-tuple-element.66), channel_id=1, source_target_pairs={{4,8},{5,9},{6,10},{7,11},{8,4},{9,5},{10,6},{11,7},{12,16},{13,17... | collective-permute-start | bytes 589832 | tf_op jit(solution)/shard_map/ppermute | solution.py:563
  19.5 13.1 %collective-permute-start.9 = (f32[6,32,256]{2,1,0:T(8,128)S(1)}, f32[6,32,256]{2,1,0:T(8,128)S(1)}, u32[]{:S(2)}, u32[]{:S(2)}) collective-permute-start(f32[6,32,256]{2,1,0:T(8,128)S(1)} %get-tuple-element.77), channel_id=1, source_target_pairs={{4,8},{5,9},{6,10},{7,11},{8,4},{9,5},{10,6},{11,7},{12,16},{13,17... | collective-permute-start | bytes 589832 | tf_op jit(solution)/shard_map/ppermute | solution.py:563
  20.2 6.1 %collective-permute-start.8 = (f32[8,8,256]{2,1,0:T(8,128)S(1)}, f32[8,8,256]{2,1,0:T(8,128)S(1)}, u32[]{:S(2)}, u32[]{:S(2)}) collective-permute-start(f32[8,8,256]{2,1,0:T(8,128)S(1)} %get-tuple-element.68), channel_id=1, source_target_pairs={{1,2},{2,1},{5,6},{6,5},{9,10},{10,9},{13,14},{14,13},{17,18},{18,... | collective-permute-start | bytes 196616 | tf_op jit(solution)/shard_map/ppermute | solution.py:563
  20.9 5.4 %collective-permute-start.7 = (f32[8,4,256]{2,1,0:T(4,128)S(1)}, f32[8,4,256]{2,1,0:T(4,128)S(1)}, u32[]{:S(2)}, u32[]{:S(2)}) collective-permute-start(f32[8,4,256]{2,1,0:T(4,128)S(1)} %get-tuple-element.67), channel_id=1, source_target_pairs={{0,1},{1,0},{2,3},{3,2},{4,5},{5,4},{6,7},{7,6},{8,9},{9,8},{10,11... | collective-permute-start | bytes 98312 | tf_op jit(solution)/shard_map/ppermute | solution.py:563
  24.9 1.3 %copy-start.8 = (bf16[2,32,16]{2,1,0:T(8,128)(2,1)S(1)}, bf16[2,32,16]{2,1,0:T(8,128)(2,1)}, u32[]{:S(2)}) copy-start(bf16[2,32,16]{2,1,0:T(8,128)(2,1)} %constant.8.clone.ye) | copy-start | bytes 6148

commit v8 on v7

--- a/solution.py
+++ b/solution.py
@@ -586,7 +586,7 @@
     scale, source, xf1, xf2, xs1, xs2 = call(
         source_kernel,
         "sources_and_planes",
-        [(topography, True), (receivers.T, True), (residuals, True), (forward, False), (ya1, True)],
+        [(topography, True), (receivers.T, True), (residuals, True), (forward, False), (s0, True)],
         [(block, True), ((STEPS,) + block, True)] + [(six, True)] * 4,
         [dma((6,))],
     )

time: 33.8 us -> 33.8 us (level)
  transfers between devices with their start and end apart: 10 -> 10, of which waited for: 3 -> 2; matrix products, arithmetic and copies ran while one was open for 0% -> 0% of each run, Pallas kernels for 16% -> 16%
where the time goes in v8:
time: 33.8 us; the launch traced here: 33.5 us
  starting transfers between devices  17.4 us (51%)
  waiting for transfers between devices  7.9 us (23%)
  Pallas kernels  7.29 us (22%)
  between operations  0.88 us (3%)
    ppermute x10, starting transfers between devices, swap(): return lax.ppermute(value, 'blk', pairs)  17.4 us
    ppermute x10, waiting for transfers between devices, swap(): return lax.ppermute(value, 'blk', pairs)  7.9 us
    pallas_call x8, Pallas kernels, call(): pl.pallas_call(kernel, name=name, in_specs=in_specs, out_specs=out_specs,...  7.29 us
  transfers between devices with their start and end apart: 10, of which 2 were waited for; matrix products, arithmetic and copies ran while one was open for 0% of the time, Pallas kernels for 16%

profile of v8, /device:TPU:0, one launch (start us, length us, event | category | flops | bytes accessed | tf_op | source)
XLA Modules:
  0.0 33.5 jit_solution(16129732282760277995)
XLA Ops:
  0.6 1.2 %scaled_and_planes.1 = (f32[2,4,32,256]{3,2,1,0:T(8,128)S(1)}, f32[2,4,32,256]{3,2,1,0:T(8,128)S(1)}, f32[8,32,256]{2,1,0:T(8,128)S(1)}) custom-call(f32[1,2,1,8,32,256]{5,4,3,2,1,0:T(8,128)} %adj.5, f32[1,8,32,256]{3,2,1,0:T(8,128)} %mod.3, f32[1,8,32,256]{3,2,1,0:T(8,128)} %buoy.5, s32[1,8,32]{2,1,0:T(8,128)} %topo.1), custom_call_target="tpu_custom_call" | custom-call | bytes 3000000 | tf_op jit(solution)/shard_map/scaled_and_planes/pallas_call | solution.py:536
  1.8 3.0 %collective-permute-start = (f32[2,4,32,256]{3,2,1,0:T(8,128)S(1)}, f32[2,4,32,256]{3,2,1,0:T(8,128)S(1)}, u32[]{:S(2)}, u32[]{:S(2)}) collective-permute-start(f32[2,4,32,256]{3,2,1,0:T(8,128)S(1)} %get-tuple-element.42), channel_id=1, source_target_pairs={{0,4},{1,5},{2,6},{3,7},{4,0},{5,1},{6,2},{7,3},{8,12},{9,13},{10,... | collective-permute-start | bytes 786440 | tf_op jit(solution)/shard_map/ppermute | solution.py:563
  4.8 0.7 %collective-permute-start.1 = (f32[2,4,32,256]{3,2,1,0:T(8,128)S(1)}, f32[2,4,32,256]{3,2,1,0:T(8,128)S(1)}, u32[]{:S(2)}, u32[]{:S(2)}) collective-permute-start(f32[2,4,32,256]{3,2,1,0:T(8,128)S(1)} %get-tuple-element.43), channel_id=1, source_target_pairs={{4,8},{5,9},{6,10},{7,11},{8,4},{9,5},{10,6},{11,7},{12,16},{13,17... | collective-permute-start | bytes 786440 | tf_op jit(solution)/shard_map/ppermute | solution.py:563
  5.5 0.0 copy-start.6
  5.5 0.0 copy-start.7
  5.5 1.1 %edges.1 = (f32[4,8,4,256]{3,2,1,0:T(4,128)S(1)}, f32[4,8,4,256]{3,2,1,0:T(4,128)S(1)}) custom-call(f32[1,8,32,256]{3,2,1,0:T(8,128)} %buoy.5, f32[1,4,1,8,32,256]{5,4,3,2,1,0:T(8,128)} %fwd.5, f32[8,32,256]{2,1,0:T(8,128)S(1)} %get-tuple-element.44.s0._), custom_call_target="tpu_custom_call" | custom-call | bytes 3000000 | tf_op jit(solution)/shard_map/edges/pallas_call | solution.py:536
  6.7 0.0 copy-start.9
  6.7 0.1 collective-permute-start.2
  6.8 0.7 %collective-permute-start.3 = (f32[4,8,4,256]{3,2,1,0:T(4,128)S(1)}, f32[4,8,4,256]{3,2,1,0:T(4,128)S(1)}, u32[]{:S(2)}, u32[]{:S(2)}) collective-permute-start(f32[4,8,4,256]{3,2,1,0:T(4,128)S(1)} %get-tuple-element.46), channel_id=1, source_target_pairs={{1,2},{2,1},{5,6},{6,5},{9,10},{10,9},{13,14},{14,13},{17,18},{18,... | collective-permute-start | bytes 393224 | tf_op jit(solution)/shard_map/ppermute | solution.py:563
  7.4 0.0 copy-done.6
  7.4 0.0 copy-done.7
  7.4 0.0 copy-done.9
  7.5 0.0 copy-start.1
  7.5 0.0 copy-start.2
  7.5 0.0 copy-start.3
  7.5 0.0 copy-start.5
  7.5 1.6 %sources_and_planes.1 = (f32[8,32,256]{2,1,0:T(8,128)S(1)}, f32[2,8,32,256]{3,2,1,0:T(8,128)S(1)}, f32[6,32,256]{2,1,0:T(8,128)S(1)}, f32[6,32,256]{2,1,0:T(8,12...) custom-call(s32[1,8,32]{2,1,0:T(8,128)S(1)} %copy-done.9, s32[2,4096]{1,0:T(2,128)S(1)} %bitcast.1, ...), custom_call_target="tpu_custom_call" | custom-call | bytes 3000000 | tf_op jit(solution)/shard_map/sources_and_planes/pallas_call | solution.py:536
  9.1 4.3 %collective-permute-start.4 = (f32[6,32,256]{2,1,0:T(8,128)S(1)}, f32[6,32,256]{2,1,0:T(8,128)S(1)}, u32[]{:S(2)}, u32[]{:S(2)}) collective-permute-start(f32[6,32,256]{2,1,0:T(8,128)S(1)} %get-tuple-element.63), channel_id=1, source_target_pairs={{0,4},{1,5},{2,6},{3,7},{4,0},{5,1},{6,2},{7,3},{8,12},{9,13},{10,... | collective-permute-start | bytes 589832 | tf_op jit(solution)/shard_map/ppermute | solution.py:563
  13.4 0.0 collective-permute-done.2.y1.yf1
  13.4 0.0 collective-permute-done.3.y2.yf2
  13.4 0.0 copy-done.1
  13.4 0.0 copy-done.2
  13.4 0.0 copy-done.3
  13.5 0.0 copy-done.5
  13.5 0.0 copy-start.4
  13.5 0.8 %step0_own.1 = (f32[8,32,256]{2,1,0:T(8,128)S(1)}, f32[8,32,256]{2,1,0:T(8,128)S(1)}, f32[8,32,256]{2,1,0:T(8,128)S(1)}, f32[8,32,256]{2,1,0:T(8,128)S(1)}, f32[...) custom-call(f32[1,2,1,8,32,256]{5,4,3,2,1,0:T(8,128)S(1)} %copy-done.1, ...), custom_call_target="tpu_custom_call" | custom-call | bytes 12000000 | tf_op jit(solution)/shard_map/step0_own/pallas_call | solution.py:536
  14.3 1.8 %collective-permute-done.xa1 = f32[2,4,32,256]{3,2,1,0:T(8,128)S(1)} collective-permute-done((f32[2,4,32,256]{3,2,1,0:T(8,128)S(1)}, f32[2,4,32,256]{3,2,1,0:T(8,128)S(1)}, u32[]{:S(2)}, u32[]{:S(2)}) %collective-permute-start) | collective-permute-done | bytes 262176 | tf_op jit(solution)/shard_map/ppermute | solution.py:563
  16.0 0.0 collective-permute-done.1.xa2
  16.0 0.0 copy-done.4
  16.0 0.0 copy-start
  16.0 0.2 step0_planes.1
  16.3 2.6 %collective-permute-start.5 = (f32[6,32,256]{2,1,0:T(8,128)S(1)}, f32[6,32,256]{2,1,0:T(8,128)S(1)}, u32[]{:S(2)}, u32[]{:S(2)}) collective-permute-start(f32[6,32,256]{2,1,0:T(8,128)S(1)} %get-tuple-element.65), channel_id=1, source_target_pairs={{0,4},{1,5},{2,6},{3,7},{4,0},{5,1},{6,2},{7,3},{8,12},{9,13},{10,... | collective-permute-start | bytes 589832 | tf_op jit(solution)/shard_map/ppermute | solution.py:563
  18.8 0.7 %collective-permute-start.6 = (f32[6,32,256]{2,1,0:T(8,128)S(1)}, f32[6,32,256]{2,1,0:T(8,128)S(1)}, u32[]{:S(2)}, u32[]{:S(2)}) collective-permute-start(f32[6,32,256]{2,1,0:T(8,128)S(1)} %get-tuple-element.66), channel_id=1, source_target_pairs={{4,8},{5,9},{6,10},{7,11},{8,4},{9,5},{10,6},{11,7},{12,16},{13,17... | collective-permute-start | bytes 589832 | tf_op jit(solution)/shard_map/ppermute | solution.py:563
  19.5 0.7 %collective-permute-start.9 = (f32[6,32,256]{2,1,0:T(8,128)S(1)}, f32[6,32,256]{2,1,0:T(8,128)S(1)}, u32[]{:S(2)}, u32[]{:S(2)}) collective-permute-start(f32[6,32,256]{2,1,0:T(8,128)S(1)} %get-tuple-element.77), channel_id=1, source_target_pairs={{4,8},{5,9},{6,10},{7,11},{8,4},{9,5},{10,6},{11,7},{12,16},{13,17... | collective-permute-start | bytes 589832 | tf_op jit(solution)/shard_map/ppermute | solution.py:563
  20.2 0.7 %collective-permute-start.8 = (f32[8,8,256]{2,1,0:T(8,128)S(1)}, f32[8,8,256]{2,1,0:T(8,128)S(1)}, u32[]{:S(2)}, u32[]{:S(2)}) collective-permute-start(f32[8,8,256]{2,1,0:T(8,128)S(1)} %get-tuple-element.68), channel_id=1, source_target_pairs={{1,2},{2,1},{5,6},{6,5},{9,10},{10,9},{13,14},{14,13},{17,18},{18,... | collective-permute-start | bytes 196616 | tf_op jit(solution)/shard_map/ppermute | solution.py:563
  20.9 0.0 collective-permute-done.4.xf.xf1
  20.9 4.1 %collective-permute-start.7 = (f32[8,4,256]{2,1,0:T(4,128)S(1)}, f32[8,4,256]{2,1,0:T(4,128)S(1)}, u32[]{:S(2)}, u32[]{:S(2)}) collective-permute-start(f32[8,4,256]{2,1,0:T(4,128)S(1)} %get-tuple-element.67), channel_id=1, source_target_pairs={{0,1},{1,0},{2,3},{3,2},{4,5},{5,4},{6,7},{7,6},{8,9},{9,8},{10,11... | collective-permute-start | bytes 98312 | tf_op jit(solution)/shard_map/ppermute | solution.py:563
  24.9 0.0 copy-done
  24.9 0.0 copy-start.8
  24.9 1.3 %images_and_step1_own.1 = (f32[8,32,256]{2,1,0:T(8,128)S(1)}, f32[8,32,256]{2,1,0:T(8,128)S(1)}, f32[8,32,256]{2,1,0:T(8,128)S(1)}, f32[8,32,256]{2,1,0:T(8,128)...) custom-call(f32[1,2,1,8,32,256]{5,4,3,2,1,0:T(8,128)S(1)} %copy-done.1, ...), custom_call_target="tpu_custom_call" | custom-call | bytes 60000000 | tf_op jit(solution)/shard_map/images_and_step1_own/pallas_call | solution.py:536
  26.3 0.0 collective-permute-done.7.ys1
  26.3 0.0 collective-permute-done.8.ys2
  26.3 0.0 copy-done.8
  26.3 0.2 column_edges.1
  26.5 6.1 %collective-permute-done.5.xs1 = f32[6,32,256]{2,1,0:T(8,128)S(1)} collective-permute-done((f32[6,32,256]{2,1,0:T(8,128)S(1)}, f32[6,32,256]{2,1,0:T(8,128)S(1)}, u32[]{:S(2)}, u32[]{:S(2)}) %collective-permute-start.5) | collective-permute-done | bytes 196640 | tf_op jit(solution)/shard_map/ppermute | solution.py:563
  32.6 0.0 collective-permute-done.6.xs2
  32.6 0.0 collective-permute-done.9.xf2
  32.6 0.9 %step1_planes.1 = (f32[1,8,32,256]{3,2,1,0:T(8,128)}, f32[1,2,1,8,32,256]{5,4,3,2,1,0:T(8,128)}) custom-call(f32[6,32,256]{2,1,0:T(8,128)S(1)} %collective-permute-done.5.xs1, f32[6,32,256]{2,1,0:T(8,128)S(1)} %collective-permute-done.6.xs2, f32[8,32,256]{2,1,0:T(8,128)S(1)} %get-tuple-element.72.rest, ...), custom_call_target="tpu_custom_call", output_to_operand_aliasing={{1}: (11, {})} | custom-call | bytes 3000000 | tf_op jit(solution)/shard_map/step1_planes/pallas_call | solution.py:536
Async XLA Ops:
  1.8 14.2 %collective-permute-start = (f32[2,4,32,256]{3,2,1,0:T(8,128)S(1)}, f32[2,4,32,256]{3,2,1,0:T(8,128)S(1)}, u32[]{:S(2)}, u32[]{:S(2)}) collective-permute-start(f32[2,4,32,256]{3,2,1,0:T(8,128)S(1)} %get-tuple-element.42), channel_id=1, source_target_pairs={{0,4},{1,5},{2,6},{3,7},{4,0},{5,1},{6,2},{7,3},{8,12},{9,13},{10,... | collective-permute-start | bytes 786440 | tf_op jit(solution)/shard_map/ppermute | solution.py:563
  4.8 11.2 %collective-permute-start.1 = (f32[2,4,32,256]{3,2,1,0:T(8,128)S(1)}, f32[2,4,32,256]{3,2,1,0:T(8,128)S(1)}, u32[]{:S(2)}, u32[]{:S(2)}) collective-permute-start(f32[2,4,32,256]{3,2,1,0:T(8,128)S(1)} %get-tuple-element.43), channel_id=1, source_target_pairs={{4,8},{5,9},{6,10},{7,11},{8,4},{9,5},{10,6},{11,7},{12,16},{13,17... | collective-permute-start | bytes 786440 | tf_op jit(solution)/shard_map/ppermute | solution.py:563
  5.5 1.9 %copy-start.6 = (s32[4096,2]{0,1:T(2,128)S(1)}, s32[4096,2]{0,1:T(2,128)}, u32[]{:S(2)}) copy-start(s32[4096,2]{0,1:T(2,128)} %param.15) | copy-start | bytes 98308
  5.5 1.9 %copy-start.7 = (f32[1,2,4096]{2,1,0:T(2,128)S(1)}, f32[1,2,4096]{2,1,0:T(2,128)}, u32[]{:S(2)}) copy-start(f32[1,2,4096]{2,1,0:T(2,128)} %res.1) | copy-start | bytes 98308
  6.7 0.8 %copy-start.9 = (s32[1,8,32]{2,1,0:T(8,128)S(1)}, s32[1,8,32]{2,1,0:T(8,128)}, u32[]{:S(2)}) copy-start(s32[1,8,32]{2,1,0:T(8,128)} %topo.1) | copy-start | bytes 3076
  6.7 6.8 %collective-permute-start.2 = (f32[4,8,4,256]{3,2,1,0:T(4,128)S(1)}, f32[4,8,4,256]{3,2,1,0:T(4,128)S(1)}, u32[]{:S(2)}, u32[]{:S(2)}) collective-permute-start(f32[4,8,4,256]{3,2,1,0:T(4,128)S(1)} %get-tuple-element.45), channel_id=1, source_target_pairs={{0,1},{1,0},{2,3},{3,2},{4,5},{5,4},{6,7},{7,6},{8,9},{9,8},{10,11... | collective-permute-start | bytes 393224 | tf_op jit(solution)/shard_map/ppermute | solution.py:563
  6.8 6.7 %collective-permute-start.3 = (f32[4,8,4,256]{3,2,1,0:T(4,128)S(1)}, f32[4,8,4,256]{3,2,1,0:T(4,128)S(1)}, u32[]{:S(2)}, u32[]{:S(2)}) collective-permute-start(f32[4,8,4,256]{3,2,1,0:T(4,128)S(1)} %get-tuple-element.46), channel_id=1, source_target_pairs={{1,2},{2,1},{5,6},{6,5},{9,10},{10,9},{13,14},{14,13},{17,18},{18,... | collective-permute-start | bytes 393224 | tf_op jit(solution)/shard_map/ppermute | solution.py:563
  7.5 6.0 %copy-start.1 = (f32[1,2,1,8,32,256]{5,4,3,2,1,0:T(8,128)S(1)}, f32[1,2,1,8,32,256]{5,4,3,2,1,0:T(8,128)}, u32[]{:S(2)}) copy-start(f32[1,2,1,8,32,256]{5,4,3,2,1,0:T(8,128)} %adj.5) | copy-start | bytes 1572868
  7.5 6.0 %copy-start.2 = (f32[1,8,32,256]{3,2,1,0:T(8,128)S(1)}, f32[1,8,32,256]{3,2,1,0:T(8,128)}, u32[]{:S(2)}) copy-start(f32[1,8,32,256]{3,2,1,0:T(8,128)} %buoy.5) | copy-start | bytes 786436
  7.5 6.0 %copy-start.3 = (bf16[256,512]{1,0:T(8,128)(2,1)S(1)}, bf16[256,512]{1,0:T(8,128)(2,1)}, u32[]{:S(2)}) copy-start(bf16[256,512]{1,0:T(8,128)(2,1)} %constant.6.clone.zf) | copy-start | bytes 786436
  7.5 6.0 %copy-start.5 = (bf16[2,64,80]{2,1,0:T(8,128)(2,1)S(1)}, bf16[2,64,80]{2,1,0:T(8,128)(2,1)}, u32[]{:S(2)}) copy-start(bf16[2,64,80]{2,1,0:T(8,128)(2,1)} %constant.7.clone.yf) | copy-start | bytes 61444
  9.1 11.8 %collective-permute-start.4 = (f32[6,32,256]{2,1,0:T(8,128)S(1)}, f32[6,32,256]{2,1,0:T(8,128)S(1)}, u32[]{:S(2)}, u32[]{:S(2)}) collective-permute-start(f32[6,32,256]{2,1,0:T(8,128)S(1)} %get-tuple-element.63), channel_id=1, source_target_pairs={{0,4},{1,5},{2,6},{3,7},{4,0},{5,1},{6,2},{7,3},{8,12},{9,13},{10,... | collective-permute-start | bytes 589832 | tf_op jit(solution)/shard_map/ppermute | solution.py:563
  13.5 2.6 %copy-start.4 = (f32[1,8,32,256]{3,2,1,0:T(8,128)S(1)}, f32[1,8,32,256]{3,2,1,0:T(8,128)}, u32[]{:S(2)}) copy-start(f32[1,8,32,256]{3,2,1,0:T(8,128)} %mod.3) | copy-start | bytes 786436
  16.0 8.9 %copy-start = (f32[1,4,1,8,32,256]{5,4,3,2,1,0:T(8,128)S(1)}, f32[1,4,1,8,32,256]{5,4,3,2,1,0:T(8,128)}, u32[]{:S(2)}) copy-start(f32[1,4,1,8,32,256]{5,4,3,2,1,0:T(8,128)} %fwd.5) | copy-start | bytes 3145732
  16.3 16.4 %collective-permute-start.5 = (f32[6,32,256]{2,1,0:T(8,128)S(1)}, f32[6,32,256]{2,1,0:T(8,128)S(1)}, u32[]{:S(2)}, u32[]{:S(2)}) collective-permute-start(f32[6,32,256]{2,1,0:T(8,128)S(1)} %get-tuple-element.65), channel_id=1, source_target_pairs={{0,4},{1,5},{2,6},{3,7},{4,0},{5,1},{6,2},{7,3},{8,12},{9,13},{10,... | collective-permute-start | bytes 589832 | tf_op jit(solution)/shard_map/ppermute | solution.py:563
  18.8 13.8 %collective-permute-start.6 = (f32[6,32,256]{2,1,0:T(8,128)S(1)}, f32[6,32,256]{2,1,0:T(8,128)S(1)}, u32[]{:S(2)}, u32[]{:S(2)}) collective-permute-start(f32[6,32,256]{2,1,0:T(8,128)S(1)} %get-tuple-element.66), channel_id=1, source_target_pairs={{4,8},{5,9},{6,10},{7,11},{8,4},{9,5},{10,6},{11,7},{12,16},{13,17... | collective-permute-start | bytes 589832 | tf_op jit(solution)/shard_map/ppermute | solution.py:563
  19.5 13.1 %collective-permute-start.9 = (f32[6,32,256]{2,1,0:T(8,128)S(1)}, f32[6,32,256]{2,1,0:T(8,128)S(1)}, u32[]{:S(2)}, u32[]{:S(2)}) collective-permute-start(f32[6,32,256]{2,1,0:T(8,128)S(1)} %get-tuple-element.77), channel_id=1, source_target_pairs={{4,8},{5,9},{6,10},{7,11},{8,4},{9,5},{10,6},{11,7},{12,16},{13,17... | collective-permute-start | bytes 589832 | tf_op jit(solution)/shard_map/ppermute | solution.py:563
  20.2 6.1 %collective-permute-start.8 = (f32[8,8,256]{2,1,0:T(8,128)S(1)}, f32[8,8,256]{2,1,0:T(8,128)S(1)}, u32[]{:S(2)}, u32[]{:S(2)}) collective-permute-start(f32[8,8,256]{2,1,0:T(8,128)S(1)} %get-tuple-element.68), channel_id=1, source_target_pairs={{1,2},{2,1},{5,6},{6,5},{9,10},{10,9},{13,14},{14,13},{17,18},{18,... | collective-permute-start | bytes 196616 | tf_op jit(solution)/shard_map/ppermute | solution.py:563
  20.9 5.4 %collective-permute-start.7 = (f32[8,4,256]{2,1,0:T(4,128)S(1)}, f32[8,4,256]{2,1,0:T(4,128)S(1)}, u32[]{:S(2)}, u32[]{:S(2)}) collective-permute-start(f32[8,4,256]{2,1,0:T(4,128)S(1)} %get-tuple-element.67), channel_id=1, source_target_pairs={{0,1},{1,0},{2,3},{3,2},{4,5},{5,4},{6,7},{7,6},{8,9},{9,8},{10,11... | collective-permute-start | bytes 98312 | tf_op jit(solution)/shard_map/ppermute | solution.py:563
  24.9 1.3 %copy-start.8 = (bf16[2,32,16]{2,1,0:T(8,128)(2,1)S(1)}, bf16[2,32,16]{2,1,0:T(8,128)(2,1)}, u32[]{:S(2)}) copy-start(bf16[2,32,16]{2,1,0:T(8,128)(2,1)} %constant.8.clone.ye) | copy-start | bytes 6148
